TPU v7x, 32 devices: a whole 2x2x4 slice. The times are simulated.
32 devices in a mesh: shard: 8 (over y, x, core), rep: 4 (over z).
Axes of the slice: x: 2, y: 2, z: 4, core: 2. Of those that a mesh axis runs over, the one named last changes fastest.
Arguments:
- tokens: bfloat16 [16384, 2048], P(('shard', 'rep')), may hold values from -6 to 6
- out_grad: bfloat16 [16384, 2048], P(('shard', 'rep')), may hold values from -6 to 6
- token_perm: int32 [16384], replicated, may hold values from 0 to 16383, as said below
- seq_lens: int32 [32, 4], P(('shard', 'rep')), may hold values from 0 to 512, as said below
- adapter_ids: int32 [32, 4, 5], P(('shard', 'rep')), may hold values from 0 to 7
- attn_norm_gain: bfloat16 [2048], P('shard'), may hold values from 0.099609375 to 1.8984375
- attn_norm_bias: bfloat16 [2048], P('shard'), may hold values from -1.75 to 1.75
- query_weight: bfloat16 [2048, 2048], P('shard'), may hold values from -0.125 to 0.125
- query_bias: bfloat16 [2048], P('shard'), may hold values from -1.75 to 1.75
- keyval_weight: bfloat16 [2048, 256], P('shard'), may hold values from -0.125 to 0.125
- value_bias: bfloat16 [128], P('shard'), may hold values from -0.625 to 0.625
- mixer_weight: bfloat16 [2048, 2048], P('shard'), may hold values from -0.75 to 0.75
- mixer_bias: bfloat16 [2048], P('shard'), may hold values from -1.75 to 1.75
- mlp_norm_gain: bfloat16 [2048], P('shard'), may hold values from 0.099609375 to 1.8984375
- mlp_norm_bias: bfloat16 [2048], P('shard'), may hold values from -1.75 to 1.75
- expand_weight: bfloat16 [2048, 8192], P('shard'), may hold values from -0.125 to 0.125
- expand_bias: bfloat16 [8192], P('shard'), may hold values from -1.75 to 1.75
- reduce_weight: bfloat16 [8192, 2048], P('shard'), may hold values from -0.09375 to 0.09375
- reduce_bias: bfloat16 [2048], P('shard'), may hold values from -1.75 to 1.75
- query_down: bfloat16 [8, 16, 2048], replicated, may hold values from -0.125 to 0.125
- query_up: bfloat16 [8, 16, 2048], replicated, may hold values from -0.75 to 0.75
- keyval_down: bfloat16 [8, 16, 2048], replicated, may hold values from -0.125 to 0.125
- keyval_up: bfloat16 [8, 16, 256], replicated, may hold values from -0.75 to 0.75
- mixer_down: bfloat16 [8, 16, 2048], replicated, may hold values from -0.75 to 0.75
- mixer_up: bfloat16 [8, 16, 2048], replicated, may hold values from -0.75 to 0.75
- expand_down: bfloat16 [8, 16, 2048], replicated, may hold values from -0.125 to 0.125
- expand_up: bfloat16 [8, 16, 8192], replicated, may hold values from -0.75 to 0.75
- reduce_down: bfloat16 [8, 16, 8192], replicated, may hold values from -0.09375 to 0.09375
- reduce_up: bfloat16 [8, 16, 2048], replicated, may hold values from -0.75 to 0.75
Outputs:
- layer_out: bfloat16 [16384, 2048], P(('shard', 'rep'))
- tokens_grad: bfloat16 [16384, 2048], P(('shard', 'rep'))
- query_down_grad: float32 [8, 16, 2048], P(None, None, 'shard')
- query_up_grad: float32 [8, 16, 2048], P(None, None, 'shard')
- keyval_down_grad: float32 [8, 16, 2048], P(None, None, 'shard')
- keyval_up_grad: float32 [8, 16, 256], P(None, None, 'shard')
- mixer_down_grad: float32 [8, 16, 2048], P(None, None, 'shard')
- mixer_up_grad: float32 [8, 16, 2048], P(None, None, 'shard')
- expand_down_grad: float32 [8, 16, 2048], P(None, None, 'shard')
- expand_up_grad: float32 [8, 16, 8192], P(None, None, 'shard')
- reduce_down_grad: float32 [8, 16, 8192], P(None, None, 'shard')
- reduce_up_grad: float32 [8, 16, 2048], P(None, None, 'shard')
Inputs may be any that keep to these rules, and one draw needn't show every extreme that they name: token_perm is a permutation. Dealt block s * 4 + r takes its tokens only from the given-order blocks of devices with the same rep index r. From any device to any one device of its shard group go at most 96 tokens, and in every draw some pair carries exactly 96. `seq_lens`: each row sums to 512; every length is a multiple of 128, and a length of 0 is an empty slot. Some block holds one sequence of 512 tokens in every draw.
All inputs are finite; a program needn't handle non-finite values.
Results may differ from a plain program's by a relative error of at most 0.015.
Values may be sent and summed in bfloat16 or wider, within the bound.
A program may use at most 320 MiB of HBM per device.

v0:
```python
import math

import jax
import jax.numpy as jnp
from jax import lax
from jax.sharding import PartitionSpec as P

adapter_scale = 0.5
norm_epsilon = 1e-05
masked_score = -1e30


def layer_norm(values, norm_gain, norm_bias):
    center = values - jnp.mean(values, axis=-1, keepdims=True)
    spread = jnp.mean(center * center, axis=-1, keepdims=True)
    return center * lax.rsqrt(spread + norm_epsilon) * norm_gain.astype(
        jnp.float32
    ) + norm_bias.astype(jnp.float32)


def norm_grad(values, norm_gain, norm_bias, gradient):

    def apply_norm(inner_values):
        return layer_norm(inner_values, norm_gain, norm_bias)

    result, pull_back = jax.vjp(apply_norm, values)
    return pull_back(gradient)[0]


def contract_last(left_mat, right_mat):
    return lax.dot_general(
        left_mat, right_mat, (((1,), (1,)), ((), ())), preferred_element_type=jnp.float32
    )


def contract_first(left_mat, right_mat):
    return lax.dot_general(
        left_mat, right_mat, (((0,), (0,)), ((), ())), preferred_element_type=jnp.float32
    )


def flatten_rank(stacked):
    return stacked.reshape(stacked.shape[0] * stacked.shape[1], stacked.shape[2])


def project(inputs, weight, bias_row, down_mat, up_mat, col_mask):
    lowered = (contract_last(inputs, down_mat) * col_mask).astype(jnp.bfloat16)
    output = jnp.dot(inputs, weight, preferred_element_type=jnp.float32) + bias_row.astype(
        jnp.float32
    )
    output = output + adapter_scale * jnp.dot(lowered, up_mat, preferred_element_type=jnp.float32)
    return (output, lowered)


def project_back(inputs, lowered, gradient, weight, down_mat, up_mat, col_mask):
    grad_low = gradient.astype(jnp.bfloat16)
    through = (adapter_scale * contract_last(grad_low, up_mat) * col_mask).astype(jnp.bfloat16)
    input_grad = contract_last(grad_low, weight) + jnp.dot(
        through, down_mat, preferred_element_type=jnp.float32
    )
    return (
        input_grad,
        contract_first(through, inputs),
        adapter_scale * contract_first(lowered, grad_low),
    )


def pack_rows(row_data, slot_ids, members, capacity):
    buffer = (
        jnp.zeros((members * capacity, row_data.shape[1]), row_data.dtype)
        .at[slot_ids]
        .set(row_data)
    )
    return buffer.reshape(members, capacity, row_data.shape[1])


def unpack_rows(received, slot_ids):
    return received.reshape(received.shape[0] * received.shape[1], received.shape[2])[slot_ids]


def masked_scores(query_rows, key_rows, row_place, row_segment, places, segment):
    scores = contract_last(query_rows, key_rows) * key_rows.shape[1] ** (-0.5)
    allowed = (row_segment[:, None] == segment[None, :]) & (row_place[:, None] >= places[None, :])
    return jnp.where(allowed, scores, masked_score)


def local(
    tokens,
    out_grad,
    token_perm,
    seq_lens,
    adapter_ids,
    attn_norm_gain,
    attn_norm_bias,
    query_weight,
    query_bias,
    keyval_weight,
    value_bias,
    mixer_weight,
    mixer_bias,
    mlp_norm_gain,
    mlp_norm_bias,
    expand_weight,
    expand_bias,
    reduce_weight,
    reduce_bias,
    query_down,
    query_up,
    keyval_down,
    keyval_up,
    mixer_down,
    mixer_up,
    expand_down,
    expand_up,
    reduce_down,
    reduce_up,
):
    members = lax.axis_size("shard")
    replicas = lax.axis_size("rep")
    member_idx = lax.axis_index("shard")
    replica_idx = lax.axis_index("rep")
    length = tokens.shape[0]
    model_width = tokens.shape[1]
    capacity = 3 * length // (2 * members)
    own_block = member_idx * replicas + replica_idx
    adapter_count = query_down.shape[0]
    rank_size = query_down.shape[1]

    def unflatten(flat_grad):
        return flat_grad.reshape(adapter_count, rank_size, flat_grad.shape[1])

    incoming = lax.dynamic_slice_in_dim(token_perm, own_block * length, length)
    from_member = incoming // length // replicas
    earlier_in = (from_member[:, None] == from_member[None, :]) & (
        incoming[None, :] < incoming[:, None]
    )
    in_slots = from_member * capacity + jnp.sum(earlier_in.astype(jnp.int32), axis=1)
    group_perm = lax.dynamic_index_in_dim(
        token_perm.reshape(members, replicas, length), replica_idx, 1, keepdims=False
    ).reshape(members * length)
    offset = group_perm - own_block * length
    in_range = (offset >= 0) & (offset < length)
    target = (
        jnp.zeros((length,), jnp.int32)
        .at[jnp.where(in_range, offset, length)]
        .set(jnp.arange(members * length, dtype=jnp.int32), mode="drop")
    )
    to_member = target // length
    order_ids = jnp.arange(length, dtype=jnp.int32)
    earlier_out = (to_member[:, None] == to_member[None, :]) & (
        order_ids[None, :] < order_ids[:, None]
    )
    out_slots = to_member * capacity + jnp.sum(earlier_out.astype(jnp.int32), axis=1)
    dealt_tokens, dealt_grad = (
        lax.all_to_all(
            pack_rows(tokens, out_slots, members, capacity),
            "shard",
            split_axis=0,
            concat_axis=0,
            tiled=True,
        ),
        lax.all_to_all(
            pack_rows(out_grad, out_slots, members, capacity),
            "shard",
            split_axis=0,
            concat_axis=0,
            tiled=True,
        ),
    )
    here_tokens = unpack_rows(dealt_tokens, in_slots)
    here_grad = unpack_rows(dealt_grad, in_slots)
    slot_lens = seq_lens[0]
    seq_ends = jnp.cumsum(slot_lens)
    places = jnp.arange(length, dtype=jnp.int32)
    segment = jnp.sum((places[:, None] >= seq_ends[None, :]).astype(jnp.int32), axis=1)
    slot_hits = (
        segment[:, None] == jnp.arange(slot_lens.shape[0], dtype=jnp.int32)[None, :]
    ).astype(jnp.int32)
    chosen = jnp.sum(slot_hits[:, :, None] * adapter_ids[0][None, :, :], axis=1)
    rank_cols = jnp.arange(query_down.shape[0] * rank_size, dtype=jnp.int32) // rank_size
    col_masks = [
        (rank_cols[None, :] == chosen[:, which_proj : which_proj + 1]).astype(jnp.float32)
        for which_proj in range(5)
    ]
    adapter_flat = [
        flatten_rank(stacked)
        for stacked in (
            query_down,
            query_up,
            keyval_down,
            keyval_up,
            mixer_down,
            mixer_up,
            expand_down,
            expand_up,
            reduce_down,
            reduce_up,
        )
    ]
    attn_full = (
        lax.all_gather(attn_norm_gain, "shard", axis=0, tiled=True),
        lax.all_gather(attn_norm_bias, "shard", axis=0, tiled=True),
        lax.all_gather(query_weight, "shard", axis=0, tiled=True),
        lax.all_gather(query_bias, "shard", axis=0, tiled=True),
        lax.all_gather(keyval_weight, "shard", axis=0, tiled=True),
        lax.all_gather(value_bias, "shard", axis=0, tiled=True),
        lax.all_gather(mixer_weight, "shard", axis=0, tiled=True),
        lax.all_gather(mixer_bias, "shard", axis=0, tiled=True),
    )
    head_size = attn_full[5].shape[0]
    head_count = model_width // head_size
    query_block = math.gcd(length, 128)
    block_total = length // query_block
    block_rows = query_block * head_count
    here_x = here_tokens.astype(jnp.float32)
    normed_attn = layer_norm(here_x, attn_full[0], attn_full[1]).astype(jnp.bfloat16)
    query_raw, query_rank = project(
        normed_attn, attn_full[2], attn_full[3], adapter_flat[0], adapter_flat[1], col_masks[0]
    )
    query_low = query_raw.astype(jnp.bfloat16)
    keyval_bias = jnp.concatenate(
        [jnp.zeros((head_size,), jnp.float32), attn_full[5].astype(jnp.float32)]
    )
    keyval_raw, keyval_rank = project(
        normed_attn, attn_full[4], keyval_bias, adapter_flat[2], adapter_flat[3], col_masks[1]
    )
    keyval_low = keyval_raw.astype(jnp.bfloat16)
    key_rows = keyval_low[:, :head_size]
    value_rows = keyval_low[:, head_size:]

    def block_info(block_index):
        first_row = block_index * query_block
        row_place = first_row + jnp.arange(block_rows, dtype=jnp.int32) // head_count
        row_segment = jnp.repeat(
            lax.dynamic_slice_in_dim(segment, first_row, query_block), head_count
        )
        query_rows = lax.dynamic_slice_in_dim(query_low, first_row, query_block).reshape(
            block_rows, head_size
        )
        return (first_row, row_place, row_segment, query_rows)

    def attend_forward(block_index):
        first_row, row_place, row_segment, query_rows = block_info(block_index)
        scores = masked_scores(query_rows, key_rows, row_place, row_segment, places, segment)
        row_max = jnp.max(scores, axis=1, keepdims=True)
        shifted = jnp.exp(scores - row_max)
        row_total = jnp.sum(shifted, axis=1, keepdims=True)
        softmax_rows = (shifted / row_total).astype(jnp.bfloat16)
        mixed_rows = jnp.dot(softmax_rows, value_rows, preferred_element_type=jnp.float32)
        return (mixed_rows.reshape(query_block, model_width), (row_max + jnp.log(row_total))[:, 0])

    mixed_blocks, log_totals = lax.map(attend_forward, jnp.arange(block_total, dtype=jnp.int32))
    attended = mixed_blocks.reshape(length, model_width).astype(jnp.bfloat16)
    mixer_raw, mixer_rank = project(
        attended, attn_full[6], attn_full[7], adapter_flat[4], adapter_flat[5], col_masks[2]
    )
    resid = here_x + mixer_raw
    mlp_full = (
        lax.all_gather(mlp_norm_gain, "shard", axis=0, tiled=True),
        lax.all_gather(mlp_norm_bias, "shard", axis=0, tiled=True),
        lax.all_gather(expand_weight, "shard", axis=0, tiled=True),
        lax.all_gather(expand_bias, "shard", axis=0, tiled=True),
        lax.all_gather(reduce_weight, "shard", axis=0, tiled=True),
        lax.all_gather(reduce_bias, "shard", axis=0, tiled=True),
    )
    normed_mlp = layer_norm(resid, mlp_full[0], mlp_full[1]).astype(jnp.bfloat16)
    expand_raw, expand_rank = project(
        normed_mlp, mlp_full[2], mlp_full[3], adapter_flat[6], adapter_flat[7], col_masks[3]
    )

    def gelu_tanh(inner_values):
        return jax.nn.gelu(inner_values, approximate=True)

    act_value, gelu_pull = jax.vjp(gelu_tanh, expand_raw)
    act_low = act_value.astype(jnp.bfloat16)
    reduce_raw, reduce_rank = project(
        act_low, mlp_full[4], mlp_full[5], adapter_flat[8], adapter_flat[9], col_masks[4]
    )
    layer_here = (resid + reduce_raw).astype(jnp.bfloat16)
    back_out = lax.all_to_all(
        pack_rows(layer_here, in_slots, members, capacity),
        "shard",
        split_axis=0,
        concat_axis=0,
        tiled=True,
    )
    mlp_back = (
        lax.all_gather(mlp_norm_gain, "shard", axis=0, tiled=True),
        lax.all_gather(mlp_norm_bias, "shard", axis=0, tiled=True),
        lax.all_gather(expand_weight, "shard", axis=0, tiled=True),
        lax.all_gather(expand_bias, "shard", axis=0, tiled=True),
        lax.all_gather(reduce_weight, "shard", axis=0, tiled=True),
        lax.all_gather(reduce_bias, "shard", axis=0, tiled=True),
    )
    grad_here = here_grad.astype(jnp.float32)
    act_grad, reduce_down_grad, reduce_up_grad = project_back(
        act_low, reduce_rank, grad_here, mlp_back[4], adapter_flat[8], adapter_flat[9], col_masks[4]
    )
    hidden_grad = gelu_pull(act_grad)[0]
    normed_mlp_grad, expand_down_grad, expand_up_grad = project_back(
        normed_mlp,
        expand_rank,
        hidden_grad,
        mlp_back[2],
        adapter_flat[6],
        adapter_flat[7],
        col_masks[3],
    )
    resid_grad = grad_here + norm_grad(resid, mlp_back[0], mlp_back[1], normed_mlp_grad)
    attn_back = (
        lax.all_gather(attn_norm_gain, "shard", axis=0, tiled=True),
        lax.all_gather(attn_norm_bias, "shard", axis=0, tiled=True),
        lax.all_gather(query_weight, "shard", axis=0, tiled=True),
        lax.all_gather(query_bias, "shard", axis=0, tiled=True),
        lax.all_gather(keyval_weight, "shard", axis=0, tiled=True),
        lax.all_gather(value_bias, "shard", axis=0, tiled=True),
        lax.all_gather(mixer_weight, "shard", axis=0, tiled=True),
        lax.all_gather(mixer_bias, "shard", axis=0, tiled=True),
    )
    mixed_grad, mixer_down_grad, mixer_up_grad = project_back(
        attended,
        mixer_rank,
        resid_grad,
        attn_back[6],
        adapter_flat[4],
        adapter_flat[5],
        col_masks[2],
    )
    mixed_low_grad = mixed_grad.astype(jnp.bfloat16)

    def attend_backward(running, block_index):
        key_sum, value_sum = running
        first_row, row_place, row_segment, query_rows = block_info(block_index)
        scores = masked_scores(query_rows, key_rows, row_place, row_segment, places, segment)
        block_lse = lax.dynamic_index_in_dim(log_totals, block_index, 0, keepdims=False)
        softmax_rows = jnp.exp(scores - block_lse[:, None])
        out_rows = lax.dynamic_slice_in_dim(mixed_low_grad, first_row, query_block).reshape(
            block_rows, head_size
        )
        prob_grad = contract_last(out_rows, value_rows)
        row_dot = jnp.sum(prob_grad * softmax_rows, axis=1, keepdims=True)
        score_grad = (softmax_rows * (prob_grad - row_dot)).astype(jnp.bfloat16)
        head_scale = head_size ** (-0.5)
        query_part = jnp.dot(score_grad, key_rows, preferred_element_type=jnp.float32) * head_scale
        key_sum = key_sum + contract_first(score_grad, query_rows) * head_scale
        value_sum = value_sum + contract_first(softmax_rows.astype(jnp.bfloat16), out_rows)
        return ((key_sum, value_sum), query_part.reshape(query_block, model_width))

    start_sums = (
        jnp.zeros((length, head_size), jnp.float32),
        jnp.zeros((length, head_size), jnp.float32),
    )
    (key_grad, value_grad), query_blocks = lax.scan(
        attend_backward, start_sums, jnp.arange(block_total, dtype=jnp.int32)
    )
    query_grad = query_blocks.reshape(length, model_width)
    normed_q_grad, query_down_grad, query_up_grad = project_back(
        normed_attn,
        query_rank,
        query_grad,
        attn_back[2],
        adapter_flat[0],
        adapter_flat[1],
        col_masks[0],
    )
    keyval_grad = jnp.concatenate([key_grad, value_grad], axis=1)
    normed_kv_grad, keyval_down_grad, keyval_up_grad = project_back(
        normed_attn,
        keyval_rank,
        keyval_grad,
        attn_back[4],
        adapter_flat[2],
        adapter_flat[3],
        col_masks[1],
    )
    input_grad = resid_grad + norm_grad(
        here_x, attn_back[0], attn_back[1], normed_q_grad + normed_kv_grad
    )
    input_low = input_grad.astype(jnp.bfloat16)
    back_grad = lax.all_to_all(
        pack_rows(input_low, in_slots, members, capacity),
        "shard",
        split_axis=0,
        concat_axis=0,
        tiled=True,
    )
    layer_out = unpack_rows(back_out, out_slots)
    tokens_grad = unpack_rows(back_grad, out_slots)
    shares = (
        lax.psum_scatter(unflatten(query_down_grad), "shard", scatter_dimension=2, tiled=True),
        lax.psum_scatter(unflatten(query_up_grad), "shard", scatter_dimension=2, tiled=True),
        lax.psum_scatter(unflatten(keyval_down_grad), "shard", scatter_dimension=2, tiled=True),
        lax.psum_scatter(unflatten(keyval_up_grad), "shard", scatter_dimension=2, tiled=True),
        lax.psum_scatter(unflatten(mixer_down_grad), "shard", scatter_dimension=2, tiled=True),
        lax.psum_scatter(unflatten(mixer_up_grad), "shard", scatter_dimension=2, tiled=True),
        lax.psum_scatter(unflatten(expand_down_grad), "shard", scatter_dimension=2, tiled=True),
        lax.psum_scatter(unflatten(expand_up_grad), "shard", scatter_dimension=2, tiled=True),
        lax.psum_scatter(unflatten(reduce_down_grad), "shard", scatter_dimension=2, tiled=True),
        lax.psum_scatter(unflatten(reduce_up_grad), "shard", scatter_dimension=2, tiled=True),
    )
    totals = lax.psum(
        (
            shares[0],
            shares[1],
            shares[2],
            shares[3],
            shares[4],
            shares[5],
            shares[6],
            shares[7],
            shares[8],
            shares[9],
        ),
        "rep",
    )
    return (
        layer_out,
        tokens_grad,
        totals[0],
        totals[1],
        totals[2],
        totals[3],
        totals[4],
        totals[5],
        totals[6],
        totals[7],
        totals[8],
        totals[9],
    )


def solution(mesh):
    in_specs = (
        P(("shard", "rep"), None),
        P(("shard", "rep"), None),
        P(),
        P(("shard", "rep"), None),
        P(("shard", "rep"), None, None),
        P("shard"),
        P("shard"),
        P("shard", None),
        P("shard"),
        P("shard", None),
        P("shard"),
        P("shard", None),
        P("shard"),
        P("shard"),
        P("shard"),
        P("shard", None),
        P("shard"),
        P("shard", None),
        P("shard"),
        P(),
        P(),
        P(),
        P(),
        P(),
        P(),
        P(),
        P(),
        P(),
        P(),
    )
    out_specs = (
        P(("shard", "rep"), None),
        P(("shard", "rep"), None),
        P(None, None, "shard"),
        P(None, None, "shard"),
        P(None, None, "shard"),
        P(None, None, "shard"),
        P(None, None, "shard"),
        P(None, None, "shard"),
        P(None, None, "shard"),
        P(None, None, "shard"),
        P(None, None, "shard"),
        P(None, None, "shard"),
    )
    return jax.shard_map(local, mesh=mesh, in_specs=in_specs, out_specs=out_specs, check_vma=False)
```

profile of v0, /device:TPU:0, one launch (start us, length us, event | category | flops | bytes accessed | tf_op | source)
XLA Modules:
  0.0 1114.1 jit_solution(15358637797142280130)
XLA Ops:
  10.7 15.5 %scatter_custom_fusion = s32[512]{0:T(512)S(1)} fusion(s32[4096]{0:T(1024)S(1)} %bitcast.237, s32[4096]{0:T(1024)S(1)} %iota.60, s32[]{:T(128)} %constant.252.clone.1), kind=kCustom, calls=%fused_computation.190 | custom fusion | bytes 2052 | tf_op jit(solution)/shard_map/scatter | solution.py:146
  26.5 6.7 scatter_custom_fusion.1
  33.2 5.2 all-to-all-start
  38.5 6.7 scatter_custom_fusion.3
  45.2 42.3 %all-to-all-done = bf16[8,96,2048]{2,1,0:T(8,128)(2,1)} async-done(((bf16[8,96,2048]{2,1,0:T(8,128)(2,1)}), bf16[8,96,2048]{2,1,0:T(8,128)(2,1)}, u32[]{:S(2)}, u32[]{:S(2)}) %all-to-all-start) | async-done | bytes 3145760 | tf_op jit(solution)/shard_map/all_to_all | solution.py:155
  87.5 4.4 all-to-all-start.2
  92.5 57.3 %all-gather.5 = bf16[8,1,256]{2,1,0:T(2,128)(2,1)S(1)} all-gather(bf16[1,1,256]{2,1,0:T(2,128)(2,1)S(1)} %reshape.489), channel_id=1, replica_groups=mesh['shard'=8,'rep'=4] {'shard'}, dimensions={0}, use_global_device_ids=true | all-gather | bytes 4608 | tf_op jit(solution)/shard_map/all_gather | solution.py:260
  149.8 8.1 all-gather.4
  157.9 8.9 all-gather.3
  167.4 8.1 all-gather.2
  176.1 8.7 all-gather.1
  184.8 8.1 all-gather
  192.9 8.7 all_gather.60
  203.8 13.2 %all-reduce.1 = bf16[128]{0:T(256)(128)(2,1)S(1)} all-reduce(bf16[128]{0:T(256)(128)(2,1)S(1)} %dynamic-update-slice), channel_id=1, replica_groups=mesh['shard'=8,'rep'=4] {'shard'}, use_global_device_ids=true, to_apply=%add.1 | all-reduce | flops 128 | bytes 512
  220.1 8.1 gather_fusion
  228.2 7.5 gather_fusion.2
  235.8 2.1 convert_reduce_fusion
  237.9 2.3 fusion.33
  244.9 2.8 fusion.50
  250.7 7.8 fusion.93
  262.1 38.1 %while.32 = (s32[]{:T(128)}, bf16[4,128,2048]{2,1,0:T(8,128)(2,1)}, f32[4,2048]{1,0:T(4,128)}, s32[4]{0:T(128)S(1)}, s32[512]{0:T(512)}, /*index=5*/bf16[512,204...) while((s32[]{:T(128)}, bf16[4,128,2048]{2,1,0:T(8,128)(2,1)}, ...), condition=%wide.region_12.13_spmd.clone, body=%wide.region_9.12_spmd.clone.sunk | while | flops 548421632 | bytes 18222796 | solution.py:252
  300.3 2.5 fusion.59
  302.9 7.7 fusion.94
  316.3 50.2 %all-gather.19.cloned.1.call-done = bf16[2048,8192]{1,0:T(8,128)(2,1)} async-done(((bf16[256,8192]{1,0:T(8,128)(2,1)}), bf16[2048,8192]{1,0:T(8,128)(2,1)}) %all-gather.19.cloned.1.call-update) | async-done | bytes 33554448 | tf_op jit(solution)/shard_map/all_gather | solution.py:261
  366.5 27.7 %fusion.95 = f32[512,8192]{1,0:T(8,128)} fusion(bf16[512,2048]{1,0:T(8,128)(2,1)} %copy-done.21, bf16[2048,8192]{1,0:T(8,128)(2,1)} %all-gather.19.cloned.1.call-done), kind=kOutput, calls=%fused_computation.205 | convolution fusion | flops 17179869184 | bytes 52428800 | tf_op jit(solution)/shard_map/dot_general | solution.py:48
  394.3 14.3 %multiply_convert_fusion.1 = (bf16[512,8192]{1,0:T(8,128)(2,1)S(1)}, f32[512,8192]{1,0:T(8,128)}) fusion(bf16[512,128]{1,0:T(8,128)(2,1)S(1)} %fusion.60, bf16[128,8192]{1,0:T(8,128)(2,1)S(1)} %bitcast.185, f32[512,8192]{1,0:T(8,128)} %fusion.95, f32[8192]{0:T(1024)S(1)} %copy-done.63), kind=kOutput, calls=%fused_computation.61 | convolution fusion | flops 1124073472 | bytes 44204032 | tf_op jit(solution)/shard_map/dot_general | solution.py:51
  408.6 5.6 fusion.55
  415.8 113.2 %all-gather.21.cloned.1.call-done = bf16[8192,2048]{1,0:T(8,128)(2,1)} async-done(((bf16[1024,2048]{1,0:T(8,128)(2,1)}), bf16[8192,2048]{1,0:T(8,128)(2,1)}) %all-gather.21.cloned.1.call-update) | async-done | bytes 33554448 | tf_op jit(solution)/shard_map/all_gather | solution.py:263
  529.1 25.8 %fusion.97 = f32[512,8192]{1,0:T(8,128)} fusion(bf16[512,2048]{1,0:T(8,128)(2,1)} %gather_fusion.2, bf16[8192,2048]{1,0:T(8,128)(2,1)} %all-gather.21.cloned.1.call-done), kind=kOutput, calls=%fused_computation.207 | convolution fusion | flops 17179869184 | bytes 52428800 | tf_op jit(solution)/shard_map/dot_general | solution.py:31
  554.9 20.0 %fusion.28 = bf16[512,8192]{1,0:T(8,128)(2,1)} fusion(f32[512,8192]{1,0:T(8,128)} %get-tuple-element.409, f32[512,8192]{1,0:T(8,128)} %fusion.97, bf16[512,128]{1,0:T(8,128)(2,1)S(1)} %copy-done.46, bf16[128,8192]{1,0:T(8,128)(2,1)} %bitcast.252), kind=kOutput, calls=%fused_computation.60 | convolution fusion | flops 1161822208 | bytes 44171264 | tf_op jit(solution)/shard_map/dot_general | solution.py:58
  574.9 24.2 %fusion.98 = f32[512,2048]{1,0:T(8,128)S(1)} fusion(bf16[512,8192]{1,0:T(8,128)(2,1)} %fusion.28, bf16[2048,8192]{1,0:T(8,128)(2,1)} %all-gather.19.cloned.1.call-done), kind=kOutput, calls=%fused_computation.208 | convolution fusion | flops 17179869184 | bytes 46137344 | tf_op jit(solution)/shard_map/dot_general | solution.py:31
  599.1 5.9 fusion.56
  605.1 3.2 multiply_reduce_fusion.1
  609.9 4.6 fusion.88
  618.0 3.3 fusion.104
  622.8 7.0 fusion.99
  629.9 2.1 add_convert_fusion.1
  633.6 56.4 %while.33 = (s32[]{:T(128)}, f32[512,128]{1,0:T(8,128)S(1)}, f32[512,128]{1,0:T(8,128)S(1)}, bf16[4,128,2048]{2,1,0:T(8,128)(2,1)}, s32[4]{0:T(128)S(1)}, /*inde...) while((s32[]{:T(128)}, f32[512,128]{1,0:T(8,128)S(1)}, ...), condition=%wide.region_21.22_spmd.clone, body=%wide.region_19.21_spmd.clone.sunk | while | flops 1355628544 | bytes 41905940 | solution.py:353
  640.7 2.2 subtract_exponential_fusion.3
  654.7 2.2 subtract_exponential_fusion.3
  668.7 2.2 subtract_exponential_fusion.3
  682.7 2.2 subtract_exponential_fusion.3
  690.0 3.2 convolution_multiply_fusion.5
  695.1 2.5 fusion.62
  699.1 6.8 fusion.106
  706.6 8.9 all-gather.6
  715.6 6.7 convolution_multiply_fusion.2
  722.4 24.2 %fusion.96 = f32[512,2048]{1,0:T(8,128)S(1)} fusion(bf16[512,8192]{1,0:T(8,128)(2,1)} %copy-done.19, bf16[8192,2048]{1,0:T(8,128)(2,1)} %all-gather.21.cloned.1.call-done), kind=kOutput, calls=%fused_computation.206 | convolution fusion | flops 17179869184 | bytes 46137344 | tf_op jit(solution)/shard_map/dot_general | solution.py:48
  747.4 5.9 scatter_custom_fusion.2
  753.2 4.8 all-to-all-start.1
  759.8 7.1 fusion.100
  768.8 3.1 fusion.87
  771.8 9.8 scatter_custom_fusion.4
  781.7 15.6 %all-to-all-done.1 = bf16[8,96,2048]{2,1,0:T(8,128)(2,1)} async-done(((bf16[8,96,2048]{2,1,0:T(8,128)(2,1)}), bf16[8,96,2048]{2,1,0:T(8,128)(2,1)}, u32[]{:S(2)}, u32[]{:S(2)}) %all-to-all-start.1) | async-done | bytes 3145760 | tf_op jit(solution)/shard_map/all_to_all | solution.py:280
  797.3 4.6 all-to-all-start.3
  804.0 10.0 reduce-scatter.17.cloned.1.call-done
  814.0 42.5 %reduce-scatter.13.cloned.1.call-done = f32[8,16,256]{2,1,0:T(8,128)} async-done(((f32[8,16,2048]{2,1,0:T(8,128)}), f32[8,16,256]{2,1,0:T(8,128)}) %reduce-scatter.13.cloned.1.call-update) | async-done | bytes 131088 | tf_op jit(solution)/shard_map/reduce_scatter | solution.py:390
  856.4 54.7 %reduce-scatter.27.cloned.1.call-done = f32[8,16,1024]{2,1,0:T(8,128)} async-done(((f32[8,16,8192]{2,1,0:T(8,128)}), f32[8,16,1024]{2,1,0:T(8,128)}) %reduce-scatter.27.cloned.1.call-update) | async-done | bytes 524304 | tf_op jit(solution)/shard_map/reduce_scatter | solution.py:398
  911.1 55.0 %reduce-scatter.25.cloned.1.call-done = f32[8,16,1024]{2,1,0:T(8,128)} async-done(((f32[8,16,8192]{2,1,0:T(8,128)}), f32[8,16,1024]{2,1,0:T(8,128)}) %reduce-scatter.25.cloned.1.call-update) | async-done | bytes 524304 | tf_op jit(solution)/shard_map/reduce_scatter | solution.py:397
  966.1 36.7 %reduce-scatter.31.cloned.1.call-done = f32[32,128]{1,0:T(8,128)} async-done(((f32[256,128]{1,0:T(8,128)}), f32[32,128]{1,0:T(8,128)}) %reduce-scatter.31.cloned.1.call-update) | async-done | bytes 16400
  1003.8 21.4 %psum.73 = f32[8,16,32]{2,1,0:T(8,128)} all-reduce(f32[8,16,32]{2,1,0:T(8,128)S(1)} %copy.52), channel_id=1, replica_groups=mesh['shard'=8,'rep'=4] {'rep'}, use_global_device_ids=true, to_apply=%region_32.33 | all-reduce | flops 4096 | bytes 32768 | tf_op jit(solution)/shard_map/psum | solution.py:401
  1025.1 7.5 gather_fusion.1
  1032.7 7.7 gather_fusion.3
  1040.4 52.0 %all-reduce.5.cloned.1.call-done = (f32[8,16,256]{2,1,0:T(8,128)}, f32[8,16,256]{2,1,0:T(8,128)}, f32[8,16,256]{2,1,0:T(8,128)}, f32[8,16,256]{2,1,0:T(8,128)}, ...) async-done(((f32[8,16,256]{2,1,0:T(8,128)}, f32[8,16,256]{2,1,0:T(8,128)}, ...) | async-done | bytes 1966096 | tf_op jit(solution)/shard_map/psum | solution.py:401
  (459 shorter events, 134.3 us)
Async XLA Ops:
  7.2 387.1 %copy-start = (bf16[8,16,8192]{2,1,0:T(8,128)(2,1)S(1)}, bf16[8,16,8192]{2,1,0:T(8,128)(2,1)}, u32[]{:S(2)}) copy-start(bf16[8,16,8192]{2,1,0:T(8,128)(2,1)} %param.59) | copy-start | bytes 6291460
  7.2 237.7 %all-gather.15.cloned.1.call-start = ((), (), s32[]{:S(2)}) async-start(), calls=%async_computation.15 | async-start | bytes 1179648 | tf_op jit(solution)/shard_map/all_gather | solution.py:205
  7.9 242.8 %all-gather.13.cloned.1.call-start = ((), (), s32[]{:S(2)}) async-start(), calls=%async_computation.14 | async-start | bytes 9437184 | tf_op jit(solution)/shard_map/all_gather | solution.py:203
  8.7 294.2 %all-gather.17.cloned.1.call-start = ((), (), s32[]{:S(2)}) async-start(), calls=%async_computation.16 | async-start | bytes 9437184 | tf_op jit(solution)/shard_map/all_gather | solution.py:207
  9.4 357.1 %all-gather.19.cloned.1.call-start = ((), (), s32[]{:S(2)}) async-start(), calls=%async_computation.17 | async-start | bytes 37748736 | tf_op jit(solution)/shard_map/all_gather | solution.py:261
  10.0 519.1 %all-gather.21.cloned.1.call-start = ((), (), s32[]{:S(2)}) async-start(), calls=%async_computation.18 | async-start | bytes 37748736 | tf_op jit(solution)/shard_map/all_gather | solution.py:263
  26.5 11.9 %copy-start.77 = (s32[512]{0:T(512)}, s32[512]{0:T(512)S(1)}, u32[]{:S(2)}) copy-start(s32[512]{0:T(512)S(1)} %compare_select_fusion.2) | copy-start | bytes 6148
  33.2 54.3 %all-to-all-start = ((bf16[8,96,2048]{2,1,0:T(8,128)(2,1)}), bf16[8,96,2048]{2,1,0:T(8,128)(2,1)}, u32[]{:S(2)}, u32[]{:S(2)}) async-start(bf16[8,96,2048]{2,1,0:T(8,128)(2,1)} %bitcast.191), calls=%async_computation | async-start | bytes 6291456 | tf_op jit(solution)/shard_map/all_to_all | solution.py:155
  38.4 53.7 %copy-start.92 = (s32[1,4]{1,0:T(1,128)S(1)}, s32[1,4]{1,0:T(1,128)}, u32[]{:S(2)}) copy-start(s32[1,4]{1,0:T(1,128)} %param.36) | copy-start | bytes 52
  38.4 53.9 %copy-start.93 = (bf16[256]{0:T(256)(128)(2,1)S(1)}, bf16[256]{0:T(256)(128)(2,1)}, u32[]{:S(2)}) copy-start(bf16[256]{0:T(256)(128)(2,1)} %param.38) | copy-start | bytes 1540
  38.4 53.9 %copy-start.94 = (bf16[256]{0:T(256)(128)(2,1)S(1)}, bf16[256]{0:T(256)(128)(2,1)}, u32[]{:S(2)}) copy-start(bf16[256]{0:T(256)(128)(2,1)} %param.39) | copy-start | bytes 1540
  38.4 53.9 %copy-start.95 = (bf16[256]{0:T(256)(128)(2,1)S(1)}, bf16[256]{0:T(256)(128)(2,1)}, u32[]{:S(2)}) copy-start(bf16[256]{0:T(256)(128)(2,1)} %param.41) | copy-start | bytes 1540
  38.4 53.9 %copy-start.96 = (bf16[256]{0:T(256)(128)(2,1)S(1)}, bf16[256]{0:T(256)(128)(2,1)}, u32[]{:S(2)}) copy-start(bf16[256]{0:T(256)(128)(2,1)} %param.45) | copy-start | bytes 1540
  38.4 53.9 %copy-start.97 = (bf16[256]{0:T(256)(128)(2,1)S(1)}, bf16[256]{0:T(256)(128)(2,1)}, u32[]{:S(2)}) copy-start(bf16[256]{0:T(256)(128)(2,1)} %param.46) | copy-start | bytes 1540
  38.5 53.9 %copy-start.98 = (bf16[256]{0:T(256)(128)(2,1)S(1)}, bf16[256]{0:T(256)(128)(2,1)}, u32[]{:S(2)}) copy-start(bf16[256]{0:T(256)(128)(2,1)} %param.47) | copy-start | bytes 1540
  38.5 53.9 %copy-start.80 = (s32[1,4,5]{2,1,0:T(4,128)S(1)}, s32[1,4,5]{2,1,0:T(4,128)}, u32[]{:S(2)}) copy-start(s32[1,4,5]{2,1,0:T(4,128)} %param.37) | copy-start | bytes 244
  38.5 154.4 %copy-start.81 = (bf16[1024]{0:T(1024)(128)(2,1)S(1)}, bf16[1024]{0:T(1024)(128)(2,1)}, u32[]{:S(2)}) copy-start(bf16[1024]{0:T(1024)(128)(2,1)} %param.49) | copy-start | bytes 6148
  38.5 163.8 %copy-start.101 = (u32[32]{0:T(128)S(1)}, u32[32]{0:T(128)}, u32[]{:S(2)}) copy-start(u32[32]{0:T(128)} %constant.279) | copy-start | bytes 388
  38.5 165.0 %copy-start.99 = (bf16[16]{0:T(256)(128)(2,1)S(1)}, bf16[16]{0:T(256)(128)(2,1)}, u32[]{:S(2)}) copy-start(bf16[16]{0:T(256)(128)(2,1)} %param.43) | copy-start | bytes 100
  87.5 140.7 %all-to-all-start.2 = ((bf16[8,96,2048]{2,1,0:T(8,128)(2,1)}), bf16[8,96,2048]{2,1,0:T(8,128)(2,1)}, u32[]{:S(2)}, u32[]{:S(2)}) async-start(bf16[8,96,2048]{2,1,0:T(8,128)(2,1)} %bitcast.189), calls=%async_computation.2 | async-start | bytes 6291456 | tf_op jit(solution)/shard_map/all_to_all | solution.py:162
  92.0 711.9 %reduce-scatter.29.cloned.1.call-start = ((), (), s32[]{:S(2)}) async-start(), calls=%async_computation.27 | async-start | bytes 1179648 | tf_op jit(solution)/shard_map/reduce_scatter | solution.py:399
  157.9 155.4 %copy-start.53 = (f32[8,1,256]{2,1,0:T(1,128)}, f32[8,1,256]{2,1,0:T(1,128)S(1)}, u32[]{:S(2)}) copy-start(f32[8,1,256]{2,1,0:T(1,128)S(1)} %convert_element_type.195) | copy-start | bytes 24580
  192.9 47.3 %copy-start.51 = (f32[8,1,256]{2,1,0:T(1,128)}, f32[8,1,256]{2,1,0:T(1,128)S(1)}, u32[]{:S(2)}) copy-start(f32[8,1,256]{2,1,0:T(1,128)S(1)} %convert_element_type.191) | copy-start | bytes 24580
  217.0 24.2 %copy-start.89 = (s32[128]{0:T(128)}, s32[128]{0:T(128)S(1)}, u32[]{:S(2)}) copy-start(s32[128]{0:T(128)S(1)} %and_select_fusion.1) | copy-start | bytes 1540
  220.1 21.0 %copy-start.83 = (s32[512,1]{0,1:T(1,128)}, s32[512,1]{0,1:T(1,128)S(1)}, u32[]{:S(2)}) copy-start(s32[512,1]{0,1:T(1,128)S(1)} %get-tuple-element.404) | copy-start | bytes 6148
  249.3 9.3 copy-start.38
  250.7 7.9 copy-start.41
  250.7 7.9 copy-start.62
  262.1 38.2 %copy-start.75 = (s32[512,1]{0,1:T(1,128)S(1)}, s32[512,1]{0,1:T(1,128)}, u32[]{:S(2)}) copy-start(s32[512,1]{0,1:T(1,128)} %get-tuple-element.403) | copy-start | bytes 6148
  262.1 38.2 %copy-start.91 = (s32[128]{0:T(128)S(1)}, s32[128]{0:T(128)}, u32[]{:S(2)}) copy-start(s32[128]{0:T(128)} %copy-done.89) | copy-start | bytes 1540
  300.3 10.3 copy-start.23
  300.3 10.3 copy-start.25
  302.8 7.8 copy-start.30
  302.8 7.8 copy-start.44
  302.8 7.8 copy-start.64
  302.9 7.8 copy-start.6
  316.3 78.0 %copy-start.47 = (bf16[512,128]{1,0:T(8,128)(2,1)}, bf16[512,128]{1,0:T(8,128)(2,1)S(1)}, u32[]{:S(2)}) copy-start(bf16[512,128]{1,0:T(8,128)(2,1)S(1)} %fusion.60) | copy-start | bytes 393220
  316.3 78.0 %copy-start.63 = (f32[8192]{0:T(1024)S(1)}, f32[8192]{0:T(1024)}, u32[]{:S(2)}) copy-start(f32[8192]{0:T(1024)} %convert_element_type.172) | copy-start | bytes 98308
  394.2 14.3 %copy-start.88 = (s32[512,1]{0,1:T(1,128)S(1)}, s32[512,1]{0,1:T(1,128)}, u32[]{:S(2)}) copy-start(s32[512,1]{0,1:T(1,128)} %get-tuple-element.401) | copy-start | bytes 6148
  415.7 139.1 %copy-start.46 = (bf16[512,128]{1,0:T(8,128)(2,1)S(1)}, bf16[512,128]{1,0:T(8,128)(2,1)}, u32[]{:S(2)}) copy-start(bf16[512,128]{1,0:T(8,128)(2,1)} %fusion.63) | copy-start | bytes 393220
  415.8 388.2 %reduce-scatter.23.cloned.1.call-start = ((), (), s32[]{:S(2)}) async-start(), calls=%async_computation.24 | async-start | bytes 1179648 | tf_op jit(solution)/shard_map/reduce_scatter | solution.py:396
  574.9 24.2 %copy-start.86 = (s32[512,1]{0,1:T(1,128)S(1)}, s32[512,1]{0,1:T(1,128)}, u32[]{:S(2)}) copy-start(s32[512,1]{0,1:T(1,128)} %get-tuple-element.402) | copy-start | bytes 6148
  609.8 194.1 %reduce-scatter.19.cloned.1.call-start = ((), (), s32[]{:S(2)}) async-start(), calls=%async_computation.22 | async-start | bytes 1179648 | tf_op jit(solution)/shard_map/reduce_scatter | solution.py:394
  621.3 182.7 %reduce-scatter.21.cloned.1.call-start = ((), (), s32[]{:S(2)}) async-start(), calls=%async_computation.23 | async-start | bytes 1179648 | tf_op jit(solution)/shard_map/reduce_scatter | solution.py:395
  632.0 172.1 %reduce-scatter.15.cloned.1.call-start = ((), (), s32[]{:S(2)}) async-start(), calls=%async_computation.20 | async-start | bytes 1179648 | tf_op jit(solution)/shard_map/reduce_scatter | solution.py:391
  633.6 56.4 %copy-start.39 = (bf16[512,128]{1,0:T(8,128)(2,1)S(1)}, bf16[512,128]{1,0:T(8,128)(2,1)}, u32[]{:S(2)}) copy-start(bf16[512,128]{1,0:T(8,128)(2,1)} %copy-done.38) | copy-start | bytes 393220
  693.2 120.8 %reduce-scatter.17.cloned.1.call-start = ((), (), s32[]{:S(2)}) async-start(), calls=%async_computation.21 | async-start | bytes 1179648 | tf_op jit(solution)/shard_map/reduce_scatter | solution.py:392
  695.0 161.4 %reduce-scatter.13.cloned.1.call-start = ((), (), s32[]{:S(2)}) async-start(), calls=%async_computation.19 | async-start | bytes 1179648 | tf_op jit(solution)/shard_map/reduce_scatter | solution.py:390
  699.1 212.0 %reduce-scatter.27.cloned.1.call-start = ((), (), s32[]{:S(2)}) async-start(), calls=%async_computation.26 | async-start | bytes 4718592 | tf_op jit(solution)/shard_map/reduce_scatter | solution.py:398
  706.0 9.6 copy-start.48
  706.0 260.1 %reduce-scatter.25.cloned.1.call-start = ((), (), s32[]{:S(2)}) async-start(), calls=%async_computation.25 | async-start | bytes 4718592 | tf_op jit(solution)/shard_map/reduce_scatter | solution.py:397
  722.3 24.2 %copy-start.4 = (f32[512,2048]{1,0:T(8,128)S(1)}, f32[512,2048]{1,0:T(8,128)}, u32[]{:S(2)}) copy-start(f32[512,2048]{1,0:T(8,128)} %copy-done.2) | copy-start | bytes 12582916
  722.3 24.2 %copy-start.29 = (bf16[512,128]{1,0:T(8,128)(2,1)S(1)}, bf16[512,128]{1,0:T(8,128)(2,1)}, u32[]{:S(2)}) copy-start(bf16[512,128]{1,0:T(8,128)(2,1)} %copy-done.28) | copy-start | bytes 393220
  722.3 24.2 %copy-start.33 = (bf16[8,16,2048]{2,1,0:T(8,128)(2,1)S(1)}, bf16[8,16,2048]{2,1,0:T(8,128)(2,1)}, u32[]{:S(2)}) copy-start(bf16[8,16,2048]{2,1,0:T(8,128)(2,1)} %param.61) | copy-start | bytes 1572868
  747.4 10.7 copy-start.35
  753.2 44.0 %all-to-all-start.1 = ((bf16[8,96,2048]{2,1,0:T(8,128)(2,1)}), bf16[8,96,2048]{2,1,0:T(8,128)(2,1)}, u32[]{:S(2)}, u32[]{:S(2)}) async-start(bf16[8,96,2048]{2,1,0:T(8,128)(2,1)} %bitcast.190), calls=%async_computation.1 | async-start | bytes 6291456 | tf_op jit(solution)/shard_map/all_to_all | solution.py:280
  759.8 7.1 copy-start.52
  759.8 7.2 copy-start.59
  781.6 20.3 %copy-start.50 = (bf16[512,128]{1,0:T(8,128)(2,1)S(1)}, bf16[512,128]{1,0:T(8,128)(2,1)}, u32[]{:S(2)}) copy-start(bf16[512,128]{1,0:T(8,128)(2,1)} %copy-done.49) | copy-start | bytes 393220
  797.3 168.8 %copy-start.78 = (s32[512]{0:T(512)S(1)}, s32[512]{0:T(512)}, u32[]{:S(2)}) copy-start(s32[512]{0:T(512)} %copy-done.77) | copy-start | bytes 6148
  797.3 235.4 %all-to-all-start.3 = ((bf16[8,96,2048]{2,1,0:T(8,128)(2,1)}), bf16[8,96,2048]{2,1,0:T(8,128)(2,1)}, u32[]{:S(2)}, u32[]{:S(2)}) async-start(bf16[8,96,2048]{2,1,0:T(8,128)(2,1)} %bitcast.192), calls=%async_computation.3 | async-start | bytes 6291456 | tf_op jit(solution)/shard_map/all_to_all | solution.py:380
  801.9 201.0 %reduce-scatter.31.cloned.1.call-start = ((), (), s32[]{:S(2)}) async-start(), calls=%async_computation.28 | async-start | bytes 147456
  803.6 288.8 %all-reduce.5.cloned.1.call-start = ((), (), s32[]{:S(2)}) async-start(), calls=%async_computation.29 | async-start | bytes 3932160 | tf_op jit(solution)/shard_map/psum | solution.py:401
  1032.7 74.5 %copy-start.1 = (bf16[8,16,8192]{2,1,0:T(8,128)(2,1)S(1)}, bf16[8,16,8192]{2,1,0:T(8,128)(2,1)}, u32[]{:S(2)}) copy-start(bf16[8,16,8192]{2,1,0:T(8,128)(2,1)} %param.59) | copy-start | bytes 6291460
  (58 other events, 201.3 us)
Sparse Core Ops, SparseCore 0:
  9.9 26.1 all-gather.14
  38.0 101.4 all-gather.12
  141.4 62.5 all-gather.16
  205.7 160.7 all-gather.18
  368.2 160.7 all-gather.20
  532.1 36.0 reduce-scatter.28
  609.9 36.1 reduce-scatter.22
  649.3 36.0 reduce-scatter.18
  688.5 36.0 reduce-scatter.20
  727.6 37.3 reduce-scatter.14
  768.1 45.7 reduce-scatter.16
  817.0 39.3 reduce-scatter.12
  859.8 51.2 reduce-scatter.26
  914.7 51.3 reduce-scatter.24
  969.5 33.3 reduce-scatter.30
  1006.2 86.1 all-reduce.4
where the time goes:
time: 1130 us; the launch traced here: 1110 us
  waiting for transfers between devices  476 us (42%)
  matrix products  263 us (23%)
  blocking collectives  151 us (13%)
  local copies, waits for them, and re-layouts  138 us (12%)
  other arithmetic  35.7 us (3%)
  starting transfers between devices  19.9 us (2%)
  between operations  16.7 us (1%)
  loops' own time  13.9 us (1%)
    all_gather x1, waiting for transfers between devices, local(): lax.all_gather(reduce_weight, 'shard', axis=0, tiled=True)  113 us
    dot_general x27, matrix products, contract_last(): lax.dot_general(left_mat, right_mat, (((1,), (1,)), ((), ())), preferred_...  105 us
    dot_general x5, matrix products, project(): jnp.dot(inputs, weight, preferred_element_type=jnp.float32)  70.3 us
    all_gather x1, blocking collectives, local(): lax.all_gather(mlp_norm_bias, 'shard', axis=0, tiled=True)  57.3 us
    reduce_scatter x1, waiting for transfers between devices, local(): lax.psum_scatter(unflatten(expand_up_grad), 'shard', scatter_dimension=2,...  55 us
    reduce_scatter x1, waiting for transfers between devices, local(): lax.psum_scatter(unflatten(reduce_down_grad), 'shard', scatter_dimension=...  54.7 us
    psum x1, waiting for transfers between devices, local(): lax.psum((shares[0], shares[1], shares[2], shares[3], shares[4], shares[5...  52 us
    all_gather x1, waiting for transfers between devices, local(): lax.all_gather(expand_weight, 'shard', axis=0, tiled=True)  50.2 us
  transfers between devices with their start and end apart: 20, of which 10 were waited for; matrix products, arithmetic and copies ran while one was open for 37% of the time, Pallas kernels for 0%

commit v1 on v0

v1 whole, which is shorter than its diff:
```python
import jax
import jax.numpy as jnp
from jax import lax
from jax.experimental import pallas as pl
from jax.experimental.pallas import tpu as pltpu
from jax.sharding import PartitionSpec as P

scale_lora = 0.5
eps = 1e-05
f32 = jnp.float32
bf16 = jnp.bfloat16
neg_big = -1e30
gelu_c = 0.7978845608028654
VMEM_LIMIT = 60 * 1024 * 1024


def dot_nn(a, b):
    return lax.dot_general(a, b, (((1,), (0,)), ((), ())), preferred_element_type=f32)


def dot_nt(a, b):
    return lax.dot_general(a, b, (((1,), (1,)), ((), ())), preferred_element_type=f32)


def dot_tn(a, b):
    return lax.dot_general(a, b, (((0,), (0,)), ((), ())), preferred_element_type=f32)


def key_onehot(slot_row, slots):
    ids = lax.broadcasted_iota(jnp.int32, (slots, slot_row.shape[1]), 0)
    return jnp.where(ids == slot_row, 1.0, 0.0).astype(bf16)


def to_rows(x, heads):
    hd = x.shape[1] // heads
    return jnp.concatenate([x[:, h * hd : (h + 1) * hd] for h in range(heads)], axis=0)


def to_cols(x, heads):
    c = x.shape[0] // heads
    return jnp.concatenate([x[h * c : (h + 1) * c] for h in range(heads)], axis=1)


def softmax_rows(qr, kd, span, heads):
    rows, keys = qr.shape[0], kd.shape[0]
    c = rows // heads
    u = lax.broadcasted_iota(jnp.int32, (c, keys), 1)
    allowed = (u >= span[:, 0:1]) & (u <= span[:, 1:2])
    s = dot_nt(qr, kd) * (kd.shape[1] ** (-0.5))
    s = jnp.where(allowed[None], s.reshape(heads, c, keys), neg_big)
    top = jnp.max(s, axis=2, keepdims=True)
    e = jnp.exp(s - top)
    p = e / jnp.sum(e, axis=2, keepdims=True)
    return p.reshape(rows, keys)


def attn_fwd_kernel(heads, slot_ref, span_ref, q_ref, kv_ref, o_ref, kd_ref):
    m, _, c, w = kv_ref.shape
    hd = w // 2
    oh = key_onehot(slot_ref[0], m * c)
    kvd = dot_tn(oh, kv_ref[...].reshape(m * c, w)).astype(bf16)
    kd_ref[0] = kvd
    qr = to_rows(q_ref[0], heads)
    p = softmax_rows(qr, kvd[:, :hd], span_ref[0], heads).astype(bf16)
    o = dot_nn(p, kvd[:, hd:]).astype(bf16)
    o_ref[0] = to_cols(o, heads)


def attn_bwd_kernel(heads, slot_ref, span_ref, q_ref, do_ref, kd_ref, dq_ref, ds_ref):
    m, _, c, w = ds_ref.shape
    hd = w // 2
    kvd = kd_ref[0]
    kd, vd = kvd[:, :hd], kvd[:, hd:]
    qr = to_rows(q_ref[0], heads)
    dor = to_rows(do_ref[0], heads)
    p = softmax_rows(qr, kd, span_ref[0], heads)
    dp = dot_nt(dor, vd)
    rd = jnp.sum(dp * p, axis=1, keepdims=True)
    ds = (p * (dp - rd)).astype(bf16)
    sc = hd ** (-0.5)
    dq = (dot_nn(ds, kd) * sc).astype(bf16)
    dq_ref[0] = to_cols(dq, heads)
    dk = dot_tn(ds, qr) * sc
    dv = dot_tn(p.astype(bf16), dor)
    dkv = jnp.concatenate([dk, dv], axis=1).astype(bf16)
    oh = key_onehot(slot_ref[0], m * c)
    ds_ref[...] = dot_nn(oh, dkv).astype(bf16).reshape(ds_ref.shape)


def attn_fwd(heads, slot, span, qpad, kvs):
    m, c, w = kvs.shape[0], kvs.shape[2], kvs.shape[3]
    length = slot.shape[2]
    d = qpad.shape[2]
    return pl.pallas_call(
        lambda *refs: attn_fwd_kernel(heads, *refs),
        grid=(m,),
        in_specs=[
            pl.BlockSpec((1, 1, length), lambda k: (k, 0, 0)),
            pl.BlockSpec((1, c, 2), lambda k: (k, 0, 0)),
            pl.BlockSpec((1, c, d), lambda k: (k, 0, 0)),
            pl.BlockSpec((m, 1, c, w), lambda k: (0, k, 0, 0)),
        ],
        out_specs=[
            pl.BlockSpec((1, c, d), lambda k: (k, 0, 0)),
            pl.BlockSpec((1, length, w), lambda k: (k, 0, 0)),
        ],
        out_shape=[
            jax.ShapeDtypeStruct((m, c, d), bf16),
            jax.ShapeDtypeStruct((m, length, w), bf16),
        ],
        compiler_params=pltpu.CompilerParams(vmem_limit_bytes=VMEM_LIMIT),
    )(slot, span, qpad, kvs)


def attn_bwd(heads, slot, span, qpad, dopad, kd):
    m, c, d = qpad.shape
    length, w = kd.shape[1], kd.shape[2]
    return pl.pallas_call(
        lambda *refs: attn_bwd_kernel(heads, *refs),
        grid=(m,),
        in_specs=[
            pl.BlockSpec((1, 1, length), lambda k: (k, 0, 0)),
            pl.BlockSpec((1, c, 2), lambda k: (k, 0, 0)),
            pl.BlockSpec((1, c, d), lambda k: (k, 0, 0)),
            pl.BlockSpec((1, c, d), lambda k: (k, 0, 0)),
            pl.BlockSpec((1, length, w), lambda k: (k, 0, 0)),
        ],
        out_specs=[
            pl.BlockSpec((1, c, d), lambda k: (k, 0, 0)),
            pl.BlockSpec((m, 1, c, w), lambda k: (0, k, 0, 0)),
        ],
        out_shape=[
            jax.ShapeDtypeStruct((m, c, d), bf16),
            jax.ShapeDtypeStruct((m, m, c, w), bf16),
        ],
        compiler_params=pltpu.CompilerParams(vmem_limit_bytes=VMEM_LIMIT),
    )(slot, span, qpad, dopad, kd)


def mlp_kernel(m_ref, dy_ref, low_ref, e_ref, we_ref, wr_ref, be_ref, bup_ref, adn_ref,
               y_ref, dm_ref, lowr_ref, er_ref, gup_ref, gdn_ref):
    j = pl.program_id(0)
    members, _, rows, fc = we_ref.shape
    we = we_ref[...].reshape(members * rows, fc)
    wr = wr_ref[...].reshape(fc, wr_ref.shape[3])
    bup, adn = bup_ref[0], adn_ref[0]
    hid = dot_nn(m_ref[...], we) + be_ref[0].astype(f32)
    hid = hid + scale_lora * dot_nn(low_ref[...], bup)
    cube = hid * hid * hid
    t = jnp.tanh(gelu_c * (hid + 0.044715 * cube))
    act = (0.5 * hid * (1.0 + t)).astype(bf16)
    slope = 0.5 * (1.0 + t) + 0.5 * hid * (1.0 - t * t) * (
        gelu_c * (1.0 + 3.0 * 0.044715 * hid * hid)
    )
    dact = dot_nt(dy_ref[...], wr) + dot_nn(e_ref[...], adn)
    dh = (dact * slope).astype(bf16)

    @pl.when(j == 0)
    def _():
        y_ref[...] = jnp.zeros_like(y_ref)
        dm_ref[...] = jnp.zeros_like(dm_ref)
        lowr_ref[...] = jnp.zeros_like(lowr_ref)
        er_ref[...] = jnp.zeros_like(er_ref)

    y_ref[...] += dot_nn(act, wr)
    dm_ref[...] += dot_nt(dh, we)
    lowr_ref[...] += dot_nt(act, adn)
    er_ref[...] += dot_nt(dh, bup)
    gup_ref[0] = scale_lora * dot_tn(low_ref[...], dh)
    gdn_ref[0] = dot_tn(e_ref[...], act)


def mlp(m, dy, low3, e4, we, wr, be, bup, adn):
    n, d = m.shape
    members, chunks, rows, fc = we.shape
    sub = wr.shape[2]
    rk = low3.shape[1]
    whole = lambda j: (0, 0)
    return pl.pallas_call(
        mlp_kernel,
        grid=(chunks,),
        in_specs=[
            pl.BlockSpec((n, d), whole),
            pl.BlockSpec((n, d), whole),
            pl.BlockSpec((n, rk), whole),
            pl.BlockSpec((n, rk), whole),
            pl.BlockSpec((members, 1, rows, fc), lambda j: (0, j, 0, 0)),
            pl.BlockSpec((members, 1, sub, d), lambda j: (0, j, 0, 0)),
            pl.BlockSpec((1, 1, fc), lambda j: (j, 0, 0)),
            pl.BlockSpec((1, rk, fc), lambda j: (j, 0, 0)),
            pl.BlockSpec((1, rk, fc), lambda j: (j, 0, 0)),
        ],
        out_specs=[
            pl.BlockSpec((n, d), whole),
            pl.BlockSpec((n, d), whole),
            pl.BlockSpec((n, rk), whole),
            pl.BlockSpec((n, rk), whole),
            pl.BlockSpec((1, rk, fc), lambda j: (j, 0, 0)),
            pl.BlockSpec((1, rk, fc), lambda j: (j, 0, 0)),
        ],
        out_shape=[
            jax.ShapeDtypeStruct((n, d), f32),
            jax.ShapeDtypeStruct((n, d), f32),
            jax.ShapeDtypeStruct((n, rk), f32),
            jax.ShapeDtypeStruct((n, rk), f32),
            jax.ShapeDtypeStruct((chunks, rk, fc), f32),
            jax.ShapeDtypeStruct((chunks, rk, fc), f32),
        ],
        compiler_params=pltpu.CompilerParams(vmem_limit_bytes=VMEM_LIMIT),
    )(m, dy, low3, e4, we, wr, be, bup, adn)


def norm_parts(v):
    center = v - jnp.mean(v, axis=-1, keepdims=True)
    inv = lax.rsqrt(jnp.mean(center * center, axis=-1, keepdims=True) + eps)
    return center * inv, inv


def norm_back(n, inv, gain, dn):
    w = gain * dn
    return (w - jnp.mean(w, axis=-1, keepdims=True)
            - n * jnp.mean(w * n, axis=-1, keepdims=True)) * inv


def local(tokens, out_grad, token_perm, seq_lens, adapter_ids,
          attn_g, attn_b, wq, bq, wkv, bv, wmix, bmix, mlp_g, mlp_b, wexp, bexp, wred, bred,
          q_dn, q_up, kv_dn, kv_up, mix_dn, mix_up, exp_dn, exp_up, red_dn, red_up):
    members = lax.axis_size("shard")
    replicas = lax.axis_size("rep")
    me = lax.axis_index("shard")
    rep = lax.axis_index("rep")
    length, d = tokens.shape
    cap = 3 * length // (2 * members)
    slots = members * cap
    block = me * replicas + rep
    experts, rank = q_dn.shape[:2]
    rk = experts * rank
    seqs = seq_lens.shape[1]
    projs = adapter_ids.shape[2]
    hd = bv.shape[0] * members
    heads = d // hd
    ff = wexp.shape[1]
    chunks = 8
    sub = ff // members // chunks
    fc = sub * members

    smalls = [attn_g, attn_b, bq, bmix, mlp_g, mlp_b, bred, bexp, bv]
    small = lax.all_gather(jnp.concatenate(smalls)[None], "shard", axis=0, tiled=True)
    wide = []
    at = 0
    for part in smalls:
        wide.append(small[:, at : at + part.shape[0]])
        at += part.shape[0]
    attn_gain, attn_bias, q_bias, mix_bias, mlp_gain, mlp_bias, red_bias = (
        w.reshape(-1).astype(f32) for w in wide[:7])
    be = wide[7].reshape(members, chunks, sub).transpose(1, 0, 2).reshape(chunks, 1, fc)
    v_bias = wide[8].reshape(-1).astype(f32)
    table = jnp.concatenate([seq_lens[0], adapter_ids[0].reshape(-1)])[None]
    table = lax.all_gather(table, "shard", axis=0, tiled=True)
    lens, ids = table[:, :seqs], table[:, seqs:].reshape(members, seqs, projs)

    attn_w = lax.all_gather(jnp.concatenate([wq, wkv, wmix], axis=1), "shard", axis=0, tiled=True)
    wq_f, wkv_f, wmix_f = attn_w[:, :d], attn_w[:, d : d + 2 * hd], attn_w[:, d + 2 * hd :]
    we_c = wexp.reshape(wexp.shape[0], members, chunks, sub).transpose(2, 0, 1, 3)
    we_f = lax.all_gather(we_c.reshape(chunks, wexp.shape[0], fc), "shard", axis=0, tiled=False)
    wr_f = lax.all_gather(wred.reshape(chunks, sub, d), "shard", axis=0, tiled=False)

    group = lax.dynamic_index_in_dim(
        token_perm.reshape(members, replicas, length), rep, 1, keepdims=False)
    src = group // (length * replicas)
    places = jnp.arange(length, dtype=jnp.int32)
    same = (src[:, :, None] == src[:, None, :]) & (places[None, None, :] < places[None, :, None])
    order = jnp.sum(same.astype(jnp.int32), axis=2)
    key_slot = (src * cap + order).reshape(members, 1, length)
    ends = jnp.sum(jnp.where(jnp.arange(seqs)[:, None] >= jnp.arange(seqs)[None, :],
                             lens[:, None, :], 0), axis=2)
    seg = jnp.sum((places[None, :, None] >= ends[:, None, :]).astype(jnp.int32), axis=2)
    start = jnp.sum(jnp.where(places[None, :, None] >= ends[:, None, :], lens[:, None, :], 0), axis=2)
    hit = (src == me)[:, None, :] & (order[:, None, :] == jnp.arange(cap)[None, :, None])

    def pick(values, empty):
        return jnp.sum(jnp.where(hit, values[:, None, :] - empty, 0), axis=2) + empty

    tok = pick(group - block * length, -1)
    lo = pick(start, 1)
    hi = pick(jnp.broadcast_to(places, group.shape), 0)
    span = jnp.stack([lo, hi], axis=2)
    slot_seg = pick(seg, 0)
    put = (tok.reshape(slots, 1) == places[None, :]).astype(bf16)
    seg_hits = slot_seg[:, :, None] == jnp.arange(seqs)[None, None, :]
    slot_ids = jnp.sum(jnp.where(seg_hits[:, :, :, None], ids[:, None, :, :], 0), axis=2)
    chosen = dot_tn(put, slot_ids.reshape(slots, projs).astype(bf16)).astype(jnp.int32)
    owner = jnp.arange(rk, dtype=jnp.int32) // rank
    masks = [(owner[None, :] == chosen[:, p : p + 1]).astype(f32) for p in range(projs)]

    flat = lambda s: s.reshape(rk, s.shape[2])
    q_dn, q_up, kv_dn, kv_up, mix_dn, mix_up, exp_dn, exp_up, red_dn, red_up = map(
        flat, (q_dn, q_up, kv_dn, kv_up, mix_dn, mix_up, exp_dn, exp_up, red_dn, red_up))
    by_chunk = lambda s: s.reshape(rk, members, chunks, sub).transpose(2, 0, 1, 3).reshape(chunks, rk, fc)

    x = tokens.astype(f32)
    nx, inv_x = norm_parts(x)
    a = (nx * attn_gain + attn_bias).astype(bf16)
    both = dot_nt(a, jnp.concatenate([q_dn, kv_dn], axis=0))
    low0 = (both[:, :rk] * masks[0]).astype(bf16)
    low1 = (both[:, rk:] * masks[1]).astype(bf16)
    q = (dot_nn(a, wq_f) + q_bias + scale_lora * dot_nn(low0, q_up)).astype(bf16)
    kv_bias = jnp.concatenate([jnp.zeros((hd,), f32), v_bias])
    kv = (dot_nn(a, wkv_f) + kv_bias + scale_lora * dot_nn(low1, kv_up)).astype(bf16)
    kvp = dot_nn(put, kv).astype(bf16).reshape(members, cap, 2 * hd)
    kvs = lax.all_gather(kvp, "shard", axis=0, tiled=False)
    qpad = dot_nn(put, q).astype(bf16).reshape(members, cap, d)
    opad, kd = attn_fwd(heads, key_slot, span, qpad, kvs)
    o = dot_tn(put, opad.reshape(slots, d)).astype(bf16)
    low2 = (dot_nt(o, mix_dn) * masks[2]).astype(bf16)
    resid = x + dot_nn(o, wmix_f) + mix_bias + scale_lora * dot_nn(low2, mix_up)

    nr, inv_r = norm_parts(resid)
    m = (nr * mlp_gain + mlp_bias).astype(bf16)
    low3 = (dot_nt(m, exp_dn) * masks[3]).astype(bf16)
    e4 = (scale_lora * dot_nt(out_grad, red_up) * masks[4]).astype(bf16)
    y, dm, low4, e3, g_exp_up, g_red_dn = mlp(
        m, out_grad, low3, e4, we_f, wr_f, be, by_chunk(exp_up), by_chunk(red_dn))
    low4 = (low4 * masks[4]).astype(bf16)
    layer_out = (resid + y + red_bias + scale_lora * dot_nn(low4, red_up)).astype(bf16)
    g_red_up = scale_lora * dot_tn(low4, out_grad)
    e3 = (scale_lora * e3 * masks[3]).astype(bf16)
    dm = dm + dot_nn(e3, exp_dn)
    g_exp_dn = dot_tn(e3, m)
    dres = out_grad.astype(f32) + norm_back(nr, inv_r, mlp_gain, dm)

    def to_share(g):
        return g.reshape(rk, members, -1).transpose(1, 0, 2)

    def chunk_share(g):
        return g.reshape(chunks, rk, members, sub).transpose(2, 1, 0, 3).reshape(members, rk, chunks * sub)

    def reduce(parts):
        sizes = [p.shape[2] for p in parts]
        got = lax.psum_scatter(jnp.concatenate(parts, axis=2), "shard", scatter_dimension=0, tiled=True)
        got = lax.psum(got[0], "rep")
        outs, at = [], 0
        for size in sizes:
            outs.append(got[:, at : at + size].reshape(experts, rank, size))
            at += size
        return outs

    r_exp_dn, r_exp_up, r_red_dn, r_red_up = reduce(
        [to_share(g_exp_dn), chunk_share(g_exp_up), chunk_share(g_red_dn), to_share(g_red_up)])

    dresl = dres.astype(bf16)
    e2 = (scale_lora * dot_nt(dresl, mix_up) * masks[2]).astype(bf16)
    do = (dot_nt(dresl, wmix_f) + dot_nn(e2, mix_dn)).astype(bf16)
    g_mix_dn = dot_tn(e2, o)
    g_mix_up = scale_lora * dot_tn(low2, dresl)
    dopad = dot_nn(put, do).astype(bf16).reshape(members, cap, d)
    dqpad, dslots = attn_bwd(heads, key_slot, span, qpad, dopad, kd)
    got = lax.all_to_all(dslots, "shard", split_axis=0, concat_axis=0, tiled=True)
    dkvp = jnp.sum(got.astype(f32), axis=0).astype(bf16).reshape(slots, 2 * hd)
    dq = dot_tn(put, dqpad.reshape(slots, d)).astype(bf16)
    dkv = dot_tn(put, dkvp).astype(bf16)
    e0 = (scale_lora * dot_nt(dq, q_up) * masks[0]).astype(bf16)
    e1 = (scale_lora * dot_nt(dkv, kv_up) * masks[1]).astype(bf16)
    da = (dot_nt(dq, wq_f) + dot_nn(e0, q_dn)) + (dot_nt(dkv, wkv_f) + dot_nn(e1, kv_dn))
    tokens_grad = (dres + norm_back(nx, inv_x, attn_gain, da)).astype(bf16)
    g_down = dot_tn(jnp.concatenate([e0, e1], axis=1), a)
    g_q_up = scale_lora * dot_tn(low0, dq)
    g_kv_up = scale_lora * dot_tn(low1, dkv)
    r_q_dn, r_q_up, r_kv_dn, r_kv_up, r_mix_dn, r_mix_up = reduce(
        [to_share(g_down[:rk]), to_share(g_q_up), to_share(g_down[rk:]), to_share(g_kv_up),
         to_share(g_mix_dn), to_share(g_mix_up)])
    return (layer_out, tokens_grad, r_q_dn, r_q_up, r_kv_dn, r_kv_up, r_mix_dn, r_mix_up,
            r_exp_dn, r_exp_up, r_red_dn, r_red_up)


def solution(mesh):
    both = ("shard", "rep")
    row, vec = P("shard", None), P("shard")
    in_specs = (
        P(both, None), P(both, None), P(), P(both, None), P(both, None, None),
        vec, vec, row, vec, row, vec, row, vec, vec, vec, row, vec, row, vec,
    ) + (P(),) * 10
    out_specs = (P(both, None), P(both, None)) + (P(None, None, "shard"),) * 10
    return jax.shard_map(local, mesh=mesh, in_specs=in_specs, out_specs=out_specs, check_vma=False)
```

time: 1130 us -> 941 us (0.83)
  matrix products: 263 us -> 111 us
  Pallas kernels: 0 us -> 147 us
  blocking collectives: 151 us -> 33.6 us
  local copies, waits for them, and re-layouts: 138 us -> 100 us
  waiting for transfers between devices: 476 us -> 490 us
  loops' own time: 13.9 us -> 0 us
  starting transfers between devices: 19.9 us -> 6.11 us
    dot_general x68 -> x30, matrix products: 263 us -> 105 us  [the longest x11 54.1 us: dot_nn(): lax.dot_general(a, b, (((1,), (0,)), ((), ())), preferred_element_type=f32)]
    all_gather x5 -> x4, waiting for transfers between devices: 163 us -> 313 us  [the longest x1 163 us: local(): lax.all_gather(we_c.reshape(chunks, wexp.shape[0], fc), 'shard', axis=0,...]
    pallas_call x0 -> x3, Pallas kernels: none -> 147 us  [the longest x1 91.8 us: mlp(): pl.pallas_call(mlp_kernel, grid=(chunks,), in_specs=[pl.BlockSpec((n, d),...]
    all_gather x8 -> x0, blocking collectives: 117 us -> none  [the longest x1 57.3 us: local(): lax.all_gather(mlp_norm_bias, 'shard', axis=0, tiled=True)]
    reduce_scatter x9 -> x2, waiting for transfers between devices: 162 us -> 84 us  [reduce(): lax.psum_scatter(jnp.concatenate(parts, axis=2), 'shard', scatter_dimensi...]
    all_to_all x4 -> x1, waiting for transfers between devices: 58 us -> 16 us  [local(): lax.all_to_all(dslots, 'shard', split_axis=0, concat_axis=0, tiled=True)]
    unnamed x17 -> x7, waiting for transfers between devices: 40 us -> 0.78 us
    scatter x4 -> x0, local copies, waits for them, and re-layouts: 34.8 us -> none  [the longest x3 19.3 us: pack_rows(): buffer = jnp.zeros((members * capacity, row_data.shape[1]), row_data.dtyp...]
  transfers between devices with their start and end apart: 20 -> 8, of which waited for: 10 -> 6; matrix products, arithmetic and copies ran while one was open for 37% -> 18% of each run, Pallas kernels for 0% -> 2%
where the time goes in v1:
time: 941 us; the launch traced here: 932 us
  waiting for transfers between devices  490 us (52%)
  Pallas kernels  147 us (16%)
  matrix products  111 us (12%)
  local copies, waits for them, and re-layouts  100 us (11%)
  blocking collectives  33.6 us (4%)
  other arithmetic  27.3 us (3%)
  between operations  16.7 us (2%)
    all_gather x1, waiting for transfers between devices, local(): lax.all_gather(we_c.reshape(chunks, wexp.shape[0], fc), 'shard', axis=0,...  163 us
    all_gather x1, waiting for transfers between devices, local(): lax.all_gather(wred.reshape(chunks, sub, d), 'shard', axis=0, tiled=False)  102 us
    pallas_call x1, Pallas kernels, mlp(): pl.pallas_call(mlp_kernel, grid=(chunks,), in_specs=[pl.BlockSpec((n, d),...  91.8 us
    reduce_scatter x2, waiting for transfers between devices, reduce(): lax.psum_scatter(jnp.concatenate(parts, axis=2), 'shard', scatter_dimensi...  84 us
    psum x1, waiting for transfers between devices, reduce(): got = lax.psum(got[0], 'rep')  76.3 us
    dot_general x11, matrix products, dot_nn(): lax.dot_general(a, b, (((1,), (0,)), ((), ())), preferred_element_type=f32)  54.1 us
    all_gather x1, waiting for transfers between devices, local(): lax.all_gather(jnp.concatenate([wq, wkv, wmix], axis=1), 'shard', axis=0,...  48.4 us
    unnamed x156, local copies, waits for them, and re-layouts  36.5 us
  transfers between devices with their start and end apart: 8, of which 6 were waited for; matrix products, arithmetic and copies ran while one was open for 18% of the time, Pallas kernels for 2%

profile of v1, /device:TPU:0, one launch (start us, length us, event | category | flops | bytes accessed | tf_op | source)
XLA Modules:
  0.0 931.8 jit_solution(2631402870010250747)
XLA Ops:
  7.4 3.3 pad_maximum_fusion.1
  12.9 9.5 %all-reduce.1 = s32[192]{0:T(256)S(1)} all-reduce(s32[192]{0:T(256)S(1)} %add_dynamic-update-slice_fusion), channel_id=2, replica_groups=mesh['shard'=8,'rep'=4] {'shard'}, use_global_device_ids=true, to_apply=%add.1 | all-reduce | flops 192 | bytes 1536
  25.1 24.1 %all-reduce.2 = bf16[22656]{0:T(1024)(128)(2,1)S(1)} all-reduce(bf16[22656]{0:T(1024)(128)(2,1)S(1)} %dynamic-update-slice.1), channel_id=3, replica_groups=mesh['shard'=8,'rep'=4] {'shard'}, use_global_device_ids=true, to_apply=%add.2 | all-reduce | flops 22656 | bytes 90624
  50.6 2.3 convert_reduce_fusion
  60.2 48.4 %all-gather.7.cloned.1.call-done = bf16[2048,4352]{1,0:T(8,128)(2,1)} async-done(((bf16[256,4352]{1,0:T(8,128)(2,1)}), bf16[2048,4352]{1,0:T(8,128)(2,1)}) %all-gather.7.cloned.1.call-update) | async-done | bytes 17825808 | tf_op jit(solution)/shard_map/all_gather | solution.py:262
  108.6 4.0 fusion.27
  114.0 3.4 copy.182
  117.4 2.7 copy.195
  120.1 7.3 all_gather_reshape.10
  129.1 2.2 copy.183
  131.3 1.7 copy.197
  132.9 4.2 reshape.352.bup_ref
  137.1 2.2 copy.184
  139.3 1.7 copy.196
  141.0 4.2 reshape.353.adn_ref
  145.8 3.0 fusion.40.e_ref
  148.8 10.6 %fusion.6 = f32[512,2048]{1,0:T(8,128)} fusion(bf16[512,2048]{1,0:T(8,128)(2,1)} %copy-done.10, bf16[2048,4352]{1,0:T(8,128)(2,1)} %all-gather.7.cloned.1.call-done), kind=kOutput, calls=%fused_computation.8 | convolution fusion | flops 4294967296 | bytes 14680064 | tf_op jit(solution)/shard_map/dot_general | solution.py:18
  159.4 7.2 convolution_convert_fusion.1
  166.6 22.0 %shard_map.364 = (bf16[8,96,2048]{2,1,0:T(8,128)(2,1)}, bf16[8,512,256]{2,1,0:T(8,128)(2,1)}) custom-call(s32[8,1,512]{2,1,0:T(1,128)} %reshape_add_fusion.refs_0_, s32[8,96,2]{2,1,0:T(8,128)} %copy.135.refs_1_, bf16[8,96,2048]{2,1,0:T(8,128)(2,1)} %bitcast.204, bf16[8,8,96,256]{3,2,1,0:T(8,128)(2,1)} %all-gather.9.cloned.1.call-done.refs_3_), custom_call_target="tpu_custom_call" | custom-call | tf_op jit(solution)/shard_map/pallas_call | solution.py:94
  188.6 3.8 convolution_convert_fusion.3
  193.2 7.0 fusion.2
  203.4 1.4 copy-done.8
  204.8 1.4 fusion.36.low_ref
  206.2 101.7 %all-gather.13.cloned.1.call-done.wr_ref = bf16[8,8,128,2048]{3,2,1,0:T(8,128)(2,1)} async-done(((bf16[1,8,128,2048]{3,2,1,0:T(8,128)(2,1)}), bf16[8,8,128,2048]{3,2,1,0:T(8,128)(2,1)}) %all-gather.13.cloned.1.call-update) | async-done | bytes 33554448 | tf_op jit(solution)/shard_map/all_gather | solution.py:266
  307.9 162.6 %all-gather.11.cloned.1.call-done.we_ref = bf16[8,8,256,1024]{3,2,1,0:T(8,128)(2,1)} async-done(((bf16[1,8,256,1024]{3,2,1,0:T(8,128)(2,1)}), bf16[8,8,256,1024]{3,2,1,0:T(8,128)(2,1)}) %all-gather.11.cloned.1.call-update) | async-done | bytes 33554448 | tf_op jit(solution)/shard_map/all_gather | solution.py:265
  470.4 91.8 %shard_map.365 = (f32[512,2048]{1,0:T(8,128)}, f32[512,2048]{1,0:T(8,128)}, f32[512,128]{1,0:T(8,128)}, f32[512,128]{1,0:T(8,128)}, f32[8,128,1024]{2,1,0:T(8,128)}, /*index=5*/f32[8,128,1024]{2,1,0:T(8,128)}) custom-call(bf16[512,2048]{1,0:T(8,128)(2,1)} %copy-done.8, bf16[512,2048]{1,0:T(8,128)(2,1)} %dy_ref.1, bf16[512,128]{1,0:T(8,128)(2,1)} %fusion.36.low_ref, ...), custom_call_target="tpu_custom_call" | custom-call | tf_op jit(solution)/shard_map/pallas_call | solution.py:179
  562.3 5.1 fusion.86
  567.7 1.8 multiply_add_fusion
  571.5 9.8 %fusion = f32[512,2048]{1,0:T(8,128)} fusion(bf16[2048,4352]{1,0:T(8,128)(2,1)} %all-gather.7.cloned.1.call-done, f32[512,2048]{1,0:T(8,128)S(1)} %multiply_add_fusion), kind=kOutput, calls=%fused_computation.2 | convolution fusion | flops 4296015872 | bytes 16777216 | tf_op jit(solution)/shard_map/dot_general | solution.py:22
  581.3 6.3 convolution_convert_fusion
  587.6 32.8 %shard_map.366 = (bf16[8,96,2048]{2,1,0:T(8,128)(2,1)}, bf16[8,8,96,256]{3,2,1,0:T(8,128)(2,1)}) custom-call(s32[8,1,512]{2,1,0:T(1,128)} %reshape_add_fusion.refs_0_, s32[8,96,2]{2,1,0:T(8,128)} %copy.135.refs_1_, bf16[8,96,2048]{2,1,0:T(8,128)(2,1)} %bitcast.205, bf16[8,96,2048]{2,1,0:T(8,128)(2,1)} %bitcast.221, ...), custom_call_target="tpu_custom_call" | custom-call | tf_op jit(solution)/shard_map/pallas_call | solution.py:118
  620.4 4.4 all-to-all-start
  625.3 3.6 convolution_multiply_fusion.1
  629.0 2.5 copy.169
  631.5 3.9 convolution_convert_fusion.2
  635.4 1.3 copy-done.14
  636.7 1.5 convolution_multiply_fusion.2
  638.2 2.5 copy.166
  640.7 2.4 fusion.38
  643.1 3.6 fusion.94
  646.7 16.0 %all-to-all-done = bf16[8,8,96,256]{3,2,1,0:T(8,128)(2,1)} async-done(((bf16[8,8,96,256]{3,2,1,0:T(8,128)(2,1)}), bf16[8,8,96,256]{3,2,1,0:T(8,128)(2,1)}, u32[]{:S(2)}, u32[]{:S(2)}) %all-to-all-start) | async-done | bytes 3145760 | tf_op jit(solution)/shard_map/all_to_all | solution.py:358
  662.7 2.4 reduce_sum.183
  667.9 2.3 fusion.61
  670.3 1.5 fusion.87
  671.7 2.5 copy.167
  674.3 2.5 copy.165
  676.8 2.4 constant_dynamic-update-slice_fusion.5
  679.2 2.3 constant_dynamic-update-slice_fusion.4
  685.7 3.1 convolution_multiply_fusion
  688.9 2.5 copy.171
  691.4 5.8 copy.186
  697.2 5.6 copy.156
  702.8 5.2 copy.187
  708.0 5.7 copy.157
  713.7 2.6 fusion.77
  716.3 7.9 pad_maximum_fusion
  725.0 3.9 fusion.93
  728.9 4.5 add_convert_fusion.1
  733.4 9.5 %fusion.4 = f32[512,2048]{1,0:T(8,128)} fusion(bf16[512,2048]{1,0:T(8,128)(2,1)S(1)} %copy-done.15, bf16[2048,4352]{1,0:T(8,128)(2,1)} %all-gather.7.cloned.1.call-done), kind=kOutput, calls=%fused_computation.6 | convolution fusion | flops 4294967296 | bytes 14680064 | tf_op jit(solution)/shard_map/dot_general | solution.py:22
  742.9 84.0 %reduce-scatter.5.cloned.1.call-done = f32[1,128,2560]{1,2,0:T(8,128)} async-done(((f32[8,128,2560]{1,2,0:T(8,128)}), f32[1,128,2560]{1,2,0:T(8,128)}) %reduce-scatter.5.cloned.1.call-update) | async-done | bytes 1310736 | tf_op jit(solution)/shard_map/reduce_scatter | solution.py:340
  827.0 2.1 fusion.46
  829.5 4.0 fusion.85
  833.5 2.7 fusion.19
  836.2 76.3 %all-reduce.6.cloned.1.call-done = (f32[128,1312]{0,1:T(8,128)}, f32[128,2560]{0,1:T(8,128)}) async-done(((f32[128,1312]{0,1:T(8,128)}, f32[128,2560]{0,1:T(8,128)}), (f32[128,1312]{0,1:T(8,128)}, f32[128,2560]{0,1:T(8,128)})) %all-reduce.6.cloned.1.call-update) | async-done | bytes 1982480 | tf_op jit(solution)/shard_map/psum | solution.py:341
  (238 shorter events, 42.5 us)
Async XLA Ops:
  7.2 185.2 %copy-start = (bf16[8,16,2048]{2,1,0:T(8,128)(2,1)S(1)}, bf16[8,16,2048]{2,1,0:T(8,128)(2,1)}, u32[]{:S(2)}) copy-start(bf16[8,16,2048]{2,1,0:T(8,128)(2,1)} %param.52) | copy-start | bytes 1572868
  7.2 3.6 copy-start.61
  7.2 5.5 copy-start.49
  7.2 5.5 copy-start.59
  7.2 15.6 %copy-start.51 = (bf16[256]{0:T(256)(128)(2,1)S(1)}, bf16[256]{0:T(256)(128)(2,1)}, u32[]{:S(2)}) copy-start(bf16[256]{0:T(256)(128)(2,1)} %param.34) | copy-start | bytes 1540
  7.2 15.8 %copy-start.52 = (bf16[256]{0:T(256)(128)(2,1)S(1)}, bf16[256]{0:T(256)(128)(2,1)}, u32[]{:S(2)}) copy-start(bf16[256]{0:T(256)(128)(2,1)} %param.35) | copy-start | bytes 1540
  7.3 16.0 %copy-start.53 = (bf16[256]{0:T(256)(128)(2,1)S(1)}, bf16[256]{0:T(256)(128)(2,1)}, u32[]{:S(2)}) copy-start(bf16[256]{0:T(256)(128)(2,1)} %param.37) | copy-start | bytes 1540
  7.3 16.2 %copy-start.54 = (bf16[256]{0:T(256)(128)(2,1)S(1)}, bf16[256]{0:T(256)(128)(2,1)}, u32[]{:S(2)}) copy-start(bf16[256]{0:T(256)(128)(2,1)} %param.41) | copy-start | bytes 1540
  7.3 16.4 %copy-start.55 = (bf16[256]{0:T(256)(128)(2,1)S(1)}, bf16[256]{0:T(256)(128)(2,1)}, u32[]{:S(2)}) copy-start(bf16[256]{0:T(256)(128)(2,1)} %param.42) | copy-start | bytes 1540
  7.3 16.7 %copy-start.56 = (bf16[256]{0:T(256)(128)(2,1)S(1)}, bf16[256]{0:T(256)(128)(2,1)}, u32[]{:S(2)}) copy-start(bf16[256]{0:T(256)(128)(2,1)} %param.43) | copy-start | bytes 1540
  7.3 16.9 %copy-start.57 = (bf16[256]{0:T(256)(128)(2,1)S(1)}, bf16[256]{0:T(256)(128)(2,1)}, u32[]{:S(2)}) copy-start(bf16[256]{0:T(256)(128)(2,1)} %param.47) | copy-start | bytes 1540
  7.3 17.1 %copy-start.50 = (bf16[1024]{0:T(1024)(128)(2,1)S(1)}, bf16[1024]{0:T(1024)(128)(2,1)}, u32[]{:S(2)}) copy-start(bf16[1024]{0:T(1024)(128)(2,1)} %param.45) | copy-start | bytes 6148
  7.3 17.3 %copy-start.58 = (bf16[16]{0:T(256)(128)(2,1)S(1)}, bf16[16]{0:T(256)(128)(2,1)}, u32[]{:S(2)}) copy-start(bf16[16]{0:T(256)(128)(2,1)} %param.39) | copy-start | bytes 100
  7.3 42.7 %copy-start.35 = (s32[16384]{0:T(1024)S(1)}, s32[16384]{0:T(1024)}, u32[]{:S(2)}) copy-start(s32[16384]{0:T(1024)} %param.31) | copy-start | bytes 196612
  7.3 47.5 %copy-start.4 = (bf16[512,2048]{1,0:T(8,128)(2,1)S(1)}, bf16[512,2048]{1,0:T(8,128)(2,1)}, u32[]{:S(2)}) copy-start(bf16[512,2048]{1,0:T(8,128)(2,1)} %param.29) | copy-start | bytes 6291460
  7.3 101.3 %all-gather.7.cloned.1.call-start = ((), (), s32[]{:S(2)}) async-start(), calls=%async_computation.3 | async-start | bytes 20054016 | tf_op jit(solution)/shard_map/all_gather | solution.py:262
  10.7 155.9 %all-gather.9.cloned.1.call-start = ((), (), s32[]{:S(2)}) async-start(), calls=%async_computation.4 | async-start | bytes 3538944 | tf_op jit(solution)/shard_map/all_gather | solution.py:311
  50.1 7.7 copy-start.31
  54.3 3.5 copy-start.45
  54.9 4.3 copy-start.22
  54.9 4.3 copy-start.25
  55.2 4.7 copy-start.36
  55.9 4.0 copy-start.39
  57.0 3.0 copy-start.41
  57.8 2.1 copy-start.33
  57.9 50.8 %copy-start.46 = (s32[768]{0:T(1024)S(1)}, s32[768]{0:T(1024)}, u32[]{:S(2)}) copy-start(s32[768]{0:T(1024)} %copy-done.45) | copy-start | bytes 9220
  59.9 99.5 %copy-start.27 = (bf16[512,256]{1,0:T(8,128)(2,1)}, bf16[512,256]{1,0:T(8,128)(2,1)S(1)}, u32[]{:S(2)}) copy-start(bf16[512,256]{1,0:T(8,128)(2,1)S(1)} %fusion.42) | copy-start | bytes 786436
  112.7 195.2 %all-gather.13.cloned.1.call-start = ((), (), s32[]{:S(2)}) async-start(), calls=%async_computation.6 | async-start | bytes 37748736 | tf_op jit(solution)/shard_map/all_gather | solution.py:266
  113.4 357.0 %all-gather.11.cloned.1.call-start = ((), (), s32[]{:S(2)}) async-start(), calls=%async_computation.5 | async-start | bytes 37748736 | tf_op jit(solution)/shard_map/all_gather | solution.py:265
  139.3 6.5 copy-start.23
  148.8 10.6 %copy-start.43 = (s32[512,1]{0,1:T(1,128)S(1)}, s32[512,1]{0,1:T(1,128)}, u32[]{:S(2)}) copy-start(s32[512,1]{0,1:T(1,128)} %get-tuple-element.82) | copy-start | bytes 6148
  148.8 10.6 %copy-start.47 = (s32[768]{0:T(1024)S(1)}, s32[768]{0:T(1024)}, u32[]{:S(2)}) copy-start(s32[768]{0:T(1024)} %copy-done.45) | copy-start | bytes 9220
  148.8 10.6 %copy-start.60 = (bf16[8,16,2048]{2,1,0:T(8,128)(2,1)S(1)}, bf16[8,16,2048]{2,1,0:T(8,128)(2,1)}, u32[]{:S(2)}) copy-start(bf16[8,16,2048]{2,1,0:T(8,128)(2,1)} %param.49) | copy-start | bytes 1572868
  188.6 3.9 copy-start.44
  192.4 7.8 copy-start.16
  193.2 7.0 copy-start.17
  201.4 2.1 copy-start.1
  201.9 2.9 copy-start.20
  470.4 91.9 %copy-start.21 = (bf16[8,16,2048]{2,1,0:T(8,128)(2,1)S(1)}, bf16[8,16,2048]{2,1,0:T(8,128)(2,1)}, u32[]{:S(2)}) copy-start(bf16[8,16,2048]{2,1,0:T(8,128)(2,1)} %param.54) | copy-start | bytes 1572868
  562.3 5.2 copy-start.2
  562.3 5.4 copy-start.7
  569.5 2.0 copy-start.5
  571.5 9.8 %copy-start.48 = (s32[768]{0:T(1024)S(1)}, s32[768]{0:T(1024)}, u32[]{:S(2)}) copy-start(s32[768]{0:T(1024)} %copy-done.45) | copy-start | bytes 9220
  620.4 42.3 %all-to-all-start = ((bf16[8,8,96,256]{3,2,1,0:T(8,128)(2,1)}), bf16[8,8,96,256]{3,2,1,0:T(8,128)(2,1)}, u32[]{:S(2)}, u32[]{:S(2)}) async-start(bf16[8,8,96,256]{3,2,1,0:T(8,128)(2,1)} %get-tuple-element.29), calls=%async_computation | async-start | bytes 6291456 | tf_op jit(solution)/shard_map/all_to_all | solution.py:358
  624.8 118.1 %reduce-scatter.3.cloned.1.call-start = ((), (), s32[]{:S(2)}) async-start(), calls=%async_computation.7 | async-start | bytes 6045696 | tf_op jit(solution)/shard_map/reduce_scatter | solution.py:340
  631.5 5.2 copy-start.28
  643.1 22.8 %copy-start.34 = (bf16[8,16,256]{2,1,0:T(8,128)(2,1)S(1)}, bf16[8,16,256]{2,1,0:T(8,128)(2,1)}, u32[]{:S(2)}) copy-start(bf16[8,16,256]{2,1,0:T(8,128)(2,1)} %param.51) | copy-start | bytes 196612
  643.1 22.8 %copy-start.42 = (s32[512,1]{0,1:T(1,128)S(1)}, s32[512,1]{0,1:T(1,128)}, u32[]{:S(2)}) copy-start(s32[512,1]{0,1:T(1,128)} %copy-done.41) | copy-start | bytes 6148
  676.8 4.8 copy-start.13
  676.8 6.5 copy-start.11
  676.8 7.6 copy-start.12
  685.5 141.4 %reduce-scatter.5.cloned.1.call-start = ((), (), s32[]{:S(2)}) async-start(), calls=%async_computation.8 | async-start | bytes 11796480 | tf_op jit(solution)/shard_map/reduce_scatter | solution.py:340
  708.0 5.7 copy-start.19
  724.3 188.2 %all-reduce.6.cloned.1.call-start = ((), (), s32[]{:S(2)}) async-start(), calls=%async_computation.9 | async-start | bytes 3964928 | tf_op jit(solution)/shard_map/psum | solution.py:341
  724.6 4.4 copy-start.3
  724.6 4.3 copy-start.24
  728.9 4.5 copy-start.15
  733.4 93.6 %copy-start.30 = (bf16[512,256]{1,0:T(8,128)(2,1)S(1)}, bf16[512,256]{1,0:T(8,128)(2,1)}, u32[]{:S(2)}) copy-start(bf16[512,256]{1,0:T(8,128)(2,1)} %copy-done.29) | copy-start | bytes 786436
  742.9 86.2 %copy-start.26 = (bf16[8,16,2048]{2,1,0:T(8,128)(2,1)S(1)}, bf16[8,16,2048]{2,1,0:T(8,128)(2,1)}, u32[]{:S(2)}) copy-start(bf16[8,16,2048]{2,1,0:T(8,128)(2,1)} %param.50) | copy-start | bytes 1572868
  742.9 86.2 %copy-start.32 = (f32[1,2,8,128]{3,1,2,0:T(2,128)S(1)}, f32[1,2,8,128]{3,1,2,0:T(2,128)}, u32[]{:S(2)}) copy-start(f32[1,2,8,128]{3,1,2,0:T(2,128)} %copy-done.31) | copy-start | bytes 24580
  742.9 86.2 %copy-start.37 = (f32[512]{0:T(512)S(1)}, f32[512]{0:T(512)}, u32[]{:S(2)}) copy-start(f32[512]{0:T(512)} %copy-done.36) | copy-start | bytes 6148
  742.9 86.2 %copy-start.40 = (f32[512]{0:T(512)S(1)}, f32[512]{0:T(512)}, u32[]{:S(2)}) copy-start(f32[512]{0:T(512)} %copy-done.39) | copy-start | bytes 6148
  827.0 2.5 copy-start.9
  829.5 4.0 copy-start.6
  (6 other events, 6.7 us)
Sparse Core Ops, SparseCore 0:
  10.8 97.7 all-gather.6
  112.8 32.3 all-gather.8
  147.0 160.7 all-gather.12
  309.6 160.7 all-gather.10
  685.6 56.2 reduce-scatter.2
  745.3 81.5 reduce-scatter.4
  829.4 83.0 all-reduce.5

commit v2 on v1

--- a/solution.py
+++ b/solution.py
@@ -137,77 +137,284 @@
     )(slot, span, qpad, dopad, kd)
 
 
-def mlp_kernel(m_ref, dy_ref, low_ref, e_ref, we_ref, wr_ref, be_ref, bup_ref, adn_ref,
-               y_ref, dm_ref, lowr_ref, er_ref, gup_ref, gdn_ref):
-    j = pl.program_id(0)
-    members, _, rows, fc = we_ref.shape
-    we = we_ref[...].reshape(members * rows, fc)
-    wr = wr_ref[...].reshape(fc, wr_ref.shape[3])
-    bup, adn = bup_ref[0], adn_ref[0]
-    hid = dot_nn(m_ref[...], we) + be_ref[0].astype(f32)
-    hid = hid + scale_lora * dot_nn(low_ref[...], bup)
-    cube = hid * hid * hid
-    t = jnp.tanh(gelu_c * (hid + 0.044715 * cube))
-    act = (0.5 * hid * (1.0 + t)).astype(bf16)
-    slope = 0.5 * (1.0 + t) + 0.5 * hid * (1.0 - t * t) * (
-        gelu_c * (1.0 + 3.0 * 0.044715 * hid * hid)
-    )
-    dact = dot_nt(dy_ref[...], wr) + dot_nn(e_ref[...], adn)
-    dh = (dact * slope).astype(bf16)
-
-    @pl.when(j == 0)
-    def _():
-        y_ref[...] = jnp.zeros_like(y_ref)
-        dm_ref[...] = jnp.zeros_like(dm_ref)
-        lowr_ref[...] = jnp.zeros_like(lowr_ref)
-        er_ref[...] = jnp.zeros_like(er_ref)
-
-    y_ref[...] += dot_nn(act, wr)
-    dm_ref[...] += dot_nt(dh, we)
-    lowr_ref[...] += dot_nt(act, adn)
-    er_ref[...] += dot_nt(dh, bup)
-    gup_ref[0] = scale_lora * dot_tn(low_ref[...], dh)
-    gdn_ref[0] = dot_tn(e_ref[...], act)
-
-
-def mlp(m, dy, low3, e4, we, wr, be, bup, adn):
+class Gather:
+    def __init__(self, members, own, full, send_sem, recv_sem):
+        self.members = members
+        self.me, self.rep = lax.axis_index("shard"), lax.axis_index("rep")
+        self.own, self.full = own, full
+        self.send_sem, self.recv_sem = send_sem, recv_sem
+        self.bits = [1 << i for i in range(1, members.bit_length() - 1)]
+        self.planes = [o for o in range(0, members, 2)]
+        self.sent = {}
+
+    def partners(self):
+        near = [(self.me ^ b, self.rep) for b in [1] + self.bits]
+        return near + [(self.me, self.rep ^ 1)]
+
+    def place(self, kind, slot, offset):
+        return self.full[kind].at[slot, self.me ^ offset]
+
+    def copy(self, kind, slot, offset, there, to, from_own, to_slot):
+        mine = self.sent.setdefault((kind, slot), {})
+        at = mine.setdefault((offset, there, to_slot), len(mine))
+        src = self.own[kind](slot) if from_own else self.place(kind, slot, offset)
+        cp = pltpu.make_async_remote_copy(
+            src, self.full[kind].at[to_slot, self.me ^ offset],
+            self.send_sem.at[kind, slot, at], self.recv_sem.at[kind, to_slot, there],
+            device_id=to, device_id_type=pl.DeviceIdType.MESH)
+        cp.start()
+
+    def wait(self, kind, slot, offset):
+        piece = self.place(kind, slot, offset)
+        pltpu.make_async_copy(piece, piece, self.recv_sem.at[kind, slot, offset]).wait()
+
+    def order(self, kind):
+        return self.bits if kind % 2 == 0 else self.bits[::-1]
+
+    def stage(self, kind, offset):
+        return max(i for i, b in enumerate(self.order(kind)) if offset & b)
+
+    def issue(self, slot, kinds, plane=True):
+        for kind in kinds:
+            if plane:
+                for b in self.order(kind):
+                    self.copy(kind, slot, 0, b, (self.me ^ b, self.rep), True, slot)
+        for kind in kinds:
+            self.copy(kind, slot, 0, 1, (self.me ^ 1, self.rep), True, slot)
+
+    def arrive(self, slot, kinds, direct, swap_to=None):
+        for kind in kinds:
+            order = self.order(kind)
+            some = [o for o in self.planes if o and (bin(o).count("1") == 1) == direct]
+            some.sort(key=lambda o: self.stage(kind, o))
+            for o in some:
+                self.wait(kind, slot, o)
+                for i in range(self.stage(kind, o) + 1, len(order)):
+                    self.copy(kind, slot, o, o ^ order[i], (self.me ^ order[i], self.rep), False, slot)
+                if swap_to is not None:
+                    self.copy(kind, slot, o, o, (self.me, self.rep ^ 1), False, swap_to)
+                self.copy(kind, slot, o, o ^ 1, (self.me ^ 1, self.rep), False, slot)
+
+    def swapped(self, slot, kinds):
+        for kind in kinds:
+            for o in self.planes:
+                if o:
+                    self.wait(kind, slot, o)
+                    self.copy(kind, slot, o, o ^ 1, (self.me ^ 1, self.rep), False, slot)
+
+    def ready(self, slot, kinds):
+        for kind in kinds:
+            for o in range(1, self.members, 2):
+                self.wait(kind, slot, o)
+
+    def finish(self):
+        for (kind, slot), mine in self.sent.items():
+            piece = self.place(kind, slot, 0)
+            for at in mine.values():
+                pltpu.make_async_copy(piece, piece, self.send_sem.at[kind, slot, at]).wait()
+
+
+U, V, C = (0, 1, 2), (3, 4, 5), (6, 7)
+SLOTS = 8
+BOTH = (0, 1)
+
+
+def chunk_of(slot, parity):
+    slot = jnp.int32(slot)
+    low = jnp.where(slot < 3, slot, slot + 2)
+    high = jnp.where(slot < 3, slot + 5, slot - 3)
+    return jnp.where(slot >= 6, slot - 3, jnp.where(parity == 0, low, high))
+
+
+MLP_ORDER = (0, 1, 3, 2, 6, 4, 7, 5)
+
+
+def mlp_kernel(members, m_ref, dy_ref, low_ref, e_ref, we_ref, wr_ref, be_ref, bup_ref, adn_ref,
+               y_ref, dm_ref, lowr_ref, er_ref, gup_ref, gdn_ref, ge_ref, gr_ref,
+               we_v, wr_v, send_sem, recv_sem, load_sem):
+    parity = lax.rem(lax.axis_index("rep"), 2)
+    g = Gather(members,
+               (lambda slot: we_ref.at[chunk_of(slot, parity)], lambda slot: wr_ref.at[chunk_of(slot, parity)]),
+               (ge_ref, gr_ref), send_sem, recv_sem)
+    barrier = pltpu.get_barrier_semaphore()
+    for to in g.partners():
+        pl.semaphore_signal(barrier, inc=1, device_id=to, device_id_type=pl.DeviceIdType.MESH)
+    pl.semaphore_wait(barrier, len(g.partners()))
+
+    g.issue(U[0], BOTH)
+    y_ref[...] = jnp.zeros_like(y_ref)
+    dm_ref[...] = jnp.zeros_like(dm_ref)
+    lowr_ref[...] = jnp.zeros_like(lowr_ref)
+    er_ref[...] = jnp.zeros_like(er_ref)
+    def load(slot, buf):
+        out = []
+        for kind, held in enumerate((we_v, wr_v)):
+            for o in range(members):
+                src = g.own[kind](slot) if o == 0 else g.place(kind, slot, o)
+                out.append(pltpu.make_async_copy(src, held.at[buf, g.me ^ o], load_sem.at[kind, buf, o]))
+        return out
+
+    def fetch(slot, buf):
+        g.ready(slot, BOTH)
+        for cp in load(slot, buf):
+            cp.start()
+
+    def before(i):
+        if i == 0:
+            g.arrive(U[0], BOTH, True, V[0])
+            g.issue(U[1], BOTH)
+            g.arrive(U[0], BOTH, False, V[0])
+            for slot in V:
+                g.issue(slot, BOTH, False)
+        if i == 1:
+            g.arrive(U[1], BOTH, True, V[1])
+            g.issue(U[2], BOTH)
+            g.arrive(U[1], BOTH, False, V[1])
+        if i == 2:
+            g.swapped(V[0], BOTH)
+        if i == 3:
+            g.arrive(U[2], BOTH, True, V[2])
+            g.issue(C[0], BOTH)
+            g.arrive(U[2], BOTH, False, V[2])
+        if i == 4:
+            g.arrive(C[0], BOTH, True)
+            g.issue(C[1], BOTH)
+            g.arrive(C[0], BOTH, False)
+        if i == 5:
+            g.swapped(V[1], BOTH)
+        if i == 6:
+            g.arrive(C[1], BOTH, True)
+            g.arrive(C[1], BOTH, False)
+        if i == 7:
+            g.swapped(V[2], BOTH)
+        fetch(MLP_ORDER[i], i % 2)
+
+    def step(n, _):
+        buf = lax.rem(n, 2)
+        slot = jnp.int32(0)
+        for i, q in enumerate(MLP_ORDER):
+            slot = jnp.where(n == i, q, slot)
+        for cp in load(slot, buf):
+            cp.wait()
+        j = chunk_of(slot, parity)
+        rows, fc = we_v.shape[2], we_v.shape[3]
+        we = we_v[buf].reshape(members * rows, fc)
+        wr = wr_v[buf].reshape(fc, wr_v.shape[3])
+        bup, adn = bup_ref[j], adn_ref[j]
+        hid = dot_nn(m_ref[...], we) + be_ref[j].astype(f32)
+        hid = hid + scale_lora * dot_nn(low_ref[...], bup)
+        cube = hid * hid * hid
+        t = jnp.tanh(gelu_c * (hid + 0.044715 * cube))
+        act = (0.5 * hid * (1.0 + t)).astype(bf16)
+        slope = 0.5 * (1.0 + t) + 0.5 * hid * (1.0 - t * t) * (
+            gelu_c * (1.0 + 3.0 * 0.044715 * hid * hid)
+        )
+        dact = dot_nt(dy_ref[...], wr) + dot_nn(e_ref[...], adn)
+        dh = (dact * slope).astype(bf16)
+        for i in range(1, SLOTS):
+            pl.when(n == i - 1)(lambda i=i: before(i))
+        y_ref[...] += dot_nn(act, wr)
+        dm_ref[...] += dot_nt(dh, we)
+        lowr_ref[...] += dot_nt(act, adn)
+        er_ref[...] += dot_nt(dh, bup)
+        gup = (scale_lora * dot_tn(low_ref[...], dh)).astype(bf16)
+        gdn = dot_tn(e_ref[...], act).astype(bf16)
+        sub = fc // members
+        for to in range(members):
+            gup_ref[to, j] = gup[:, to * sub : (to + 1) * sub]
+            gdn_ref[to, j] = gdn[:, to * sub : (to + 1) * sub]
+        return 0
+
+    before(0)
+    lax.fori_loop(0, SLOTS, step, 0)
+    g.finish()
+
+
+def mlp(members, m, dy, low3, e4, we, wr, be, bup, adn):
     n, d = m.shape
-    members, chunks, rows, fc = we.shape
-    sub = wr.shape[2]
+    chunks, rows, fc = we.shape
+    sub = wr.shape[1]
     rk = low3.shape[1]
-    whole = lambda j: (0, 0)
+    vm = pl.BlockSpec(memory_space=pltpu.VMEM)
+    hbm = pl.BlockSpec(memory_space=pl.ANY)
+    sends = members - 1 + members // 2
     return pl.pallas_call(
-        mlp_kernel,
-        grid=(chunks,),
-        in_specs=[
-            pl.BlockSpec((n, d), whole),
-            pl.BlockSpec((n, d), whole),
-            pl.BlockSpec((n, rk), whole),
-            pl.BlockSpec((n, rk), whole),
-            pl.BlockSpec((members, 1, rows, fc), lambda j: (0, j, 0, 0)),
-            pl.BlockSpec((members, 1, sub, d), lambda j: (0, j, 0, 0)),
-            pl.BlockSpec((1, 1, fc), lambda j: (j, 0, 0)),
-            pl.BlockSpec((1, rk, fc), lambda j: (j, 0, 0)),
-            pl.BlockSpec((1, rk, fc), lambda j: (j, 0, 0)),
-        ],
-        out_specs=[
-            pl.BlockSpec((n, d), whole),
-            pl.BlockSpec((n, d), whole),
-            pl.BlockSpec((n, rk), whole),
-            pl.BlockSpec((n, rk), whole),
-            pl.BlockSpec((1, rk, fc), lambda j: (j, 0, 0)),
-            pl.BlockSpec((1, rk, fc), lambda j: (j, 0, 0)),
-        ],
+        lambda *refs: mlp_kernel(members, *refs),
+        in_specs=[vm, vm, vm, vm, hbm, hbm, vm, vm, vm],
+        out_specs=[vm] * 6 + [hbm] * 2,
         out_shape=[
             jax.ShapeDtypeStruct((n, d), f32),
             jax.ShapeDtypeStruct((n, d), f32),
             jax.ShapeDtypeStruct((n, rk), f32),
             jax.ShapeDtypeStruct((n, rk), f32),
-            jax.ShapeDtypeStruct((chunks, rk, fc), f32),
-            jax.ShapeDtypeStruct((chunks, rk, fc), f32),
-        ],
+            jax.ShapeDtypeStruct((members, chunks, rk, sub), bf16),
+            jax.ShapeDtypeStruct((members, chunks, rk, sub), bf16),
+            jax.ShapeDtypeStruct((chunks, members, rows, fc), bf16),
+            jax.ShapeDtypeStruct((chunks, members, sub, d), bf16),
+        ],
+        scratch_shapes=[
+            pltpu.VMEM((2, members, rows, fc), bf16),
+            pltpu.VMEM((2, members, sub, d), bf16),
+            pltpu.SemaphoreType.DMA((2, SLOTS, sends)),
+            pltpu.SemaphoreType.DMA((2, SLOTS, members)),
+            pltpu.SemaphoreType.DMA((2, 2, members)),
+        ],
+        compiler_params=pltpu.CompilerParams(
+            vmem_limit_bytes=VMEM_LIMIT, collective_id=1, has_side_effects=True),
+    )(m, dy, low3, e4, we, wr, be, bup, adn)
+
+
+def grads_kernel(scales, *refs):
+    out = refs[-1]
+    at = 0
+    for i, sc in enumerate(scales):
+        left, right = refs[2 * i][...], refs[2 * i + 1][...]
+        owners = out.shape[0]
+        w = right.shape[1] // owners
+        g = dot_tn(left, right) * sc
+        for to in range(owners):
+            out[to, :, at : at + w] = g[:, to * w : (to + 1) * w].astype(bf16)
+        at += w
+
+
+def grads(owners, pairs):
+    rk = pairs[0][0].shape[1]
+    width = sum(p[1].shape[1] for p in pairs) // owners
+    vm = pl.BlockSpec(memory_space=pltpu.VMEM)
+    return pl.pallas_call(
+        lambda *refs: grads_kernel([p[2] for p in pairs], *refs),
+        in_specs=[vm] * (2 * len(pairs)),
+        out_specs=vm,
+        out_shape=jax.ShapeDtypeStruct((owners, rk, width), bf16),
         compiler_params=pltpu.CompilerParams(vmem_limit_bytes=VMEM_LIMIT),
-    )(m, dy, low3, e4, we, wr, be, bup, adn)
+    )(*[x for p in pairs for x in p[:2]])
+
+
+def exchange(v, axis, bit):
+    return lax.ppermute(v, axis, [(i, i ^ bit) for i in range(lax.axis_size(axis))])
+
+
+def reduce_share(parts, turn):
+    me = lax.axis_index("shard")
+    count = parts.shape[0].bit_length() - 1
+    left = list(range(count))[::-1]
+    cur = parts.reshape((2,) * count + parts.shape[1:])
+    order = [0] + (list(range(1, count)) if turn == 0 else list(range(1, count))[::-1])
+    for i, bit in enumerate(order):
+        pos = left.index(bit)
+        mine = (me >> bit) & 1
+        send = lax.dynamic_index_in_dim(cur, 1 - mine, pos, keepdims=False)
+        keep = lax.dynamic_index_in_dim(cur, mine, pos, keepdims=False)
+        cur = keep.astype(f32) + exchange(send, "shard", 1 << bit).astype(f32)
+        left.remove(bit)
+        if i + 1 < count:
+            cur = cur.astype(bf16)
+    bit = 1
+    while bit < lax.axis_size("rep"):
+        low = cur.astype(bf16)
+        cur = low.astype(f32) + exchange(low, "rep", bit).astype(f32)
+        bit *= 2
+    return cur
 
 
 def norm_parts(v):
@@ -262,8 +469,8 @@
     attn_w = lax.all_gather(jnp.concatenate([wq, wkv, wmix], axis=1), "shard", axis=0, tiled=True)
     wq_f, wkv_f, wmix_f = attn_w[:, :d], attn_w[:, d : d + 2 * hd], attn_w[:, d + 2 * hd :]
     we_c = wexp.reshape(wexp.shape[0], members, chunks, sub).transpose(2, 0, 1, 3)
-    we_f = lax.all_gather(we_c.reshape(chunks, wexp.shape[0], fc), "shard", axis=0, tiled=False)
-    wr_f = lax.all_gather(wred.reshape(chunks, sub, d), "shard", axis=0, tiled=False)
+    we_c = we_c.reshape(chunks, wexp.shape[0], fc)
+    wr_c = wred.reshape(chunks, sub, d)
 
     group = lax.dynamic_index_in_dim(
         token_perm.reshape(members, replicas, length), rep, 1, keepdims=False)
@@ -319,40 +526,27 @@
     m = (nr * mlp_gain + mlp_bias).astype(bf16)
     low3 = (dot_nt(m, exp_dn) * masks[3]).astype(bf16)
     e4 = (scale_lora * dot_nt(out_grad, red_up) * masks[4]).astype(bf16)
-    y, dm, low4, e3, g_exp_up, g_red_dn = mlp(
-        m, out_grad, low3, e4, we_f, wr_f, be, by_chunk(exp_up), by_chunk(red_dn))
+    y, dm, low4, e3, g_exp_up, g_red_dn, _, _ = mlp(
+        members, m, out_grad, low3, e4, we_c, wr_c, be, by_chunk(exp_up), by_chunk(red_dn))
+    r_exp_up = reduce_share(g_exp_up, 0)
+    r_red_dn = reduce_share(g_red_dn, 1)
     low4 = (low4 * masks[4]).astype(bf16)
     layer_out = (resid + y + red_bias + scale_lora * dot_nn(low4, red_up)).astype(bf16)
-    g_red_up = scale_lora * dot_tn(low4, out_grad)
     e3 = (scale_lora * e3 * masks[3]).astype(bf16)
     dm = dm + dot_nn(e3, exp_dn)
-    g_exp_dn = dot_tn(e3, m)
     dres = out_grad.astype(f32) + norm_back(nr, inv_r, mlp_gain, dm)
 
-    def to_share(g):
-        return g.reshape(rk, members, -1).transpose(1, 0, 2)
-
-    def chunk_share(g):
-        return g.reshape(chunks, rk, members, sub).transpose(2, 1, 0, 3).reshape(members, rk, chunks * sub)
-
-    def reduce(parts):
-        sizes = [p.shape[2] for p in parts]
-        got = lax.psum_scatter(jnp.concatenate(parts, axis=2), "shard", scatter_dimension=0, tiled=True)
-        got = lax.psum(got[0], "rep")
-        outs, at = [], 0
-        for size in sizes:
-            outs.append(got[:, at : at + size].reshape(experts, rank, size))
-            at += size
-        return outs
-
-    r_exp_dn, r_exp_up, r_red_dn, r_red_up = reduce(
-        [to_share(g_exp_dn), chunk_share(g_exp_up), chunk_share(g_red_dn), to_share(g_red_up)])
+    def stack(g):
+        return g.reshape(experts, rank, g.shape[1])
+
+    def stack_chunks(g):
+        return stack(g.transpose(1, 0, 2).reshape(rk, chunks * sub))
 
     dresl = dres.astype(bf16)
     e2 = (scale_lora * dot_nt(dresl, mix_up) * masks[2]).astype(bf16)
     do = (dot_nt(dresl, wmix_f) + dot_nn(e2, mix_dn)).astype(bf16)
-    g_mix_dn = dot_tn(e2, o)
-    g_mix_up = scale_lora * dot_tn(low2, dresl)
+    r_down = reduce_share(grads(members, [(e3, m, 1.0), (e2, o, 1.0)]), 0)
+    r_up = reduce_share(grads(members, [(low4, out_grad, scale_lora), (low2, dresl, scale_lora)]), 1)
     dopad = dot_nn(put, do).astype(bf16).reshape(members, cap, d)
     dqpad, dslots = attn_bwd(heads, key_slot, span, qpad, dopad, kd)
     got = lax.all_to_all(dslots, "shard", split_axis=0, concat_axis=0, tiled=True)
@@ -363,14 +557,12 @@
     e1 = (scale_lora * dot_nt(dkv, kv_up) * masks[1]).astype(bf16)
     da = (dot_nt(dq, wq_f) + dot_nn(e0, q_dn)) + (dot_nt(dkv, wkv_f) + dot_nn(e1, kv_dn))
     tokens_grad = (dres + norm_back(nx, inv_x, attn_gain, da)).astype(bf16)
-    g_down = dot_tn(jnp.concatenate([e0, e1], axis=1), a)
-    g_q_up = scale_lora * dot_tn(low0, dq)
-    g_kv_up = scale_lora * dot_tn(low1, dkv)
-    r_q_dn, r_q_up, r_kv_dn, r_kv_up, r_mix_dn, r_mix_up = reduce(
-        [to_share(g_down[:rk]), to_share(g_q_up), to_share(g_down[rk:]), to_share(g_kv_up),
-         to_share(g_mix_dn), to_share(g_mix_up)])
-    return (layer_out, tokens_grad, r_q_dn, r_q_up, r_kv_dn, r_kv_up, r_mix_dn, r_mix_up,
-            r_exp_dn, r_exp_up, r_red_dn, r_red_up)
+    r_qkv_down = reduce_share(grads(members, [(e0, a, 1.0), (e1, a, 1.0)]), 0)
+    r_qkv_up = reduce_share(grads(members, [(low0, dq, scale_lora), (low1, dkv, scale_lora)]), 1)
+    w = d // members
+    return (layer_out, tokens_grad, stack(r_qkv_down[:, :w]), stack(r_qkv_up[:, :w]), stack(r_qkv_down[:, w:]),
+            stack(r_qkv_up[:, w:]), stack(r_down[:, w:]), stack(r_up[:, w:]), stack(r_down[:, :w]),
+            stack_chunks(r_exp_up), stack_chunks(r_red_dn), stack(r_up[:, :w]))
 
 
 def solution(mesh):

time: 941 us -> 727 us (0.77)
  waiting for transfers between devices: 490 us -> 124 us
  Pallas kernels: 147 us -> 316 us
  local copies, waits for them, and re-layouts: 100 us -> 57.9 us
  starting transfers between devices: 6.11 us -> 40.1 us
    all_gather x2 -> x0, waiting for transfers between devices: 264 us -> none  [the longest x1 163 us: local(): lax.all_gather(we_c.reshape(chunks, wexp.shape[0], fc), 'shard', axis=0,...]
    pallas_call x1 -> x5, Pallas kernels: 91.8 us -> 261 us  [the longest x1 246 us: mlp(): pl.pallas_call(lambda *refs: mlp_kernel(members, *refs), in_specs=[vm, vm...]
    reduce_scatter x2 -> x0, waiting for transfers between devices: 84 us -> none  [reduce(): lax.psum_scatter(jnp.concatenate(parts, axis=2), 'shard', scatter_dimensi...]
    psum x1 -> x0, waiting for transfers between devices: 76.3 us -> none  [reduce(): got = lax.psum(got[0], 'rep')]
    ppermute x0 -> x30, waiting for transfers between devices: none -> 75.3 us  [exchange(): lax.ppermute(v, axis, [(i, i ^ bit) for i in range(lax.axis_size(axis))])]
    ppermute x0 -> x30, starting transfers between devices: none -> 35.4 us  [exchange(): lax.ppermute(v, axis, [(i, i ^ bit) for i in range(lax.axis_size(axis))])]
    unnamed x156 -> x161, local copies, waits for them, and re-layouts: 36.5 us -> 15.4 us
    reshape x7 -> x1, local copies, waits for them, and re-layouts: 24 us -> 7.32 us  [local(): we_c = we_c.reshape(chunks, wexp.shape[0], fc)]
  transfers between devices with their start and end apart: 8 -> 33, of which waited for: 6 -> 20; matrix products, arithmetic and copies ran while one was open for 18% -> 20% of each run, Pallas kernels for 2% -> 6%
where the time goes in v2:
time: 727 us
  Pallas kernels  316 us (43%)
  waiting for transfers between devices  124 us (17%)
  matrix products  107 us (15%)
  local copies, waits for them, and re-layouts  57.9 us (8%)
  starting transfers between devices  40.1 us (6%)
  blocking collectives  33.4 us (5%)
  other arithmetic  32.1 us (4%)
  between operations  17 us (2%)
    pallas_call x1, Pallas kernels, mlp(): pl.pallas_call(lambda *refs: mlp_kernel(members, *refs), in_specs=[vm, vm...  246 us
    ppermute x30, waiting for transfers between devices, exchange(): lax.ppermute(v, axis, [(i, i ^ bit) for i in range(lax.axis_size(axis))])  75.3 us
    dot_general x11, matrix products, dot_nn(): lax.dot_general(a, b, (((1,), (0,)), ((), ())), preferred_element_type=f32)  63.8 us
    all_gather x1, waiting for transfers between devices, local(): lax.all_gather(jnp.concatenate([wq, wkv, wmix], axis=1), 'shard', axis=0,...  48.2 us
    ppermute x30, starting transfers between devices, exchange(): lax.ppermute(v, axis, [(i, i ^ bit) for i in range(lax.axis_size(axis))])  35.4 us
    unnamed x2, blocking collectives  33.4 us
    pallas_call x1, Pallas kernels, attn_bwd(): pl.pallas_call(lambda *refs: attn_bwd_kernel(heads, *refs), grid=(m,), in...  33.2 us
    dot_general x10, matrix products, dot_nt(): lax.dot_general(a, b, (((1,), (1,)), ((), ())), preferred_element_type=f32)  32.1 us
  transfers between devices with their start and end apart: 33, of which 20 were waited for; matrix products, arithmetic and copies ran while one was open for 20% of the time, Pallas kernels for 6%

profile of v2, /device:TPU:0, one launch (start us, length us, event | category | flops | bytes accessed | tf_op | source)
XLA Modules:
  0.0 727.1 jit_solution(1914152615914782209)
XLA Ops:
  7.4 3.3 pad_maximum_fusion
  12.6 9.5 %all-reduce.1 = s32[192]{0:T(256)S(1)} all-reduce(s32[192]{0:T(256)S(1)} %add_dynamic-update-slice_fusion), channel_id=2, replica_groups=mesh['shard'=8,'rep'=4] {'shard'}, use_global_device_ids=true, to_apply=%add.1 | all-reduce | flops 192 | bytes 1536
  22.6 2.2 convert_reduce_fusion
  30.0 24.0 %all-reduce.2 = bf16[22656]{0:T(1024)(128)(2,1)S(1)} all-reduce(bf16[22656]{0:T(1024)(128)(2,1)S(1)} %dynamic-update-slice.1), channel_id=3, replica_groups=mesh['shard'=8,'rep'=4] {'shard'}, use_global_device_ids=true, to_apply=%add.2 | all-reduce | flops 22656 | bytes 90624
  60.4 48.2 %all-gather.5.cloned.1.call-done = bf16[2048,4352]{1,0:T(8,128)(2,1)} async-done(((bf16[256,4352]{1,0:T(8,128)(2,1)}), bf16[2048,4352]{1,0:T(8,128)(2,1)}) %all-gather.5.cloned.1.call-update) | async-done | bytes 17825808 | tf_op jit(solution)/shard_map/all_gather | solution.py:469
  108.6 4.0 fusion.29
  115.0 3.4 copy.83
  118.4 2.7 copy.94
  121.1 7.3 %reshape.368.refs_4_ = bf16[8,256,1024]{2,1,0:T(8,128)(2,1)} reshape(bf16[8,256,8,128]{3,2,1,0:T(8,128)(2,1)} %bitcast.254) | data formatting | bytes 8388608 | tf_op jit(solution)/shard_map/reshape | solution.py:472
  128.5 2.2 copy.84
  132.3 4.3 reshape.372.refs_7_
  136.6 2.2 copy.85
  140.5 4.5 reshape.373.refs_8_
  145.6 3.0 fusion.42.refs_3_
  148.6 10.6 %fusion.6 = f32[512,2048]{1,0:T(8,128)} fusion(bf16[512,2048]{1,0:T(8,128)(2,1)} %copy-done.4, bf16[2048,4352]{1,0:T(8,128)(2,1)} %all-gather.5.cloned.1.call-done), kind=kOutput, calls=%fused_computation.7 | convolution fusion | flops 4294967296 | bytes 14680064 | tf_op jit(solution)/shard_map/dot_general | solution.py:18
  159.2 6.4 convolution_convert_fusion.1
  165.6 21.9 %shard_map.364 = (bf16[8,96,2048]{2,1,0:T(8,128)(2,1)}, bf16[8,512,256]{2,1,0:T(8,128)(2,1)}) custom-call(s32[8,1,512]{2,1,0:T(1,128)} %reshape_add_fusion.refs_0_, s32[8,96,2]{2,1,0:T(8,128)} %copy.65.refs_1_, bf16[8,96,2048]{2,1,0:T(8,128)(2,1)} %bitcast.256, bf16[8,8,96,256]{3,2,1,0:T(8,128)(2,1)} %all-gather.7.cloned.1.call-done.refs_3_), custom_call_target="tpu_custom_call" | custom-call | tf_op jit(solution)/shard_map/pallas_call | solution.py:94
  187.5 3.8 convolution_convert_fusion.3.refs_3_
  192.1 19.1 %fusion.2 = f32[512,2048]{1,0:T(8,128)S(1)} fusion(bf16[512,2048]{1,0:T(8,128)(2,1)S(1)} %convolution_convert_fusion.3.refs_3_, bf16[2048,4352]{1,0:T(8,128)(2,1)} %all-gather.5.cloned.1.call-done), kind=kOutput, calls=%fused_computation.3 | convolution fusion | flops 4294967296 | bytes 14680064 | tf_op jit(solution)/shard_map/dot_general | solution.py:18
  217.2 246.1 %shard_map.365 = (f32[512,2048]{1,0:T(8,128)}, f32[512,2048]{1,0:T(8,128)}, f32[512,128]{1,0:T(8,128)}, f32[512,128]{1,0:T(8,128)}, bf16[8,8,128,128]{3,2,1,0:T(...) custom-call(bf16[512,2048]{1,0:T(8,128)(2,1)} %copy-done.5, ...), custom_call_target="tpu_custom_call" | custom-call | tf_op jit(solution)/shard_map/pallas_call | solution.py:341
  463.3 2.5 dynamic-slice_bitcast_fusion
  465.8 2.2 collective-permute-start.25
  468.0 2.4 dynamic-slice_bitcast_fusion.1
  472.3 3.7 fusion.86
  476.0 3.5 fusion.87
  482.3 4.0 shard_map.370
  486.3 1.9 dynamic-slice_bitcast_fusion.4
  488.6 4.0 shard_map.369
  492.7 1.9 dynamic-slice_bitcast_fusion.5
  494.5 10.6 %fusion = f32[512,2048]{1,0:T(8,128)} fusion(bf16[512,2048]{1,0:T(8,128)(2,1)} %copy-done.9, bf16[2048,4352]{1,0:T(8,128)(2,1)} %all-gather.5.cloned.1.call-done), kind=kOutput, calls=%fused_computation.1 | convolution fusion | flops 4294967296 | bytes 14680064 | tf_op jit(solution)/shard_map/dot_general | solution.py:22
  505.1 6.2 convolution_convert_fusion
  511.3 33.2 %shard_map.366 = (bf16[8,96,2048]{2,1,0:T(8,128)(2,1)}, bf16[8,8,96,256]{3,2,1,0:T(8,128)(2,1)}) custom-call(s32[8,1,512]{2,1,0:T(1,128)} %reshape_add_fusion.refs_0_, s32[8,96,2]{2,1,0:T(8,128)} %copy.65.refs_1_, bf16[8,96,2048]{2,1,0:T(8,128)(2,1)} %bitcast.257, bf16[8,96,2048]{2,1,0:T(8,128)(2,1)} %bitcast.270, bf16[8,512,256]{2,1,0:T(8,128)(2,1)} %get-tuple-element.27.refs_4_), custom_call_target="tpu_custom_call" | custom-call | tf_op jit(solution)/shard_map/pallas_call | solution.py:118
  544.5 5.1 convolution_convert_fusion.2.refs_1_
  549.6 4.6 all-to-all-start
  554.2 5.7 add_convert_fusion.1
  559.9 9.8 %fusion.4 = f32[512,2048]{1,0:T(8,128)} fusion(bf16[512,2048]{1,0:T(8,128)(2,1)S(1)} %copy-done.17, bf16[2048,4352]{1,0:T(8,128)(2,1)} %all-gather.5.cloned.1.call-done), kind=kOutput, calls=%fused_computation.5 | convolution fusion | flops 4294967296 | bytes 14680064 | tf_op jit(solution)/shard_map/dot_general | solution.py:22
  570.5 2.8 fusion.93
  574.6 2.0 collective-permute-start.16
  579.4 17.3 %collective-permute-done.16 = bf16[2,128,512]{2,1,0:T(8,128)(2,1)S(1)} collective-permute-done((bf16[2,128,512]{2,1,0:T(8,128)(2,1)S(1)}, bf16[2,128,512]{2,1,0:T(8,128)(2,1)S(1)}, u32[]{:S(2)}, u32[]{:S(2)}) %collective-permute-start.16) | collective-permute-done | bytes 262176 | tf_op jit(solution)/shard_map/ppermute | solution.py:394
  598.8 3.2 collective-permute-done.17
  605.2 2.9 collective-permute-done.18
  608.1 2.8 collective-permute-start.19
  611.0 2.8 collective-permute-start.14
  619.3 6.3 collective-permute-done.26
  625.8 2.0 collective-permute-start.27
  627.8 2.5 collective-permute-done.21
  634.7 2.2 collective-permute-done.22
  639.0 5.3 collective-permute-done.28
  644.4 3.1 collective-permute-done.23
  648.5 12.0 %collective-permute-done.29 = bf16[8,128,128]{2,1,0:T(8,128)(2,1)S(1)} collective-permute-done((bf16[8,128,128]{2,1,0:T(8,128)(2,1)S(1)}, bf16[8,128,128]{2,1,0:T(8,128)(2,1)S(1)}, u32[]{:S(2)}, u32[]{:S(2)}) %collective-permute-start.29) | collective-permute-done | bytes 262176 | tf_op jit(solution)/shard_map/ppermute | solution.py:394
  665.6 2.5 reduce_sum.183
  669.5 3.2 shard_map.368
  672.7 1.9 fusion.39.refs_2_
  675.7 4.0 shard_map.367
  681.5 2.0 fusion.53
  683.6 4.0 fusion.85
  687.6 2.7 fusion.19
  690.7 1.8 collective-permute-start.1
  692.5 5.1 collective-permute-done.6
  697.7 1.8 collective-permute-start.7
  699.6 2.1 collective-permute-start.2
  702.5 2.2 collective-permute-done.2
  704.8 3.2 collective-permute-done.8
  712.1 5.6 collective-permute-done.9
  (320 shorter events, 71.3 us)
Async XLA Ops:
  7.2 184.1 %copy-start = (bf16[8,16,2048]{2,1,0:T(8,128)(2,1)S(1)}, bf16[8,16,2048]{2,1,0:T(8,128)(2,1)}, u32[]{:S(2)}) copy-start(bf16[8,16,2048]{2,1,0:T(8,128)(2,1)} %param.52) | copy-start | bytes 1572868
  7.2 20.5 %copy-start.57 = (bf16[256]{0:T(256)(128)(2,1)S(1)}, bf16[256]{0:T(256)(128)(2,1)}, u32[]{:S(2)}) copy-start(bf16[256]{0:T(256)(128)(2,1)} %param.34) | copy-start | bytes 1540
  7.3 20.7 %copy-start.58 = (bf16[256]{0:T(256)(128)(2,1)S(1)}, bf16[256]{0:T(256)(128)(2,1)}, u32[]{:S(2)}) copy-start(bf16[256]{0:T(256)(128)(2,1)} %param.35) | copy-start | bytes 1540
  7.3 20.9 %copy-start.59 = (bf16[256]{0:T(256)(128)(2,1)S(1)}, bf16[256]{0:T(256)(128)(2,1)}, u32[]{:S(2)}) copy-start(bf16[256]{0:T(256)(128)(2,1)} %param.37) | copy-start | bytes 1540
  7.3 21.1 %copy-start.60 = (bf16[256]{0:T(256)(128)(2,1)S(1)}, bf16[256]{0:T(256)(128)(2,1)}, u32[]{:S(2)}) copy-start(bf16[256]{0:T(256)(128)(2,1)} %param.41) | copy-start | bytes 1540
  7.3 21.3 %copy-start.61 = (bf16[256]{0:T(256)(128)(2,1)S(1)}, bf16[256]{0:T(256)(128)(2,1)}, u32[]{:S(2)}) copy-start(bf16[256]{0:T(256)(128)(2,1)} %param.42) | copy-start | bytes 1540
  7.3 21.6 %copy-start.62 = (bf16[256]{0:T(256)(128)(2,1)S(1)}, bf16[256]{0:T(256)(128)(2,1)}, u32[]{:S(2)}) copy-start(bf16[256]{0:T(256)(128)(2,1)} %param.43) | copy-start | bytes 1540
  7.3 21.8 %copy-start.63 = (bf16[256]{0:T(256)(128)(2,1)S(1)}, bf16[256]{0:T(256)(128)(2,1)}, u32[]{:S(2)}) copy-start(bf16[256]{0:T(256)(128)(2,1)} %param.47) | copy-start | bytes 1540
  7.3 22.0 %copy-start.56 = (bf16[1024]{0:T(1024)(128)(2,1)S(1)}, bf16[1024]{0:T(1024)(128)(2,1)}, u32[]{:S(2)}) copy-start(bf16[1024]{0:T(1024)(128)(2,1)} %param.45) | copy-start | bytes 6148
  7.3 22.2 %copy-start.64 = (bf16[16]{0:T(256)(128)(2,1)S(1)}, bf16[16]{0:T(256)(128)(2,1)}, u32[]{:S(2)}) copy-start(bf16[16]{0:T(256)(128)(2,1)} %param.39) | copy-start | bytes 100
  7.3 47.5 %copy-start.3 = (bf16[512,2048]{1,0:T(8,128)(2,1)S(1)}, bf16[512,2048]{1,0:T(8,128)(2,1)}, u32[]{:S(2)}) copy-start(bf16[512,2048]{1,0:T(8,128)(2,1)} %param.29) | copy-start | bytes 6291460
  7.3 101.2 %all-gather.5.cloned.1.call-start = ((), (), s32[]{:S(2)}) async-start(), calls=%async_computation.1 | async-start | bytes 20054016 | tf_op jit(solution)/shard_map/all_gather | solution.py:469
  10.8 154.9 %all-gather.7.cloned.1.call-start = ((), (), s32[]{:S(2)}) async-start(), calls=%async_computation.2 | async-start | bytes 3538944 | tf_op jit(solution)/shard_map/all_gather | solution.py:518
  26.7 31.1 %copy-start.50 = (s32[768]{0:T(1024)}, s32[768]{0:T(1024)S(1)}, u32[]{:S(2)}) copy-start(s32[768]{0:T(1024)S(1)} %add.323) | copy-start | bytes 9220
  57.8 50.8 %copy-start.51 = (s32[768]{0:T(1024)S(1)}, s32[768]{0:T(1024)}, u32[]{:S(2)}) copy-start(s32[768]{0:T(1024)} %copy-done.50) | copy-start | bytes 9220
  59.9 52.8 %copy-start.39 = (s32[8,96]{1,0:T(8,128)S(1)}, s32[8,96]{1,0:T(8,128)}, u32[]{:S(2)}) copy-start(s32[8,96]{1,0:T(8,128)} %get-tuple-element.39) | copy-start | bytes 9220
  60.1 58.3 %copy-start.20 = (bf16[512,128]{1,0:T(8,128)(2,1)}, bf16[512,128]{1,0:T(8,128)(2,1)S(1)}, u32[]{:S(2)}) copy-start(bf16[512,128]{1,0:T(8,128)(2,1)S(1)} %get-tuple-element.47.refs_2_) | copy-start | bytes 393220
  60.1 99.1 %copy-start.31 = (bf16[512,128]{1,0:T(8,128)(2,1)}, bf16[512,128]{1,0:T(8,128)(2,1)S(1)}, u32[]{:S(2)}) copy-start(bf16[512,128]{1,0:T(8,128)(2,1)S(1)} %get-tuple-element.48.refs_0_) | copy-start | bytes 393220
  148.6 10.6 %copy-start.52 = (s32[768]{0:T(1024)S(1)}, s32[768]{0:T(1024)}, u32[]{:S(2)}) copy-start(s32[768]{0:T(1024)} %copy-done.50) | copy-start | bytes 9220
  191.3 19.8 %copy-start.16 = (bf16[512,2048]{1,0:T(8,128)(2,1)}, bf16[512,2048]{1,0:T(8,128)(2,1)S(1)}, u32[]{:S(2)}) copy-start(bf16[512,2048]{1,0:T(8,128)(2,1)S(1)} %convolution_convert_fusion.3.refs_3_) | copy-start | bytes 6291460
  192.1 19.1 %copy-start.22 = (bf16[512,128]{1,0:T(8,128)(2,1)}, bf16[512,128]{1,0:T(8,128)(2,1)S(1)}, u32[]{:S(2)}) copy-start(bf16[512,128]{1,0:T(8,128)(2,1)S(1)} %fusion.37.refs_2_) | copy-start | bytes 393220
  192.1 19.1 %copy-start.32 = (bf16[8,16,2048]{2,1,0:T(8,128)(2,1)S(1)}, bf16[8,16,2048]{2,1,0:T(8,128)(2,1)}, u32[]{:S(2)}) copy-start(bf16[8,16,2048]{2,1,0:T(8,128)(2,1)} %param.53) | copy-start | bytes 1572868
  463.3 8.2 %copy-start.34 = (f32[512,128]{1,0:T(8,128)S(1)}, f32[512,128]{1,0:T(8,128)}, u32[]{:S(2)}) copy-start(f32[512,128]{1,0:T(8,128)} %get-tuple-element.24) | copy-start | bytes 786436
  463.3 9.0 %copy-start.2 = (f32[512,2048]{1,0:T(8,128)S(1)}, f32[512,2048]{1,0:T(8,128)}, u32[]{:S(2)}) copy-start(f32[512,2048]{1,0:T(8,128)} %copy-done.1) | copy-start | bytes 12582916
  465.8 147.9 %collective-permute-start.25 = (bf16[2,2,8,128,128]{4,3,2,1,0:T(8,128)(2,1)}, bf16[2,2,8,128,128]{4,3,2,1,0:T(8,128)(2,1)}, u32[]{:S(2)}, u32[]{:S(2)}) collective-permute-start(bf16[2,2,8,128,128]{4,3,2,1,0:T(8,128)(2,1)} %dynamic-slice_bitcast_fusion), channel_id=1, source_target_pairs={{0,4},{4,0},{8,12},{12,8},{16,20},{20,16},{24,28},{28,24},{1,5},{5... | collective-permute-start | bytes 3145736 | tf_op jit(solution)/shard_map/ppermute | solution.py:394
  470.4 145.5 %collective-permute-start.20 = (bf16[2,2,8,128,128]{4,3,2,1,0:T(8,128)(2,1)}, bf16[2,2,8,128,128]{4,3,2,1,0:T(8,128)(2,1)}, u32[]{:S(2)}, u32[]{:S(2)}) collective-permute-start(bf16[2,2,8,128,128]{4,3,2,1,0:T(8,128)(2,1)} %dynamic-slice_bitcast_fusion.1), channel_id=1, source_target_pairs={{0,4},{4,0},{8,12},{12,8},{16,20},{20,16},{24,28},{28,24},{1,5},{5... | collective-permute-start | bytes 3145736 | tf_op jit(solution)/shard_map/ppermute | solution.py:394
  488.1 85.1 %collective-permute-start.15 = (bf16[2,2,128,512]{3,2,1,0:T(8,128)(2,1)}, bf16[2,2,128,512]{3,2,1,0:T(8,128)(2,1)}, u32[]{:S(2)}, u32[]{:S(2)}) collective-permute-start(bf16[2,2,128,512]{3,2,1,0:T(8,128)(2,1)} %dynamic-slice_bitcast_fusion.4), channel_id=1, source_target_pairs={{0,4},{4,0},{8,12},{12,8},{16,20},{20,16},{24,28},{28,24},{1,5},{5... | collective-permute-start | bytes 1572872 | tf_op jit(solution)/shard_map/ppermute | solution.py:394
  494.5 10.6 %copy-start.35 = (bf16[512,128]{1,0:T(8,128)(2,1)S(1)}, bf16[512,128]{1,0:T(8,128)(2,1)}, u32[]{:S(2)}) copy-start(bf16[512,128]{1,0:T(8,128)(2,1)} %fusion.41.refs_2_) | copy-start | bytes 393220
  494.5 82.1 %collective-permute-start.10 = (bf16[2,2,128,512]{3,2,1,0:T(8,128)(2,1)}, bf16[2,2,128,512]{3,2,1,0:T(8,128)(2,1)}, u32[]{:S(2)}, u32[]{:S(2)}) collective-permute-start(bf16[2,2,128,512]{3,2,1,0:T(8,128)(2,1)} %dynamic-slice_bitcast_fusion.5), channel_id=1, source_target_pairs={{0,4},{4,0},{8,12},{12,8},{16,20},{20,16},{24,28},{28,24},{1,5},{5... | collective-permute-start | bytes 1572872 | tf_op jit(solution)/shard_map/ppermute | solution.py:394
  549.6 115.9 %all-to-all-start = ((bf16[8,8,96,256]{3,2,1,0:T(8,128)(2,1)}), bf16[8,8,96,256]{3,2,1,0:T(8,128)(2,1)}, u32[]{:S(2)}, u32[]{:S(2)}) async-start(bf16[8,8,96,256]{3,2,1,0:T(8,128)(2,1)} %get-tuple-element.29), calls=%async_computation | async-start | bytes 6291456 | tf_op jit(solution)/shard_map/all_to_all | solution.py:552
  559.9 9.8 %copy-start.43 = (s32[512,1]{0,1:T(1,128)S(1)}, s32[512,1]{0,1:T(1,128)}, u32[]{:S(2)}) copy-start(s32[512,1]{0,1:T(1,128)} %copy-done.42) | copy-start | bytes 6148
  559.9 9.8 %copy-start.48 = (s32[128]{0:T(128)S(1)}, s32[128]{0:T(128)}, u32[]{:S(2)}) copy-start(s32[128]{0:T(128)} %copy-done.46) | copy-start | bytes 1540
  559.9 9.8 %copy-start.66 = (bf16[8,16,2048]{2,1,0:T(8,128)(2,1)S(1)}, bf16[8,16,2048]{2,1,0:T(8,128)(2,1)}, u32[]{:S(2)}) copy-start(bf16[8,16,2048]{2,1,0:T(8,128)(2,1)} %param.49) | copy-start | bytes 1572868
  559.9 10.5 %copy-start.27 = (bf16[8,16,2048]{2,1,0:T(8,128)(2,1)S(1)}, bf16[8,16,2048]{2,1,0:T(8,128)(2,1)}, u32[]{:S(2)}) copy-start(bf16[8,16,2048]{2,1,0:T(8,128)(2,1)} %param.48) | copy-start | bytes 1572868
  573.3 40.5 %copy-start.15 = (bf16[8,8,128,128]{3,2,1,0:T(8,128)(2,1)S(1)}, bf16[8,8,128,128]{3,2,1,0:T(8,128)(2,1)}, u32[]{:S(2)}) copy-start(bf16[8,8,128,128]{3,2,1,0:T(8,128)(2,1)} %get-tuple-element.31) | copy-start | bytes 6291460
  574.6 22.0 %collective-permute-start.16 = (bf16[2,128,512]{2,1,0:T(8,128)(2,1)S(1)}, bf16[2,128,512]{2,1,0:T(8,128)(2,1)S(1)}, u32[]{:S(2)}, u32[]{:S(2)}) collective-permute-start(bf16[2,128,512]{2,1,0:T(8,128)(2,1)S(1)} %dynamic-slice_bitcast_fusion.10), channel_id=1, source_target_pairs={{0,16},{4,20},{8,24},{12,28},{16,0},{20,4},{24,8},{28,12},{1,17},{... | collective-permute-start | bytes 786440 | tf_op jit(solution)/shard_map/ppermute | solution.py:394
  577.8 38.1 %copy-start.14 = (bf16[8,8,128,128]{3,2,1,0:T(8,128)(2,1)S(1)}, bf16[8,8,128,128]{3,2,1,0:T(8,128)(2,1)}, u32[]{:S(2)}) copy-start(bf16[8,8,128,128]{3,2,1,0:T(8,128)(2,1)} %get-tuple-element.30) | copy-start | bytes 6291460
  577.8 20.5 %collective-permute-start.11 = (bf16[2,128,512]{2,1,0:T(8,128)(2,1)S(1)}, bf16[2,128,512]{2,1,0:T(8,128)(2,1)S(1)}, u32[]{:S(2)}, u32[]{:S(2)}) collective-permute-start(bf16[2,128,512]{2,1,0:T(8,128)(2,1)S(1)} %dynamic-slice_bitcast_fusion.11), channel_id=1, source_target_pairs={{0,8},{4,12},{8,0},{12,4},{16,24},{20,28},{24,16},{28,20},{1,9},{5... | collective-permute-start | bytes 786440 | tf_op jit(solution)/shard_map/ppermute | solution.py:394
  596.8 5.3 collective-permute-start.17
  598.4 5.3 collective-permute-start.12
  602.1 6.0 collective-permute-start.18
  603.7 7.2 collective-permute-start.13
  608.1 11.2 %collective-permute-start.19 = (bf16[128,512]{1,0:T(8,128)(2,1)S(1)}, bf16[128,512]{1,0:T(8,128)(2,1)S(1)}, u32[]{:S(2)}, u32[]{:S(2)}) collective-permute-start(bf16[128,512]{1,0:T(8,128)(2,1)S(1)} %add_convert_fusion.6), channel_id=1, source_target_pairs={{0,2},{1,3},{2,0},{3,1},{4,6},{5,7},{6,4},{7,5},{8,10},{9,11},{10,... | collective-permute-start | bytes 393224 | tf_op jit(solution)/shard_map/ppermute | solution.py:394
  611.0 21.2 %collective-permute-start.14 = (bf16[128,512]{1,0:T(8,128)(2,1)S(1)}, bf16[128,512]{1,0:T(8,128)(2,1)S(1)}, u32[]{:S(2)}, u32[]{:S(2)}) collective-permute-start(bf16[128,512]{1,0:T(8,128)(2,1)S(1)} %add_convert_fusion.7), channel_id=1, source_target_pairs={{0,2},{1,3},{2,0},{3,1},{4,6},{5,7},{6,4},{7,5},{8,10},{9,11},{10,... | collective-permute-start | bytes 393224 | tf_op jit(solution)/shard_map/ppermute | solution.py:394
  615.4 10.2 %collective-permute-start.26 = (bf16[2,8,128,128]{3,2,1,0:T(8,128)(2,1)S(1)}, bf16[2,8,128,128]{3,2,1,0:T(8,128)(2,1)S(1)}, u32[]{:S(2)}, u32[]{:S(2)}) collective-permute-start(bf16[2,8,128,128]{3,2,1,0:T(8,128)(2,1)S(1)} %dynamic-slice_bitcast_fusion.2), channel_id=1, source_target_pairs={{0,16},{4,20},{8,24},{12,28},{16,0},{20,4},{24,8},{28,12},{1,17},{... | collective-permute-start | bytes 1572872 | tf_op jit(solution)/shard_map/ppermute | solution.py:394
  617.5 12.7 %collective-permute-start.21 = (bf16[2,8,128,128]{3,2,1,0:T(8,128)(2,1)S(1)}, bf16[2,8,128,128]{3,2,1,0:T(8,128)(2,1)S(1)}, u32[]{:S(2)}, u32[]{:S(2)}) collective-permute-start(bf16[2,8,128,128]{3,2,1,0:T(8,128)(2,1)S(1)} %dynamic-slice_bitcast_fusion.3), channel_id=1, source_target_pairs={{0,8},{4,12},{8,0},{12,4},{16,24},{20,28},{24,16},{28,20},{1,9},{5... | collective-permute-start | bytes 1572872 | tf_op jit(solution)/shard_map/ppermute | solution.py:394
  625.8 7.2 collective-permute-start.27
  630.4 6.4 collective-permute-start.22
  633.1 11.2 %collective-permute-start.28 = (bf16[8,128,128]{2,1,0:T(8,128)(2,1)S(1)}, bf16[8,128,128]{2,1,0:T(8,128)(2,1)S(1)}, u32[]{:S(2)}, u32[]{:S(2)}) collective-permute-start(bf16[8,128,128]{2,1,0:T(8,128)(2,1)S(1)} %fusion.65), channel_id=1, source_target_pairs={{0,1},{1,0},{2,3},{3,2},{4,5},{5,4},{6,7},{7,6},{8,9},{9,8},{10,11... | collective-permute-start | bytes 786440 | tf_op jit(solution)/shard_map/ppermute | solution.py:394
  637.0 10.6 %collective-permute-start.23 = (bf16[8,128,128]{2,1,0:T(8,128)(2,1)S(1)}, bf16[8,128,128]{2,1,0:T(8,128)(2,1)S(1)}, u32[]{:S(2)}, u32[]{:S(2)}) collective-permute-start(bf16[8,128,128]{2,1,0:T(8,128)(2,1)S(1)} %fusion.66), channel_id=1, source_target_pairs={{0,1},{1,0},{2,3},{3,2},{4,5},{5,4},{6,7},{7,6},{8,9},{9,8},{10,11... | collective-permute-start | bytes 786440 | tf_op jit(solution)/shard_map/ppermute | solution.py:394
  644.4 16.1 %collective-permute-start.29 = (bf16[8,128,128]{2,1,0:T(8,128)(2,1)S(1)}, bf16[8,128,128]{2,1,0:T(8,128)(2,1)S(1)}, u32[]{:S(2)}, u32[]{:S(2)}) collective-permute-start(bf16[8,128,128]{2,1,0:T(8,128)(2,1)S(1)} %add_convert_fusion.4), channel_id=1, source_target_pairs={{0,2},{1,3},{2,0},{3,1},{4,6},{5,7},{6,4},{7,5},{8,10},{9,11},{10,... | collective-permute-start | bytes 786440 | tf_op jit(solution)/shard_map/ppermute | solution.py:394
  647.6 15.7 %collective-permute-start.24 = (bf16[8,128,128]{2,1,0:T(8,128)(2,1)S(1)}, bf16[8,128,128]{2,1,0:T(8,128)(2,1)}, u32[]{:S(2)}, u32[]{:S(2)}) collective-permute-start(bf16[8,128,128]{2,1,0:T(8,128)(2,1)S(1)} %add_convert_fusion.5), channel_id=1, source_target_pairs={{0,2},{1,3},{2,0},{3,1},{4,6},{5,7},{6,4},{7,5},{8,10},{9,11},{10,... | collective-permute-start | bytes 786440 | tf_op jit(solution)/shard_map/ppermute | solution.py:394
  660.5 7.5 %copy-start.53 = (s32[768]{0:T(1024)S(1)}, s32[768]{0:T(1024)}, u32[]{:S(2)}) copy-start(s32[768]{0:T(1024)} %copy-done.50) | copy-start | bytes 9220
  672.7 8.9 %copy-start.21 = (bf16[512,256]{1,0:T(8,128)(2,1)S(1)}, bf16[512,256]{1,0:T(8,128)(2,1)}, u32[]{:S(2)}) copy-start(bf16[512,256]{1,0:T(8,128)(2,1)} %fusion.32.refs_3_) | copy-start | bytes 786436
  675.6 14.6 %collective-permute-start.5 = (bf16[2,2,128,288]{3,2,1,0:T(8,128)(2,1)S(1)}, bf16[2,2,128,288]{3,2,1,0:T(8,128)(2,1)S(1)}, u32[]{:S(2)}, u32[]{:S(2)}) collective-permute-start(bf16[2,2,128,288]{3,2,1,0:T(8,128)(2,1)S(1)} %dynamic-slice_bitcast_fusion.7), channel_id=1, source_target_pairs={{0,4},{4,0},{8,12},{12,8},{16,20},{20,16},{24,28},{28,24},{1,5},{5... | collective-permute-start | bytes 884744 | tf_op jit(solution)/shard_map/ppermute | solution.py:394
  681.0 9.5 %collective-permute-start = (bf16[2,2,128,512]{3,2,1,0:T(8,128)(2,1)S(1)}, bf16[2,2,128,512]{3,2,1,0:T(8,128)(2,1)S(1)}, u32[]{:S(2)}, u32[]{:S(2)}) collective-permute-start(bf16[2,2,128,512]{3,2,1,0:T(8,128)(2,1)S(1)} %dynamic-slice_bitcast_fusion.6), channel_id=1, source_target_pairs={{0,4},{4,0},{8,12},{12,8},{16,20},{20,16},{24,28},{28,24},{1,5},{5... | collective-permute-start | bytes 1572872 | tf_op jit(solution)/shard_map/ppermute | solution.py:394
  690.4 7.2 collective-permute-start.6
  690.7 8.8 %collective-permute-start.1 = (bf16[2,128,512]{2,1,0:T(8,128)(2,1)S(1)}, bf16[2,128,512]{2,1,0:T(8,128)(2,1)S(1)}, u32[]{:S(2)}, u32[]{:S(2)}) collective-permute-start(bf16[2,128,512]{2,1,0:T(8,128)(2,1)S(1)} %dynamic-slice_bitcast_fusion.12), channel_id=1, source_target_pairs={{0,8},{4,12},{8,0},{12,4},{16,24},{20,28},{24,16},{28,20},{1,9},{5... | collective-permute-start | bytes 786440 | tf_op jit(solution)/shard_map/ppermute | solution.py:394
  697.7 4.7 collective-permute-start.7
  699.6 5.0 collective-permute-start.2
  702.4 5.6 collective-permute-start.8
  704.7 5.9 collective-permute-start.3
  708.0 9.8 %collective-permute-start.9 = (bf16[128,288]{1,0:T(8,128)(2,1)S(1)}, bf16[128,288]{1,0:T(8,128)(2,1)S(1)}, u32[]{:S(2)}, u32[]{:S(2)}) collective-permute-start(bf16[128,288]{1,0:T(8,128)(2,1)S(1)} %add_convert_fusion.9), channel_id=1, source_target_pairs={{0,2},{1,3},{2,0},{3,1},{4,6},{5,7},{6,4},{7,5},{8,10},{9,11},{10,... | collective-permute-start | bytes 221192 | tf_op jit(solution)/shard_map/ppermute | solution.py:394
  710.7 8.6 %collective-permute-start.4 = (bf16[128,512]{1,0:T(8,128)(2,1)S(1)}, bf16[128,512]{1,0:T(8,128)(2,1)S(1)}, u32[]{:S(2)}, u32[]{:S(2)}) collective-permute-start(bf16[128,512]{1,0:T(8,128)(2,1)S(1)} %add_convert_fusion.8), channel_id=1, source_target_pairs={{0,2},{1,3},{2,0},{3,1},{4,6},{5,7},{6,4},{7,5},{8,10},{9,11},{10,... | collective-permute-start | bytes 393224 | tf_op jit(solution)/shard_map/ppermute | solution.py:394
  (37 other events, 157.7 us)
Sparse Core Ops, SparseCore 0:
  10.9 97.6 all-gather.4
  112.8 32.3 all-gather.6

commit v3 on v2

v3 whole, which is shorter than its diff:
```python
import jax
import jax.numpy as jnp
from jax import lax
from jax.experimental import pallas as pl
from jax.experimental.pallas import tpu as pltpu
from jax.sharding import PartitionSpec as P

scale_lora = 0.5
eps = 1e-05
f32 = jnp.float32
bf16 = jnp.bfloat16
neg_big = -1e30
gelu_c = 0.7978845608028654
VMEM_LIMIT = 60 * 1024 * 1024


def dot_nn(a, b):
    return lax.dot_general(a, b, (((1,), (0,)), ((), ())), preferred_element_type=f32)


def dot_nt(a, b):
    return lax.dot_general(a, b, (((1,), (1,)), ((), ())), preferred_element_type=f32)


def dot_tn(a, b):
    return lax.dot_general(a, b, (((0,), (0,)), ((), ())), preferred_element_type=f32)


def key_onehot(slot_row, slots):
    ids = lax.broadcasted_iota(jnp.int32, (slots, slot_row.shape[1]), 0)
    return jnp.where(ids == slot_row, 1.0, 0.0).astype(bf16)


def to_rows(x, heads):
    hd = x.shape[1] // heads
    return jnp.concatenate([x[:, h * hd : (h + 1) * hd] for h in range(heads)], axis=0)


def to_cols(x, heads):
    c = x.shape[0] // heads
    return jnp.concatenate([x[h * c : (h + 1) * c] for h in range(heads)], axis=1)


def softmax_rows(qr, kd, span, heads):
    rows, keys = qr.shape[0], kd.shape[0]
    c = rows // heads
    u = lax.broadcasted_iota(jnp.int32, (c, keys), 1).astype(f32)
    allowed = (u >= span[:, 0:1]) & (u <= span[:, 1:2])
    s = dot_nt(qr, kd) * (kd.shape[1] ** (-0.5))
    s = jnp.where(allowed[None], s.reshape(heads, c, keys), neg_big)
    top = jnp.max(s, axis=2, keepdims=True)
    e = jnp.exp(s - top)
    p = e / jnp.sum(e, axis=2, keepdims=True)
    return p.reshape(rows, keys)


def attn_bwd_kernel(heads, slot_ref, span_ref, q_ref, do_ref, kd_ref, dq_ref, ds_ref):
    m, _, c, w = ds_ref.shape
    hd = w // 2
    kvd = kd_ref[0]
    kd, vd = kvd[:, :hd], kvd[:, hd:]
    qr = to_rows(q_ref[0], heads)
    dor = to_rows(do_ref[0], heads)
    p = softmax_rows(qr, kd, span_ref[0], heads)
    dp = dot_nt(dor, vd)
    rd = jnp.sum(dp * p, axis=1, keepdims=True)
    ds = (p * (dp - rd)).astype(bf16)
    sc = hd ** (-0.5)
    dq = (dot_nn(ds, kd) * sc).astype(bf16)
    dq_ref[0] = to_cols(dq, heads)
    dk = dot_tn(ds, qr) * sc
    dv = dot_tn(p.astype(bf16), dor)
    dkv = jnp.concatenate([dk, dv], axis=1).astype(bf16)
    oh = key_onehot(slot_ref[0], m * c)
    ds_ref[...] = dot_nn(oh, dkv).astype(bf16).reshape(ds_ref.shape)


def attn_bwd(heads, slot, span, qpad, dopad, kd):
    m, c, d = qpad.shape
    length, w = kd.shape[1], kd.shape[2]
    return pl.pallas_call(
        lambda *refs: attn_bwd_kernel(heads, *refs),
        grid=(m,),
        in_specs=[
            pl.BlockSpec((1, 1, length), lambda k: (k, 0, 0)),
            pl.BlockSpec((1, c, 128), lambda k: (k, 0, 0)),
            pl.BlockSpec((1, c, d), lambda k: (k, 0, 0)),
            pl.BlockSpec((1, c, d), lambda k: (k, 0, 0)),
            pl.BlockSpec((1, length, w), lambda k: (k, 0, 0)),
        ],
        out_specs=[
            pl.BlockSpec((1, c, d), lambda k: (k, 0, 0)),
            pl.BlockSpec((m, 1, c, w), lambda k: (0, k, 0, 0)),
        ],
        out_shape=[
            jax.ShapeDtypeStruct((m, c, d), bf16),
            jax.ShapeDtypeStruct((m, m, c, w), bf16),
        ],
        compiler_params=pltpu.CompilerParams(vmem_limit_bytes=VMEM_LIMIT),
    )(slot, span, qpad, dopad, kd)


MESH = pl.DeviceIdType.MESH


class Gather:
    def __init__(self, members, own, full, slots, send_sem, recv_sem):
        self.members = members
        self.me, self.rep = lax.axis_index("shard"), lax.axis_index("rep")
        self.own, self.full = own, full
        self.base = [sum(slots[:i]) for i in range(len(slots))]
        self.send_sem, self.recv_sem = send_sem, recv_sem
        self.bits = [1 << i for i in range(1, members.bit_length() - 1)]
        self.planes = list(range(0, members, 2))
        self.sent = {}

    def place(self, kind, slot, offset):
        return self.full[kind].at[slot, self.me ^ offset]

    def copy(self, kind, slot, offset, there, to, to_slot):
        mine = self.sent.setdefault((kind, slot), {})
        at = mine.setdefault((offset, there, to_slot), len(mine))
        src = self.own[kind](slot) if offset == 0 else self.place(kind, slot, offset)
        pltpu.make_async_remote_copy(
            src, self.full[kind].at[to_slot, self.me ^ offset],
            self.send_sem.at[self.base[kind] + slot, at],
            self.recv_sem.at[self.base[kind] + to_slot, there],
            device_id=to, device_id_type=MESH).start()

    def wait(self, kind, slot, offset):
        piece = self.place(kind, slot, offset)
        pltpu.make_async_copy(piece, piece, self.recv_sem.at[self.base[kind] + slot, offset]).wait()

    def order(self, kind):
        return self.bits if kind % 2 == 0 else self.bits[::-1]

    def stage(self, kind, offset):
        return max(i for i, b in enumerate(self.order(kind)) if offset & b)

    def issue(self, slot, kinds, plane=True):
        for kind in kinds:
            if plane:
                for b in self.order(kind):
                    self.copy(kind, slot, 0, b, (self.me ^ b, self.rep), slot)
            self.copy(kind, slot, 0, 1, (self.me ^ 1, self.rep), slot)

    def arrive(self, slot, kinds, direct, swap_to=None):
        for kind in kinds:
            order = self.order(kind)
            some = [o for o in self.planes if o and (bin(o).count("1") == 1) == direct]
            some.sort(key=lambda o: self.stage(kind, o))
            for o in some:
                self.wait(kind, slot, o)
                for i in range(self.stage(kind, o) + 1, len(order)):
                    self.copy(kind, slot, o, o ^ order[i], (self.me ^ order[i], self.rep), slot)
                if swap_to is not None:
                    self.copy(kind, slot, o, o, (self.me, self.rep ^ 1), swap_to)
                self.copy(kind, slot, o, o ^ 1, (self.me ^ 1, self.rep), slot)

    def swapped(self, slot, kinds):
        for kind in kinds:
            for o in self.planes[1:]:
                self.wait(kind, slot, o)
                self.copy(kind, slot, o, o ^ 1, (self.me ^ 1, self.rep), slot)

    def ready(self, slot, kinds):
        for kind in kinds:
            for o in range(1, self.members, 2):
                self.wait(kind, slot, o)

    def finish(self):
        for (kind, slot), mine in self.sent.items():
            piece = self.place(kind, slot, 0)
            for at in mine.values():
                pltpu.make_async_copy(piece, piece, self.send_sem.at[self.base[kind] + slot, at]).wait()


U, V, C = (0, 1, 2), (3, 4, 5), (6, 7)
SLOTS = 8
WE, WR, AT, AB, KV = range(5)
BOTH, HALVES = (WE, WR), (AT, AB)
WQ, WMIX = 0, 1
SEND, NEAR, FAR, SWAP = range(4)
MLP_ORDER = (0, 3, 4, 1, 2, 6, 5, 7)
SERVE = {
    "p0": ((SEND, KV, 0),),
    "stage": ((SEND, WR, 0),),
    "norm_0": ((NEAR, KV, 0),),
    "idx_1": ((SEND, AT, 0),),
    "idx_5": ((NEAR, WR, 0),),
    "idx_6": ((FAR, KV, 0),),
    "wqneed": ((NEAR, AT, 0), (FAR, WR, 0), (SEND, AB, 0), (SWAP, WR, 3), (FAR, AT, 0), (SEND, WE, 0), (NEAR, AB, 0), (SEND, AB, 1), (NEAR, WE, 0), (FAR, AB, 0),),
    "q_1": ((SEND, WE, 1),),
    "att_0": ((NEAR, AB, 1),),
    "att_1": ((FAR, WE, 0),),
    "att_3": ((SEND, AT, 1),),
    "att_5": ((NEAR, WE, 1),),
    "att_6": ((SWAP, WE, 3),),
    "mixneed": ((FAR, AB, 1), (SEND, WR, 1), (NEAR, AT, 1), (FAR, WE, 1), (SEND, WE, 2), (NEAR, WR, 1), (SWAP, WE, 4), (FAR, AT, 1),),
    "mix_0": ((SEND, WR, 2),),
    "mix_1": ((FAR, WR, 1),),
    "norm2_0": ((NEAR, WE, 2), (SEND, WE, 6),),
    "mlp_0_0": ((NEAR, WR, 2),),
    "mlp_0_1": ((SWAP, WR, 4),),
    "mlp_1_0": ((FAR, WE, 2), (SEND, WR, 6),),
    "mlp_2_0": ((FAR, WR, 2), (NEAR, WE, 6), (SEND, WR, 7),),
    "mlp_3_0": ((NEAR, WR, 6),),
    "mlp_4_0": ((FAR, WE, 6), (SEND, WE, 7),),
    "mlp_4_1": ((FAR, WR, 6),),
    "mlp_5_0": ((NEAR, WR, 7), (SWAP, WE, 5),),
    "mlp_5_1": ((NEAR, WE, 7), (SWAP, WR, 5),),
    "mlp_6_0": ((FAR, WR, 7), (FAR, WE, 7),),
}


def chunk_of(slot, parity):
    slot = jnp.int32(slot)
    low = jnp.where(slot < 3, slot, slot + 2)
    high = jnp.where(slot < 3, slot + 5, slot - 3)
    return jnp.where(slot >= 6, slot - 3, jnp.where(parity == 0, low, high))


def norm_parts(v):
    center = v - jnp.mean(v, axis=-1, keepdims=True)
    inv = lax.rsqrt(jnp.mean(center * center, axis=-1, keepdims=True) + eps)
    return center * inv, inv


def norm_back(n, inv, gain, dn):
    w = gain * dn
    return (w - jnp.mean(w, axis=-1, keepdims=True)
            - n * jnp.mean(w * n, axis=-1, keepdims=True)) * inv


class Sizes:
    def __init__(self, members, replicas, length, d, ff, hd, rk, rank, seqs, projs):
        self.members, self.replicas, self.length, self.d, self.ff = members, replicas, length, d, ff
        self.hd, self.rk, self.rank, self.seqs, self.projs = hd, rk, rank, seqs, projs
        self.heads = d // hd
        self.cap = 3 * length // (2 * members)
        self.slots = members * self.cap
        self.w = 2 * hd
        self.rows = d // members
        self.sub = ff // members // SLOTS
        self.fc = self.sub * members
        self.aligned = self.sub % 128 == 0
        self.small_cols = -(-max(self.rows + self.sub, seqs * (projs + 1)) // 128) * 128


FWD_IN = ("x", "dy", "small", "group", "group_t", "q_dn", "q_up", "kv_dn", "kv_up", "mix_dn", "mix_up",
          "exp_dn", "exp_up", "red_dn", "red_up", "wq", "wkv", "wmix", "wexp", "wred")
FWD_OUT = ("dres", "put", "slot", "info", "chosen", "low0", "low1", "low2", "low4", "e3",
           "a", "q", "o", "m", "resid", "kd", "gup", "gdn", "layer", "kvs", "ge", "gr", "ga", "gb", "gk")
FWD_SCRATCH = ("y", "we_v", "wr_v", "a_v", "q_v", "kvp", "kvb", "kd_st", "gup_st", "gdn_st", "sm",
               "lowr", "er", "low3", "e4",
               "send_sem", "recv_sem", "sm_send", "sm_recv", "kv_send", "kv_recv", "stage_sem", "store_sem",
               "load_sem", "kvb_sem", "kd_sem", "g_sem", "out_sem")


def fwd_kernel(z, *refs):
    r = dict(zip(FWD_IN + FWD_OUT + FWD_SCRATCH, refs))
    members, rows, fc, sub, d, hd = z.members, z.rows, z.fc, z.sub, z.d, z.hd
    length, cap, w, heads, rk = z.length, z.cap, z.w, z.heads, z.rk
    me, rep = lax.axis_index("shard"), lax.axis_index("rep")
    parity = lax.rem(rep, 2)
    half = rows // 2
    att = (r["wq"], r["wmix"])
    g = Gather(
        members,
        [lambda s: r["ge"].at[s, me],
         lambda s: r["wred"].at[chunk_of(s, parity)],
         lambda s: att[s].at[0:half],
         lambda s: att[s].at[half:rows],
         lambda s: r["wkv"]],
        [r["ge"], r["gr"], r["ga"], r["gb"], r["gk"]],
        [SLOTS, SLOTS, 2, 2, 1], r["send_sem"], r["recv_sem"])
    we_v, wr_v, sm, y, dm = r["we_v"], r["wr_v"], r["sm"], r["y"], r["dres"]

    def serve(point):
        for op, kind, slot in SERVE.get(point, ()):
            swap_to = slot + 3 if slot in U and kind in BOTH else None
            if op == SEND:
                g.issue(slot, (kind,))
            elif op == SWAP:
                g.swapped(slot, (kind,))
            else:
                g.arrive(slot, (kind,), op == NEAR, swap_to)

    barrier = pltpu.get_barrier_semaphore()
    others = [(me ^ o, rep) for o in range(1, members)] + [(me, rep ^ 1)]
    for to in others:
        pl.semaphore_signal(barrier, inc=1, device_id=to, device_id_type=MESH)

    def stage_copies(slot):
        j = chunk_of(slot, parity)
        to = we_v.at[0, slot]
        if not z.aligned:
            return [pltpu.make_async_copy(r["wexp"].at[j], to, r["stage_sem"].at[slot])]
        return [pltpu.make_async_copy(
            r["wexp"].at[:, pl.ds(pl.multiple_of(s * (z.ff // members) + j * sub, sub), sub)],
            to.at[:, s * sub : (s + 1) * sub], r["stage_sem"].at[slot]) for s in range(members)]

    def stored(slot):
        return pltpu.make_async_copy(we_v.at[0, slot], r["ge"].at[slot, me], r["store_sem"].at[slot])

    def staged(slot):
        pltpu.make_async_copy(we_v.at[0, slot], we_v.at[0, slot], r["stage_sem"].at[slot]).wait()
        stored(slot).start()

    for slot in range(SLOTS):
        for cp in stage_copies(slot):
            cp.start()
    pl.semaphore_wait(barrier, len(others))

    def small_copy(o):
        return pltpu.make_async_remote_copy(
            r["small"], sm.at[me], r["sm_send"].at[o], r["sm_recv"].at[o],
            device_id=(me ^ o, rep), device_id_type=MESH)

    for o in range(1, members):
        small_copy(o).start()
    serve("p0")
    sm[me] = r["small"][...]
    for slot in range(SLOTS):
        staged(slot)
    for slot in range(SLOTS):
        stored(slot).wait()
    serve("stage")
    for o in range(1, members):
        pltpu.make_async_copy(sm.at[me ^ o], sm.at[me ^ o], r["sm_recv"].at[o]).wait()

    def vec(row):
        return jnp.concatenate([sm[s, row : row + 1, 0:rows] for s in range(members)], axis=1)

    def norm_rows(src, gain, bias, dst, part):
        gv, bv = vec(gain), vec(bias)

        def body(i, _):
            at = pl.ds(pl.multiple_of(i * 128, 128), 128)
            n, _inv = norm_parts(src[at, :].astype(f32))
            dst[at, :] = (n * gv + bv).astype(bf16)
            return 0

        lax.fori_loop(part * length // 256, (part + 1) * length // 256, body, 0)

    for part in range(2):
        serve("norm_%d" % part)
        norm_rows(r["x"], 0, 1, r["a_v"], part)

    t_row = lax.broadcasted_iota(jnp.int32, (1, length), 1)
    before_t = lax.broadcasted_iota(jnp.int32, (length, length), 0) < lax.broadcasted_iota(
        jnp.int32, (length, length), 1)
    c_ids = lax.broadcasted_iota(jnp.int32, (cap, length), 0)
    lane = lax.broadcasted_iota(jnp.int32, (cap, 128), 1)
    span = length * z.replicas
    first = (me * z.replicas + rep) * length
    tf = t_row.astype(f32)
    chosen = jnp.zeros((length, 128), f32)
    for k in range(members):
        serve("idx_%d" % k)
        row = r["group"][k]
        src = lax.div(row, span)
        src_col = lax.div(r["group_t"][:, k : k + 1], span)
        earlier = jnp.where((src_col == src) & before_t, 1.0, 0.0)
        slot_row = src * cap + jnp.sum(earlier, axis=0, keepdims=True).astype(jnp.int32)
        r["slot"][k] = slot_row
        hit = slot_row == c_ids + me * cap

        def pick(values):
            return jnp.sum(jnp.where(hit, values, 0.0), axis=1, keepdims=True)

        full = pick(jnp.ones_like(tf))
        tok = pick((row - first + 1).astype(f32)) - 1.0
        put = jnp.where(tok == tf, 1.0, 0.0).astype(bf16)
        r["put"][k] = put
        end = jnp.zeros((1, 1), f32)
        start = jnp.zeros_like(tf)
        ids = [jnp.zeros_like(tf) for _ in range(z.projs)]
        for j in range(z.seqs):
            n = sm[k, 8:9, j : j + 1]
            inside = (tf >= end) & (tf < end + n)
            end = end + n
            start = start + jnp.where(tf >= end, n, 0.0)
            for p in range(z.projs):
                at = z.seqs + j * z.projs + p
                ids[p] = ids[p] + jnp.where(inside, sm[k, 8:9, at : at + 1], 0.0)
        info = jnp.where(lane == 0, pick(start) + (1.0 - full), 0.0)
        info = jnp.where(lane == 1, pick(tf), info)
        for p in range(z.projs):
            info = jnp.where(lane == 2 + p, pick(ids[p]), info)
        r["info"][k] = info
        chosen = chosen + dot_tn(put, info.astype(bf16))
    r["chosen"][...] = chosen
    rank_of = lax.broadcasted_iota(jnp.int32, (length, rk), 1) // z.rank

    def mask(p):
        return jnp.where(rank_of.astype(f32) == r["chosen"][:, 2 + p : 3 + p], 1.0, 0.0)

    a_v, q_v = r["a_v"], r["q_v"]
    o_v = q_v
    serve("low")
    r["low0"][...] = (dot_nt(a_v[...], r["q_dn"][...]) * mask(0)).astype(bf16)
    r["low1"][...] = (dot_nt(a_v[...], r["kv_dn"][...]) * mask(1)).astype(bf16)
    out_a = pltpu.make_async_copy(a_v, r["a"], r["out_sem"].at[0])
    out_a.start()

    serve("kvneed")
    g.ready(0, (KV,))
    kv_loads = [pltpu.make_async_copy(
        r["wkv"] if o == 0 else g.place(KV, 0, o), we_v.at[1, me ^ o, :, 0:w], r["kv_send"].at[o]) for o in range(members)]
    for cp in kv_loads:
        cp.start()
    for cp in kv_loads:
        cp.wait()
    back_kv = pltpu.make_async_copy(we_v.at[1, me, :, 0:w], g.place(KV, 0, 0), r["kv_send"].at[0])
    back_kv.start()
    vb = jnp.concatenate([sm[s, 7:8, 0 : hd // members] for s in range(members)], axis=1)
    kv_bias = jnp.concatenate([jnp.zeros((1, hd), f32), vb], axis=1)
    kv = (dot_nn(a_v[...], we_v[1, :, :, 0:w].reshape(d, w)) + kv_bias
          + scale_lora * dot_nn(r["low1"][...], r["kv_up"][...])).astype(bf16)
    for k in range(members):
        r["kvp"][k] = dot_nn(r["put"][k], kv).astype(bf16)

    def kv_copy(o):
        return pltpu.make_async_remote_copy(
            r["kvp"], r["kvs"].at[me], r["kv_send"].at[o], r["kv_recv"].at[o],
            device_id=(me ^ o, rep), device_id_type=MESH)

    back_kv.wait()
    own_kv = pltpu.make_async_copy(r["kvp"], r["kvs"].at[me], r["kv_send"].at[0])
    for o in range(1, members):
        kv_copy(o).start()
    own_kv.start()

    for slot in V:
        g.issue(slot, BOTH, False)
    serve("afterkvx")

    def wide_load(which):
        g.ready(which, HALVES)
        out = []
        for kind in HALVES:
            for o in range(members):
                src = g.own[kind](which) if o == 0 else g.place(kind, which, o)
                for c in range(d // fc):
                    out.append(pltpu.make_async_copy(
                        src.at[:, c * fc : (c + 1) * fc],
                        we_v.at[c, me ^ o, (kind - AT) * half : (kind - AT + 1) * half],
                        r["load_sem"].at[kind - AT, c, o]))
        for cp in out:
            cp.start()
        for cp in out:
            cp.wait()
        back = [pltpu.make_async_copy(
            we_v.at[c, me, (kind - AT) * half : (kind - AT + 1) * half],
            g.place(kind, which, 0).at[:, c * fc : (c + 1) * fc],
            r["load_sem"].at[kind - AT, c, 0]) for kind in HALVES for c in range(d // fc)]
        for cp in back:
            cp.start()
        return back

    serve("wqneed")
    back_q = wide_load(WQ)
    q_bias = vec(2)
    for c in range(d // fc):
        serve("q_%d" % c)
        at = slice(c * fc, (c + 1) * fc)
        q_v[:, at] = (dot_nn(a_v[...], we_v[c].reshape(d, fc)) + q_bias[:, at]
                      + scale_lora * dot_nn(r["low0"][...], r["q_up"][:, at])).astype(bf16)
    out_q = pltpu.make_async_copy(q_v, r["q"], r["out_sem"].at[1])
    out_q.start()

    for cp in back_q:
        cp.wait()

    serve("kvxwait")

    for o in range(1, members):
        pltpu.make_async_copy(r["kvs"].at[me ^ o], r["kvs"].at[me ^ o], r["kv_recv"].at[o]).wait()
    own_kv.wait()
    dm[...] = jnp.zeros_like(dm)

    def kvb_load(k, buf):
        return pltpu.make_async_copy(r["kvs"].at[:, k], r["kvb"].at[buf], r["kvb_sem"].at[buf])

    def kd_out(k, buf):
        return pltpu.make_async_copy(r["kd_st"].at[buf], r["kd"].at[k], r["kd_sem"].at[buf])

    kvb_load(0, 0).start()
    groups = 2

    def attend(k, _):
        buf = lax.rem(k, 2)

        @pl.when(k + 1 < members)
        def _():
            kvb_load(k + 1, 1 - buf).start()

        for i in range(members):
            if "att_%d" % i in SERVE:
                pl.when(k == i)(lambda i=i: serve("att_%d" % i))
        kvb_load(k, buf).wait()
        oh = key_onehot(r["slot"][k], z.slots)
        kvd = dot_tn(oh, r["kvb"][buf].reshape(z.slots, w)).astype(bf16)

        @pl.when(k >= 2)
        def _():
            kd_out(k, buf).wait()

        r["kd_st"][buf] = kvd
        kd_out(k, buf).start()
        put = r["put"][k]
        qp = dot_nn(put, q_v[...]).astype(bf16)
        info = r["info"][k]
        outs = []
        per = heads // groups
        for h in range(groups):
            qr = to_rows(qp[:, h * per * hd : (h + 1) * per * hd], per)
            p = softmax_rows(qr, kvd[:, :hd], info, per).astype(bf16)
            outs.append(to_cols(dot_nn(p, kvd[:, hd:]).astype(bf16), per))
        dm[...] += dot_tn(put, jnp.concatenate(outs, axis=1))
        return 0

    lax.fori_loop(0, members, attend, 0)
    out_q.wait()
    o_v[...] = dm[...].astype(bf16)
    out_o = pltpu.make_async_copy(o_v, r["o"], r["out_sem"].at[2])
    out_o.start()
    r["low2"][...] = (dot_nt(o_v[...], r["mix_dn"][...]) * mask(2)).astype(bf16)
    serve("mixneed")
    back_m = wide_load(WMIX)
    mix_bias = vec(3)
    for c in range(d // fc):
        serve("mix_%d" % c)
        at = slice(c * fc, (c + 1) * fc)
        y[:, at] = (r["x"][:, at].astype(f32) + dot_nn(o_v[...], we_v[c].reshape(d, fc)) + mix_bias[:, at]
                    + scale_lora * dot_nn(r["low2"][...], r["mix_up"][:, at]))

    def load(slot, buf):
        out = [pltpu.make_async_copy(r["ge"].at[slot], we_v.at[buf], r["load_sem"].at[0, buf, 0])]
        for o in range(members):
            src = g.own[WR](slot) if o == 0 else g.place(WR, slot, o)
            out.append(pltpu.make_async_copy(src, wr_v.at[buf, me ^ o], r["load_sem"].at[1, buf, o]))
        return out

    def fetch(slot, buf):
        g.ready(slot, BOTH)
        for cp in load(slot, buf):
            cp.start()

    for cp in back_m:
        cp.wait()
    out_r = pltpu.make_async_copy(y, r["resid"], r["out_sem"].at[3])
    out_r.start()
    out_a.wait()
    m_v = a_v
    for part in range(2):
        serve("norm2_%d" % part)
        norm_rows(y, 4, 5, m_v, part)
    serve("low3")
    out_m = pltpu.make_async_copy(m_v, r["m"], r["out_sem"].at[0])
    out_m.start()
    r["low3"][...] = (dot_nt(m_v[...], r["exp_dn"][...]) * mask(3)).astype(bf16)
    r["e4"][...] = (scale_lora * dot_nt(r["dy"][...], r["red_up"][...]) * mask(4)).astype(bf16)
    dm[...] = jnp.zeros_like(dm)
    r["lowr"][...] = jnp.zeros_like(r["lowr"])
    r["er"][...] = jnp.zeros_like(r["er"])
    out_r.wait()
    y[...] += vec(6)

    def g_out(j, buf):
        return (pltpu.make_async_copy(r["gup_st"].at[buf], r["gup"].at[:, j], r["g_sem"].at[0, buf]),
                pltpu.make_async_copy(r["gdn_st"].at[buf], r["gdn"].at[:, j], r["g_sem"].at[1, buf]))

    serve("mlp_f0")
    fetch(MLP_ORDER[0], 0)

    def step(n, _):
        for i in range(SLOTS):
            if "mlp_%d_0" % i in SERVE:
                pl.when(n == i)(lambda i=i: serve("mlp_%d_0" % i))
        buf = lax.rem(n, 2)
        slot = jnp.int32(0)
        for i, q in enumerate(MLP_ORDER):
            slot = jnp.where(n == i, q, slot)
        for cp in load(slot, buf):
            cp.wait()
        j = chunk_of(slot, parity)
        we = we_v[buf].reshape(d, fc)
        wr = wr_v[buf].reshape(fc, d)
        if z.aligned:
            def cut(ref):
                return jnp.concatenate([ref[:, pl.ds(pl.multiple_of(s * (z.ff // members) + j * sub, sub), sub)]
                                        for s in range(members)], axis=1)
            bup, adn = cut(r["exp_up"]), cut(r["red_dn"])
        else:
            bup, adn = r["exp_up"][j], r["red_dn"][j]
        be = jnp.concatenate([sm[s, 0:SLOTS, rows : rows + sub] for s in range(members)], axis=1)
        be = jnp.sum(jnp.where(lax.broadcasted_iota(jnp.int32, (SLOTS, fc), 0) == j, be, 0.0), axis=0, keepdims=True)
        hid = dot_nn(m_v[...], we) + be
        hid = hid + scale_lora * dot_nn(r["low3"][...], bup)
        cube = hid * hid * hid
        t = jnp.tanh(gelu_c * (hid + 0.044715 * cube))
        act = (0.5 * hid * (1.0 + t)).astype(bf16)
        slope = 0.5 * (1.0 + t) + 0.5 * hid * (1.0 - t * t) * (
            gelu_c * (1.0 + 3.0 * 0.044715 * hid * hid)
        )
        dact = dot_nt(r["dy"][...], wr) + dot_nn(r["e4"][...], adn)
        dh = (dact * slope).astype(bf16)
        for i in range(SLOTS):
            def middle(i=i):
                serve("mlp_%d_1" % i)
                if i + 1 < SLOTS:
                    fetch(MLP_ORDER[i + 1], (i + 1) % 2)
            pl.when(n == i)(middle)
        y[...] += dot_nn(act, wr)
        dm[...] += dot_nt(dh, we)
        r["lowr"][...] += dot_nt(act, adn)
        r["er"][...] += dot_nt(dh, bup)
        gup = (scale_lora * dot_tn(r["low3"][...], dh)).astype(bf16)
        gdn = dot_tn(r["e4"][...], act).astype(bf16)

        @pl.when(n >= 2)
        def _():
            for cp in g_out(j, buf):
                cp.wait()

        for to in range(members):
            r["gup_st"][buf, to] = gup[:, to * sub : (to + 1) * sub]
            r["gdn_st"][buf, to] = gdn[:, to * sub : (to + 1) * sub]
        for cp in g_out(j, buf):
            cp.start()
        return 0

    lax.fori_loop(0, SLOTS, step, 0)

    low4 = (r["lowr"][...] * mask(4)).astype(bf16)
    r["low4"][...] = low4
    out_o.wait()
    layer_v = q_v
    for c in range(d // fc):
        at = slice(c * fc, (c + 1) * fc)
        layer_v[:, at] = (y[:, at] + scale_lora * dot_nn(low4, r["red_up"][:, at])).astype(bf16)
    out_l = pltpu.make_async_copy(layer_v, r["layer"], r["out_sem"].at[1])
    out_l.start()
    back_r = pltpu.make_async_copy(r["resid"], y, r["out_sem"].at[3])
    back_r.start()
    e3 = (scale_lora * r["er"][...] * mask(3)).astype(bf16)
    r["e3"][...] = e3
    gain = vec(4)
    back_r.wait()

    def last(i, _):
        at = pl.ds(pl.multiple_of(i * 128, 128), 128)
        n, inv = norm_parts(y[at, :])
        dn = dm[at, :] + dot_nn(r["e3"][at, :], r["exp_dn"][...])
        dm[at, :] = r["dy"][at, :].astype(f32) + norm_back(n, inv, gain, dn)
        return 0

    lax.fori_loop(0, length // 128, last, 0)
    out_l.wait()
    out_m.wait()
    for buf in range(2):
        kd_out(buf, buf).wait()
        for cp in g_out(buf, buf):
            cp.wait()
    for o in range(1, members):
        small_copy(o).wait_send()
        kv_copy(o).wait_send()
    g.finish()


def forward(z, args):
    vm = pl.BlockSpec(memory_space=pltpu.VMEM)
    hbm = pl.BlockSpec(memory_space=pl.ANY)
    m, n, d, rk, w = z.members, z.length, z.d, z.rk, z.w
    s = jax.ShapeDtypeStruct
    half = z.rows // 2
    outs = dict(
        dres=s((n, d), f32), put=s((m, z.cap, n), bf16), slot=s((m, 1, n), jnp.int32),
        info=s((m, z.cap, 128), f32), chosen=s((n, 128), f32),
        low0=s((n, rk), bf16), low1=s((n, rk), bf16), low2=s((n, rk), bf16), low4=s((n, rk), bf16), e3=s((n, rk), bf16),
        a=s((n, d), bf16), q=s((n, d), bf16), o=s((n, d), bf16), m=s((n, d), bf16), resid=s((n, d), f32),
        kd=s((m, n, w), bf16), gup=s((m, SLOTS, rk, z.sub), bf16), gdn=s((m, SLOTS, rk, z.sub), bf16),
        layer=s((n, d), bf16), kvs=s((m, m, z.cap, w), bf16),
        ge=s((SLOTS, m, z.rows, z.fc), bf16), gr=s((SLOTS, m, z.sub, d), bf16),
        ga=s((2, m, half, d), bf16), gb=s((2, m, half, d), bf16), gk=s((1, m, z.rows, w), bf16))
    in_vmem = FWD_OUT[:10]
    sends = m - 1 + m // 2
    dma = pltpu.SemaphoreType.DMA
    items = 2 * SLOTS + 5
    scratch = dict(
        y=pltpu.VMEM((n, d), f32), we_v=pltpu.VMEM((2, m, z.rows, z.fc), bf16), wr_v=pltpu.VMEM((2, m, z.sub, d), bf16),
        a_v=pltpu.VMEM((n, d), bf16), q_v=pltpu.VMEM((n, d), bf16),
        kvp=pltpu.VMEM((m, z.cap, w), bf16), kvb=pltpu.VMEM((2, m, z.cap, w), bf16),
        kd_st=pltpu.VMEM((2, n, w), bf16), gup_st=pltpu.VMEM((2, m, rk, z.sub), bf16),
        gdn_st=pltpu.VMEM((2, m, rk, z.sub), bf16), sm=pltpu.VMEM((m, 16, z.small_cols), f32),
        lowr=pltpu.VMEM((n, rk), f32), er=pltpu.VMEM((n, rk), f32), low3=pltpu.VMEM((n, rk), bf16), e4=pltpu.VMEM((n, rk), bf16),
        send_sem=dma((items, sends)), recv_sem=dma((items, m)), sm_send=dma((m,)), sm_recv=dma((m,)),
        kv_send=dma((m,)), kv_recv=dma((m,)), stage_sem=dma((SLOTS,)), store_sem=dma((SLOTS,)),
        load_sem=dma((2, 2, m)), kvb_sem=dma((2,)), kd_sem=dma((2,)), g_sem=dma((2, 2)), out_sem=dma((4,)))
    got = pl.pallas_call(
        lambda *refs: fwd_kernel(z, *refs),
        in_specs=[hbm if k.startswith("w") else vm for k in FWD_IN],
        out_specs=[vm if k in in_vmem else hbm for k in FWD_OUT],
        out_shape=[outs[k] for k in FWD_OUT],
        scratch_shapes=[scratch[k] for k in FWD_SCRATCH],
        compiler_params=pltpu.CompilerParams(
            vmem_limit_bytes=FWD_VMEM, collective_id=1, has_side_effects=True),
    )(*[args[k] for k in FWD_IN])
    return dict(zip(FWD_OUT, got))


FWD_VMEM = 62 * 1024 * 1024


def grads_kernel(scales, *refs):
    out = refs[-1]
    at = 0
    for i, sc in enumerate(scales):
        left, right = refs[2 * i][...], refs[2 * i + 1][...]
        owners = out.shape[0]
        w = right.shape[1] // owners
        g = dot_tn(left, right) * sc
        for to in range(owners):
            out[to, :, at : at + w] = g[:, to * w : (to + 1) * w].astype(bf16)
        at += w


def grads(owners, pairs):
    rk = pairs[0][0].shape[1]
    width = sum(p[1].shape[1] for p in pairs) // owners
    vm = pl.BlockSpec(memory_space=pltpu.VMEM)
    return pl.pallas_call(
        lambda *refs: grads_kernel([p[2] for p in pairs], *refs),
        in_specs=[vm] * (2 * len(pairs)),
        out_specs=vm,
        out_shape=jax.ShapeDtypeStruct((owners, rk, width), bf16),
        compiler_params=pltpu.CompilerParams(vmem_limit_bytes=VMEM_LIMIT),
    )(*[x for p in pairs for x in p[:2]])


def exchange(v, axis, bit):
    return lax.ppermute(v, axis, [(i, i ^ bit) for i in range(lax.axis_size(axis))])


def reduce_share(parts, turn):
    me = lax.axis_index("shard")
    count = parts.shape[0].bit_length() - 1
    left = list(range(count))[::-1]
    cur = parts.reshape((2,) * count + parts.shape[1:])
    order = [0] + (list(range(1, count)) if turn == 0 else list(range(1, count))[::-1])
    for i, bit in enumerate(order):
        pos = left.index(bit)
        mine = (me >> bit) & 1
        send = lax.dynamic_index_in_dim(cur, 1 - mine, pos, keepdims=False)
        keep = lax.dynamic_index_in_dim(cur, mine, pos, keepdims=False)
        cur = keep.astype(f32) + exchange(send, "shard", 1 << bit).astype(f32)
        left.remove(bit)
        if i + 1 < count:
            cur = cur.astype(bf16)
    bit = 1
    while bit < lax.axis_size("rep"):
        low = cur.astype(bf16)
        cur = low.astype(f32) + exchange(low, "rep", bit).astype(f32)
        bit *= 2
    return cur


def local(tokens, out_grad, token_perm, seq_lens, adapter_ids,
          attn_g, attn_b, wq, bq, wkv, bv, wmix, bmix, mlp_g, mlp_b, wexp, bexp, wred, bred,
          q_dn, q_up, kv_dn, kv_up, mix_dn, mix_up, exp_dn, exp_up, red_dn, red_up):
    members = lax.axis_size("shard")
    replicas = lax.axis_size("rep")
    rep = lax.axis_index("rep")
    length, d = tokens.shape
    experts, rank = q_dn.shape[:2]
    rk = experts * rank
    z = Sizes(members, replicas, length, d, wexp.shape[1], bv.shape[0] * members, rk, rank,
              seq_lens.shape[1], adapter_ids.shape[2])
    flat = lambda s: s.reshape(rk, s.shape[2])
    q_dn, q_up, kv_dn, kv_up, mix_dn, mix_up, exp_dn, exp_up, red_dn, red_up = map(
        flat, (q_dn, q_up, kv_dn, kv_up, mix_dn, mix_up, exp_dn, exp_up, red_dn, red_up))
    group = lax.dynamic_index_in_dim(
        token_perm.reshape(members, replicas, length), rep, 1, keepdims=False)

    def pad(rows, cols):
        return jnp.pad(rows.astype(f32), ((0, 0), (0, cols - rows.shape[1])))

    vecs = jnp.concatenate([v[None] for v in (attn_g, attn_b, bq, bmix, mlp_g, mlp_b, bred)]
                           + [pad(bv[None], z.rows).astype(bf16)], axis=0)
    top = pad(jnp.concatenate([vecs, bexp.reshape(SLOTS, z.sub)], axis=1), z.small_cols)
    table = pad(jnp.concatenate([seq_lens[0], adapter_ids[0].reshape(-1)])[None], z.small_cols)
    small = jnp.concatenate([top, table, jnp.zeros((7, z.small_cols), f32)], axis=0)
    by_chunk = lambda s: s.reshape(s.shape[0], members, SLOTS, z.sub).transpose(2, 0, 1, 3).reshape(
        SLOTS, s.shape[0], z.fc)
    chunked = (lambda s: s) if z.aligned else by_chunk
    got = forward(z, dict(
        x=tokens, dy=out_grad, small=small, group=group.reshape(members, 1, length), group_t=group.T,
        q_dn=q_dn, q_up=q_up, kv_dn=kv_dn, kv_up=kv_up, mix_dn=mix_dn, mix_up=mix_up, exp_dn=exp_dn,
        exp_up=chunked(exp_up), red_dn=chunked(red_dn), red_up=red_up,
        wq=wq, wkv=wkv, wmix=wmix, wexp=chunked(wexp), wred=wred.reshape(SLOTS, z.sub, d)))
    r_exp_up = reduce_share(got["gup"], 0)
    r_red_dn = reduce_share(got["gdn"], 1)
    wq_f, wmix_f = (jnp.stack([got["ga"][i], got["gb"][i]], axis=1).reshape(d, d) for i in (WQ, WMIX))
    wkv_f = got["gk"].reshape(d, z.w)
    attn_gain = lax.all_gather(attn_g, "shard", axis=0, tiled=True).astype(f32)
    owner = jnp.arange(rk, dtype=jnp.int32) // rank
    masks = [(owner[None, :].astype(f32) == got["chosen"][:, 2 + p : 3 + p]).astype(f32) for p in range(3)]
    put = got["put"].reshape(z.slots, length)
    low0, low1, low2, low4, e3 = (got[k] for k in ("low0", "low1", "low2", "low4", "e3"))
    a, o, m, dres, layer_out = (got[k] for k in ("a", "o", "m", "dres", "layer"))
    x = tokens.astype(f32)
    nx, inv_x = norm_parts(x)
    qpad = dot_nn(put, got["q"]).astype(bf16).reshape(members, z.cap, d)

    def stack(g):
        return g.reshape(experts, rank, g.shape[1])

    def stack_chunks(g):
        return stack(g.transpose(1, 0, 2).reshape(rk, SLOTS * z.sub))

    dresl = dres.astype(bf16)
    e2 = (scale_lora * dot_nt(dresl, mix_up) * masks[2]).astype(bf16)
    do = (dot_nt(dresl, wmix_f) + dot_nn(e2, mix_dn)).astype(bf16)
    r_down = reduce_share(grads(members, [(e3, m, 1.0), (e2, o, 1.0)]), 0)
    r_up = reduce_share(grads(members, [(low4, out_grad, scale_lora), (low2, dresl, scale_lora)]), 1)
    dopad = dot_nn(put, do).astype(bf16).reshape(members, z.cap, d)
    dqpad, dslots = attn_bwd(z.heads, got["slot"], got["info"], qpad, dopad, got["kd"])
    back = lax.all_to_all(dslots, "shard", split_axis=0, concat_axis=0, tiled=True)
    dkvp = jnp.sum(back.astype(f32), axis=0).astype(bf16).reshape(z.slots, z.w)
    dq = dot_tn(put, dqpad.reshape(z.slots, d)).astype(bf16)
    dkv = dot_tn(put, dkvp).astype(bf16)
    e0 = (scale_lora * dot_nt(dq, q_up) * masks[0]).astype(bf16)
    e1 = (scale_lora * dot_nt(dkv, kv_up) * masks[1]).astype(bf16)
    da = (dot_nt(dq, wq_f) + dot_nn(e0, q_dn)) + (dot_nt(dkv, wkv_f) + dot_nn(e1, kv_dn))
    tokens_grad = (dres + norm_back(nx, inv_x, attn_gain, da)).astype(bf16)
    r_qkv_down = reduce_share(grads(members, [(e0, a, 1.0), (e1, a, 1.0)]), 0)
    r_qkv_up = reduce_share(grads(members, [(low0, dq, scale_lora), (low1, dkv, scale_lora)]), 1)
    c = d // members
    return (layer_out, tokens_grad, stack(r_qkv_down[:, :c]), stack(r_qkv_up[:, :c]), stack(r_qkv_down[:, c:]),
            stack(r_qkv_up[:, c:]), stack(r_down[:, c:]), stack(r_up[:, c:]), stack(r_down[:, :c]),
            stack_chunks(r_exp_up), stack_chunks(r_red_dn), stack(r_up[:, :c]))


def solution(mesh):
    both = ("shard", "rep")
    row, vec = P("shard", None), P("shard")
    in_specs = (
        P(both, None), P(both, None), P(), P(both, None), P(both, None, None),
        vec, vec, row, vec, row, vec, row, vec, vec, vec, row, vec, row, vec,
    ) + (P(),) * 10
    out_specs = (P(both, None), P(both, None)) + (P(None, None, "shard"),) * 10
    return jax.shard_map(local, mesh=mesh, in_specs=in_specs, out_specs=out_specs, check_vma=False)
```

time: 727 us -> 624 us (0.86); the launches traced: 727 us -> 615 us
  matrix products: 107 us -> 45.4 us
  Pallas kernels: 316 us -> 374 us
  waiting for transfers between devices: 124 us -> 67.7 us
  blocking collectives: 33.4 us -> 9.66 us
  between operations: 17 us -> 1.83 us
  starting transfers between devices: 40.1 us -> 29.3 us
    pallas_call x2 -> x1, Pallas kernels: 268 us -> 326 us  [forward(): pl.pallas_call(lambda *refs: fwd_kernel(z, *refs), in_specs=[hbm if k.sta...]
    all_gather x2 -> x0, waiting for transfers between devices: 48.2 us -> none  [the longest x1 48.2 us: local(): lax.all_gather(jnp.concatenate([wq, wkv, wmix], axis=1), 'shard', axis=0,...]
    dot_general x11 -> x4, matrix products: 63.8 us -> 16.6 us  [dot_nn(): lax.dot_general(a, b, (((1,), (0,)), ((), ())), preferred_element_type=f32)]
    unnamed x2 -> x0, blocking collectives: 33.4 us -> none
    another operation x4 -> x3, local copies, waits for them, and re-layouts: 4.36 us -> 27.9 us  [local(): jnp.stack([got['ga'][i], got['gb'][i]], axis=1).reshape(d, d)]
    reshape x5 -> x0, local copies, waits for them, and re-layouts: 19.5 us -> none  [the longest x2 8.77 us: local(): s.reshape(rk, members, chunks, sub).transpose(2, 0, 1, 3)]
    unnamed x161 -> x62, local copies, waits for them, and re-layouts: 15.4 us -> 1.46 us
    another operation x1 -> x2, other arithmetic: 0.69 us -> 13.8 us  [local(): jnp.stack([got['ga'][i], got['gb'][i]], axis=1).reshape(d, d)]
  transfers between devices with their start and end apart: 33 -> 31, of which waited for: 20 -> 21; matrix products, arithmetic and copies ran while one was open for 20% -> 18% of each run, Pallas kernels for 6% -> 7%
where the time goes in v3:
time: 624 us; the launch traced here: 615 us
  Pallas kernels  374 us (60%)
  waiting for transfers between devices  67.7 us (11%)
  local copies, waits for them, and re-layouts  56 us (9%)
  matrix products  45.4 us (7%)
  other arithmetic  31 us (5%)
  starting transfers between devices  29.3 us (5%)
  blocking collectives  9.66 us (2%)
    pallas_call x1, Pallas kernels, forward(): pl.pallas_call(lambda *refs: fwd_kernel(z, *refs), in_specs=[hbm if k.sta...  326 us
    ppermute x30, waiting for transfers between devices, exchange(): lax.ppermute(v, axis, [(i, i ^ bit) for i in range(lax.axis_size(axis))])  67.7 us
    pallas_call x1, Pallas kernels, attn_bwd(): pl.pallas_call(lambda *refs: attn_bwd_kernel(heads, *refs), grid=(m,), in...  32.7 us
    another operation x3, local copies, waits for them, and re-layouts, local(): jnp.stack([got['ga'][i], got['gb'][i]], axis=1).reshape(d, d)  27.9 us
    ppermute x30, starting transfers between devices, exchange(): lax.ppermute(v, axis, [(i, i ^ bit) for i in range(lax.axis_size(axis))])  24.3 us
    dot_general x6, matrix products, dot_nt(): lax.dot_general(a, b, (((1,), (1,)), ((), ())), preferred_element_type=f32)  23.9 us
    dot_general x4, matrix products, dot_nn(): lax.dot_general(a, b, (((1,), (0,)), ((), ())), preferred_element_type=f32)  16.6 us
    pallas_call x4, Pallas kernels, grads(): pl.pallas_call(lambda *refs: grads_kernel([p[2] for p in pairs], *refs),...  15.4 us
  transfers between devices with their start and end apart: 31, of which 21 were waited for; matrix products, arithmetic and copies ran while one was open for 18% of the time, Pallas kernels for 7%

profile of v3, /device:TPU:0, one launch (start us, length us, event | category | flops | bytes accessed | tf_op | source)
XLA Modules:
  0.0 615.0 jit_solution(18411127248442688276)
XLA Ops:
  10.6 326.1 %shard_map.364 = (f32[512,2048]{1,0:T(8,128)}, bf16[8,96,512]{2,1,0:T(8,128)(2,1)}, s32[8,1,512]{2,1,0:T(1,128)}, f32[8,96,128]{2,1,0:T(8,128)}, f32[512,128]{1,...) custom-call(bf16[512,2048]{1,0:T(8,128)(2,1)} %refs_0_.1, ...), custom_call_target="tpu_custom_call" | custom-call | tf_op jit(solution)/shard_map/pallas_call | solution.py:702
  336.7 2.5 dynamic-slice_bitcast_fusion
  339.2 2.3 dynamic-slice_bitcast_fusion.1
  342.1 1.6 convert_element_type.389.refs_3_
  343.7 4.2 shard_map.369
  347.9 1.9 dynamic-slice_bitcast_fusion.4
  350.7 1.4 fusion.18.refs_2_
  352.1 4.0 shard_map.368
  356.1 1.9 dynamic-slice_bitcast_fusion.5
  358.5 11.3 %slice_bitcast_fusion = (bf16[8,1,128,2048]{3,2,0,1:T(8,128)(2,1)}, bf16[8,1,128,2048]{3,2,0,1:T(8,128)(2,1)S(1)}, bf16[8,1,128,2048]{3,2,0,1:T(8,128)(2,1)}, bf16[8,1,128,2048]{3,2,0,1:T(8,128)(2,1)}) fusion(bf16[2,8,128,2048]{3,2,1,0:T(8,128)(2,1)} %get-tuple-element.42, bf16[2,8,128,2048]{3,2,1,0:T(8,128)(2,1)} %get-tuple-element.41), kind=kLoop, calls=%fused_computation.16 | loop fusion | bytes 33554432 | tf_op jit(solution)/shard_map/stack;squeeze | solution.py:805
  369.8 6.2 %pad_maximum_fusion = bf16[8,2,128,2048]{3,2,0,1:T(8,128)(2,1)} fusion(bf16[8,1,128,2048]{3,2,0,1:T(8,128)(2,1)S(1)} %get-tuple-element.66, bf16[8,1,128,2048]{3,2,0,1:T(8,128)(2,1)} %get-tuple-element.74), kind=kLoop, calls=%fused_computation | loop fusion | flops 4194304 | bytes 16777216 | tf_op jit(solution)/shard_map/stack | solution.py:805
  376.0 8.3 %copy.50 = bf16[8,2,128,2048]{3,2,1,0:T(8,128)(2,1)} copy(bf16[8,2,128,2048]{3,2,0,1:T(8,128)(2,1)} %pad_maximum_fusion) | data formatting | bytes 16777216 | tf_op jit(solution)/shard_map/stack | solution.py:805
  384.3 9.7 %fusion.42 = f32[512,2048]{1,0:T(8,128)} fusion(bf16[512,2048]{1,0:T(8,128)(2,1)S(1)} %copy-done.4, bf16[2048,2048]{1,0:T(8,128)(2,1)} %bitcast.170), kind=kOutput, calls=%fused_computation.124 | convolution fusion | flops 4294967296 | bytes 14680064 | tf_op jit(solution)/shard_map/dot_general | solution.py:22
  394.1 6.5 %convolution_convert_fusion = bf16[768,2048]{1,0:T(8,128)(2,1)} fusion(bf16[768,512]{1,0:T(8,128)(2,1)S(1)} %bitcast.195, f32[512,2048]{1,0:T(8,128)} %fusion.42, bf16[512,128]{1,0:T(8,128)(2,1)S(1)} %copy-done.26, bf16[128,2048]{1,0:T(8,128)(2,1)} %bitcast.202), kind=kOutput, calls=%fused_computation.21 | convolution fusion | flops 1882718208 | bytes 8781824 | tf_op jit(solution)/shard_map/dot_general | solution.py:18
  400.5 3.5 convolution_convert_fusion.1
  404.0 32.7 %shard_map.365 = (bf16[8,96,2048]{2,1,0:T(8,128)(2,1)}, bf16[8,8,96,256]{3,2,1,0:T(8,128)(2,1)}) custom-call(s32[8,1,512]{2,1,0:T(1,128)} %get-tuple-element.38.refs_0_, f32[8,96,128]{2,1,0:T(8,128)} %get-tuple-element.39.refs_1_, bf16[8,96,2048]{2,1,0:T(8,128)(2,1)} %bitcast.180, bf16[8,96,2048]{2,1,0:T(8,128)(2,1)} %bitcast.179, ...), custom_call_target="tpu_custom_call" | custom-call | tf_op jit(solution)/shard_map/pallas_call | solution.py:81
  436.8 5.0 all-to-all-start
  442.2 3.8 bitcast_convert_fusion.refs_1_
  446.7 2.7 fusion.44
  449.4 7.5 %pad_maximum_fusion.1 = bf16[8,2,128,2048]{3,2,0,1:T(8,128)(2,1)} fusion(bf16[8,1,128,2048]{3,2,0,1:T(8,128)(2,1)} %get-tuple-element.65, bf16[8,1,128,2048]{3,2,0,1:T(8,128)(2,1)} %get-tuple-element.75), kind=kLoop, calls=%fused_computation.1 | loop fusion | flops 4194304 | bytes 16777216 | tf_op jit(solution)/shard_map/stack | solution.py:805
  456.9 8.3 %copy.51 = bf16[8,2,128,2048]{3,2,1,0:T(8,128)(2,1)} copy(bf16[8,2,128,2048]{3,2,0,1:T(8,128)(2,1)} %pad_maximum_fusion.1) | data formatting | bytes 16777216 | tf_op jit(solution)/shard_map/stack | solution.py:805
  465.2 9.6 %fusion.43 = f32[512,2048]{1,0:T(8,128)} fusion(bf16[512,2048]{1,0:T(8,128)(2,1)S(1)} %bitcast_convert_fusion.refs_1_, bf16[2048,2048]{1,0:T(8,128)(2,1)} %bitcast.171), kind=kOutput, calls=%fused_computation.125 | convolution fusion | flops 4294967296 | bytes 14680064 | tf_op jit(solution)/shard_map/dot_general | solution.py:22
  474.8 9.7 %all-gather = bf16[8,1,256]{2,1,0:T(2,128)(2,1)S(1)} all-gather(bf16[1,1,256]{2,1,0:T(2,128)(2,1)S(1)} %reshape.280), channel_id=1, replica_groups=mesh['shard'=8,'rep'=4] {'shard'}, dimensions={0}, use_global_device_ids=true | all-gather | bytes 4608 | tf_op jit(solution)/shard_map/all_gather | solution.py:807
  485.2 1.3 fusion.21
  486.5 1.5 collective-permute-start.16
  488.1 1.2 fusion.22
  489.9 5.2 collective-permute-done.16
  495.2 1.5 collective-permute-start.17
  498.4 2.1 collective-permute-done.17
  500.8 2.1 collective-permute-done.12
  503.3 3.1 collective-permute-done.18
  506.4 3.2 collective-permute-start.19
  509.6 2.8 collective-permute-start.14
  512.4 1.6 fusion.10
  514.0 1.4 collective-permute-start.26
  515.4 1.6 fusion.11
  517.9 6.6 %collective-permute-done.26 = bf16[2,8,128,128]{3,2,1,0:T(8,128)(2,1)S(1)} collective-permute-done((bf16[2,8,128,128]{3,2,1,0:T(8,128)(2,1)S(1)}, bf16[2,8,128,128]{3,2,1,0:T(8,128)(2,1)S(1)}, u32[]{:S(2)}, u32[]{:S(2)}) %collective-permute-start.26) | collective-permute-done | bytes 524320 | tf_op jit(solution)/shard_map/ppermute | solution.py:744
  524.9 4.3 collective-permute-done.21
  530.4 1.5 collective-permute-done.27
  532.1 3.7 collective-permute-done.22
  536.7 4.9 collective-permute-done.28
  541.7 4.6 collective-permute-done.23
  547.2 8.8 %collective-permute-done.29 = bf16[8,128,128]{2,1,0:T(8,128)(2,1)S(1)} collective-permute-done((bf16[8,128,128]{2,1,0:T(8,128)(2,1)S(1)}, bf16[8,128,128]{2,1,0:T(8,128)(2,1)S(1)}, u32[]{:S(2)}, u32[]{:S(2)}) %collective-permute-start.29) | collective-permute-done | bytes 262176 | tf_op jit(solution)/shard_map/ppermute | solution.py:744
  557.3 1.6 collective-permute-done.24
  560.2 2.4 reduce_sum.48
  562.6 1.1 fusion.12.refs_3_
  563.7 3.2 shard_map.367
  567.0 1.9 dynamic-slice_bitcast_fusion.7
  568.9 1.7 fusion.16.refs_2_
  570.6 4.0 shard_map.366
  574.6 1.2 dynamic-slice_bitcast_fusion.6
  577.2 4.0 fusion.38
  581.3 2.7 fusion.8
  584.7 1.8 collective-permute-start.1
  586.5 4.9 collective-permute-done.6
  591.8 1.2 collective-permute-done.1
  593.2 2.5 collective-permute-start.2
  596.3 2.4 collective-permute-done.2
  598.8 2.7 collective-permute-done.8
  601.5 1.7 collective-permute-start.9
  603.2 1.3 collective-permute-done.3
  604.5 1.3 collective-permute-start.4
  605.8 5.2 collective-permute-done.9
  613.2 1.3 copy.55
  (171 shorter events, 29.4 us)
Async XLA Ops:
  1.5 9.1 %copy-start.25 = (s32[8,1,512]{2,1,0:T(1,128)}, s32[8,1,512]{2,1,0:T(1,128)S(1)}, u32[]{:S(2)}) copy-start(s32[8,1,512]{2,1,0:T(1,128)S(1)} %constant_dynamic-slice_fusion.refs_3_) | copy-start | bytes 49156
  336.7 5.4 copy-start.1
  339.2 173.1 %collective-permute-start.25 = (bf16[2,2,8,128,128]{4,3,2,1,0:T(8,128)(2,1)}, bf16[2,2,8,128,128]{4,3,2,1,0:T(8,128)(2,1)}, u32[]{:S(2)}, u32[]{:S(2)}) collective-permute-start(bf16[2,2,8,128,128]{4,3,2,1,0:T(8,128)(2,1)} %dynamic-slice_bitcast_fusion), channel_id=1, source_target_pairs={{0,4},{4,0},{8,12},{12,8},{16,20},{20,16},{24,28},{28,24},{1,5},{5... | collective-permute-start | bytes 3145736 | tf_op jit(solution)/shard_map/ppermute | solution.py:744
  341.6 173.9 %collective-permute-start.20 = (bf16[2,2,8,128,128]{4,3,2,1,0:T(8,128)(2,1)}, bf16[2,2,8,128,128]{4,3,2,1,0:T(8,128)(2,1)}, u32[]{:S(2)}, u32[]{:S(2)}) collective-permute-start(bf16[2,2,8,128,128]{4,3,2,1,0:T(8,128)(2,1)} %dynamic-slice_bitcast_fusion.1), channel_id=1, source_target_pairs={{0,4},{4,0},{8,12},{12,8},{16,20},{20,16},{24,28},{28,24},{1,5},{5... | collective-permute-start | bytes 3145736 | tf_op jit(solution)/shard_map/ppermute | solution.py:744
  343.7 6.1 copy-start.10
  343.7 7.0 %copy-start.4 = (bf16[512,2048]{1,0:T(8,128)(2,1)S(1)}, bf16[512,2048]{1,0:T(8,128)(2,1)}, u32[]{:S(2)}) copy-start(bf16[512,2048]{1,0:T(8,128)(2,1)} %convert_element_type.389.refs_3_) | copy-start | bytes 6291460
  343.7 7.0 %copy-start.23 = (bf16[8,16,2048]{2,1,0:T(8,128)(2,1)S(1)}, bf16[8,16,2048]{2,1,0:T(8,128)(2,1)}, u32[]{:S(2)}) copy-start(bf16[8,16,2048]{2,1,0:T(8,128)(2,1)} %param.53) | copy-start | bytes 1572868
  349.8 135.4 %collective-permute-start.15 = (bf16[2,2,128,512]{3,2,1,0:T(8,128)(2,1)}, bf16[2,2,128,512]{3,2,1,0:T(8,128)(2,1)}, u32[]{:S(2)}, u32[]{:S(2)}) collective-permute-start(bf16[2,2,128,512]{3,2,1,0:T(8,128)(2,1)} %dynamic-slice_bitcast_fusion.4), channel_id=1, source_target_pairs={{0,4},{4,0},{8,12},{12,8},{16,20},{20,16},{24,28},{28,24},{1,5},{5... | collective-permute-start | bytes 1572872 | tf_op jit(solution)/shard_map/ppermute | solution.py:744
  349.8 96.2 %copy-start.29 = (f32[128]{0:T(128)}, f32[128]{0:T(128)S(1)}, u32[]{:S(2)}) copy-start(f32[128]{0:T(128)S(1)} %fusion.37) | copy-start | bytes 1540
  358.0 130.1 %collective-permute-start.10 = (bf16[2,2,128,512]{3,2,1,0:T(8,128)(2,1)}, bf16[2,2,128,512]{3,2,1,0:T(8,128)(2,1)}, u32[]{:S(2)}, u32[]{:S(2)}) collective-permute-start(bf16[2,2,128,512]{3,2,1,0:T(8,128)(2,1)} %dynamic-slice_bitcast_fusion.5), channel_id=1, source_target_pairs={{0,4},{4,0},{8,12},{12,8},{16,20},{20,16},{24,28},{28,24},{1,5},{5... | collective-permute-start | bytes 1572872 | tf_op jit(solution)/shard_map/ppermute | solution.py:744
  384.3 9.7 %copy-start.18 = (bf16[8,96,512]{2,1,0:T(8,128)(2,1)S(1)}, bf16[8,96,512]{2,1,0:T(8,128)(2,1)}, u32[]{:S(2)}) copy-start(bf16[8,96,512]{2,1,0:T(8,128)(2,1)} %get-tuple-element.37) | copy-start | bytes 2359300
  384.3 9.7 %copy-start.26 = (bf16[512,128]{1,0:T(8,128)(2,1)S(1)}, bf16[512,128]{1,0:T(8,128)(2,1)}, u32[]{:S(2)}) copy-start(bf16[512,128]{1,0:T(8,128)(2,1)} %fusion.18.refs_2_) | copy-start | bytes 393220
  394.0 6.5 %copy-start.27 = (bf16[512,2048]{1,0:T(8,128)(2,1)S(1)}, bf16[512,2048]{1,0:T(8,128)(2,1)}, u32[]{:S(2)}) copy-start(bf16[512,2048]{1,0:T(8,128)(2,1)} %get-tuple-element.40) | copy-start | bytes 6291460
  436.8 5.0 copy-start
  436.8 5.4 copy-start.19
  436.8 123.4 %all-to-all-start = ((bf16[8,8,96,256]{3,2,1,0:T(8,128)(2,1)}), bf16[8,8,96,256]{3,2,1,0:T(8,128)(2,1)}, u32[]{:S(2)}, u32[]{:S(2)}) async-start(bf16[8,8,96,256]{3,2,1,0:T(8,128)(2,1)} %get-tuple-element.46), calls=%async_computation | async-start | bytes 6291456 | tf_op jit(solution)/shard_map/all_to_all | solution.py:830
  441.8 4.2 copy-start.24
  442.2 4.5 copy-start.14
  445.9 19.2 %copy-start.5 = (bf16[512,2048]{1,0:T(8,128)(2,1)}, bf16[512,2048]{1,0:T(8,128)(2,1)S(1)}, u32[]{:S(2)}) copy-start(bf16[512,2048]{1,0:T(8,128)(2,1)S(1)} %bitcast_convert_fusion.refs_1_) | copy-start | bytes 6291460
  446.7 10.2 %copy-start.22 = (bf16[512,128]{1,0:T(8,128)(2,1)}, bf16[512,128]{1,0:T(8,128)(2,1)S(1)}, u32[]{:S(2)}) copy-start(bf16[512,128]{1,0:T(8,128)(2,1)S(1)} %fusion.17.refs_0_) | copy-start | bytes 393220
  465.2 9.6 %copy-start.28 = (bf16[256]{0:T(256)(128)(2,1)S(1)}, bf16[256]{0:T(256)(128)(2,1)}, u32[]{:S(2)}) copy-start(bf16[256]{0:T(256)(128)(2,1)} %param.34) | copy-start | bytes 1540
  465.2 20.0 %copy-start.6 = (bf16[8,128,512]{2,1,0:T(8,128)(2,1)S(1)}, bf16[8,128,512]{2,1,0:T(8,128)(2,1)}, u32[]{:S(2)}) copy-start(bf16[8,128,512]{2,1,0:T(8,128)(2,1)} %shard_map.369) | copy-start | bytes 3145732
  484.4 3.6 copy-start.7
  485.1 27.2 %copy-start.12 = (bf16[8,8,128,128]{3,2,1,0:T(8,128)(2,1)S(1)}, bf16[8,8,128,128]{3,2,1,0:T(8,128)(2,1)}, u32[]{:S(2)}) copy-start(bf16[8,8,128,128]{3,2,1,0:T(8,128)(2,1)} %get-tuple-element.57) | copy-start | bytes 6291460
  486.5 8.6 %collective-permute-start.16 = (bf16[2,128,512]{2,1,0:T(8,128)(2,1)S(1)}, bf16[2,128,512]{2,1,0:T(8,128)(2,1)S(1)}, u32[]{:S(2)}, u32[]{:S(2)}) collective-permute-start(bf16[2,128,512]{2,1,0:T(8,128)(2,1)S(1)} %dynamic-slice_bitcast_fusion.10), channel_id=1, source_target_pairs={{0,16},{4,20},{8,24},{12,28},{16,0},{20,4},{24,8},{28,12},{1,17},{... | collective-permute-start | bytes 786440 | tf_op jit(solution)/shard_map/ppermute | solution.py:744
  489.2 26.2 %copy-start.11 = (bf16[8,8,128,128]{3,2,1,0:T(8,128)(2,1)S(1)}, bf16[8,8,128,128]{3,2,1,0:T(8,128)(2,1)}, u32[]{:S(2)}) copy-start(bf16[8,8,128,128]{3,2,1,0:T(8,128)(2,1)} %get-tuple-element.56) | copy-start | bytes 6291460
  489.3 8.5 %collective-permute-start.11 = (bf16[2,128,512]{2,1,0:T(8,128)(2,1)S(1)}, bf16[2,128,512]{2,1,0:T(8,128)(2,1)S(1)}, u32[]{:S(2)}, u32[]{:S(2)}) collective-permute-start(bf16[2,128,512]{2,1,0:T(8,128)(2,1)S(1)} %dynamic-slice_bitcast_fusion.11), channel_id=1, source_target_pairs={{0,8},{4,12},{8,0},{12,4},{16,24},{20,28},{24,16},{28,20},{1,9},{5... | collective-permute-start | bytes 786440 | tf_op jit(solution)/shard_map/ppermute | solution.py:744
  495.2 5.2 collective-permute-start.17
  497.9 5.0 collective-permute-start.12
  500.5 5.9 collective-permute-start.18
  502.9 6.6 %collective-permute-start.13 = (bf16[128,512]{1,0:T(8,128)(2,1)S(1)}, bf16[128,512]{1,0:T(8,128)(2,1)S(1)}, u32[]{:S(2)}, u32[]{:S(2)}) collective-permute-start(bf16[128,512]{1,0:T(8,128)(2,1)S(1)} %fusion.32), channel_id=1, source_target_pairs={{0,1},{1,0},{2,3},{3,2},{4,5},{5,4},{6,7},{7,6},{8,9},{9,8},{10,11... | collective-permute-start | bytes 393224 | tf_op jit(solution)/shard_map/ppermute | solution.py:744
  506.4 11.5 %collective-permute-start.19 = (bf16[128,512]{1,0:T(8,128)(2,1)S(1)}, bf16[128,512]{1,0:T(8,128)(2,1)S(1)}, u32[]{:S(2)}, u32[]{:S(2)}) collective-permute-start(bf16[128,512]{1,0:T(8,128)(2,1)S(1)} %add_convert_fusion.3), channel_id=1, source_target_pairs={{0,2},{1,3},{2,0},{3,1},{4,6},{5,7},{6,4},{7,5},{8,10},{9,11},{10,... | collective-permute-start | bytes 393224 | tf_op jit(solution)/shard_map/ppermute | solution.py:744
  509.6 20.8 %collective-permute-start.14 = (bf16[128,512]{1,0:T(8,128)(2,1)S(1)}, bf16[128,512]{1,0:T(8,128)(2,1)S(1)}, u32[]{:S(2)}, u32[]{:S(2)}) collective-permute-start(bf16[128,512]{1,0:T(8,128)(2,1)S(1)} %add_convert_fusion.4), channel_id=1, source_target_pairs={{0,2},{1,3},{2,0},{3,1},{4,6},{5,7},{6,4},{7,5},{8,10},{9,11},{10,... | collective-permute-start | bytes 393224 | tf_op jit(solution)/shard_map/ppermute | solution.py:744
  514.0 10.4 %collective-permute-start.26 = (bf16[2,8,128,128]{3,2,1,0:T(8,128)(2,1)S(1)}, bf16[2,8,128,128]{3,2,1,0:T(8,128)(2,1)S(1)}, u32[]{:S(2)}, u32[]{:S(2)}) collective-permute-start(bf16[2,8,128,128]{3,2,1,0:T(8,128)(2,1)S(1)} %dynamic-slice_bitcast_fusion.2), channel_id=1, source_target_pairs={{0,16},{4,20},{8,24},{12,28},{16,0},{20,4},{24,8},{28,12},{1,17},{... | collective-permute-start | bytes 1572872 | tf_op jit(solution)/shard_map/ppermute | solution.py:744
  517.1 12.1 %collective-permute-start.21 = (bf16[2,8,128,128]{3,2,1,0:T(8,128)(2,1)S(1)}, bf16[2,8,128,128]{3,2,1,0:T(8,128)(2,1)S(1)}, u32[]{:S(2)}, u32[]{:S(2)}) collective-permute-start(bf16[2,8,128,128]{3,2,1,0:T(8,128)(2,1)S(1)} %dynamic-slice_bitcast_fusion.3), channel_id=1, source_target_pairs={{0,8},{4,12},{8,0},{12,4},{16,24},{20,28},{24,16},{28,20},{1,9},{5... | collective-permute-start | bytes 1572872 | tf_op jit(solution)/shard_map/ppermute | solution.py:744
  524.7 7.3 %collective-permute-start.27 = (bf16[8,128,128]{2,1,0:T(8,128)(2,1)S(1)}, bf16[8,128,128]{2,1,0:T(8,128)(2,1)S(1)}, u32[]{:S(2)}, u32[]{:S(2)}) collective-permute-start(bf16[8,128,128]{2,1,0:T(8,128)(2,1)S(1)} %dynamic-slice_bitcast_fusion.8), channel_id=1, source_target_pairs={{0,8},{4,12},{8,0},{12,4},{16,24},{20,28},{24,16},{28,20},{1,9},{5... | collective-permute-start | bytes 786440 | tf_op jit(solution)/shard_map/ppermute | solution.py:744
  529.4 6.4 %collective-permute-start.22 = (bf16[8,128,128]{2,1,0:T(8,128)(2,1)S(1)}, bf16[8,128,128]{2,1,0:T(8,128)(2,1)S(1)}, u32[]{:S(2)}, u32[]{:S(2)}) collective-permute-start(bf16[8,128,128]{2,1,0:T(8,128)(2,1)S(1)} %dynamic-slice_bitcast_fusion.9), channel_id=1, source_target_pairs={{0,16},{4,20},{8,24},{12,28},{16,0},{20,4},{24,8},{28,12},{1,17},{... | collective-permute-start | bytes 786440 | tf_op jit(solution)/shard_map/ppermute | solution.py:744
  532.0 9.5 %collective-permute-start.28 = (bf16[8,128,128]{2,1,0:T(8,128)(2,1)S(1)}, bf16[8,128,128]{2,1,0:T(8,128)(2,1)S(1)}, u32[]{:S(2)}, u32[]{:S(2)}) collective-permute-start(bf16[8,128,128]{2,1,0:T(8,128)(2,1)S(1)} %fusion.25), channel_id=1, source_target_pairs={{0,1},{1,0},{2,3},{3,2},{4,5},{5,4},{6,7},{7,6},{8,9},{9,8},{10,11... | collective-permute-start | bytes 786440 | tf_op jit(solution)/shard_map/ppermute | solution.py:744
  535.9 10.5 %collective-permute-start.23 = (bf16[8,128,128]{2,1,0:T(8,128)(2,1)S(1)}, bf16[8,128,128]{2,1,0:T(8,128)(2,1)S(1)}, u32[]{:S(2)}, u32[]{:S(2)}) collective-permute-start(bf16[8,128,128]{2,1,0:T(8,128)(2,1)S(1)} %fusion.26), channel_id=1, source_target_pairs={{0,1},{1,0},{2,3},{3,2},{4,5},{5,4},{6,7},{7,6},{8,9},{9,8},{10,11... | collective-permute-start | bytes 786440 | tf_op jit(solution)/shard_map/ppermute | solution.py:744
  541.6 14.4 %collective-permute-start.29 = (bf16[8,128,128]{2,1,0:T(8,128)(2,1)S(1)}, bf16[8,128,128]{2,1,0:T(8,128)(2,1)S(1)}, u32[]{:S(2)}, u32[]{:S(2)}) collective-permute-start(bf16[8,128,128]{2,1,0:T(8,128)(2,1)S(1)} %add_convert_fusion.1), channel_id=1, source_target_pairs={{0,2},{1,3},{2,0},{3,1},{4,6},{5,7},{6,4},{7,5},{8,10},{9,11},{10,... | collective-permute-start | bytes 786440 | tf_op jit(solution)/shard_map/ppermute | solution.py:744
  546.5 12.4 %collective-permute-start.24 = (bf16[8,128,128]{2,1,0:T(8,128)(2,1)S(1)}, bf16[8,128,128]{2,1,0:T(8,128)(2,1)S(1)}, u32[]{:S(2)}, u32[]{:S(2)}) collective-permute-start(bf16[8,128,128]{2,1,0:T(8,128)(2,1)S(1)} %add_convert_fusion.2), channel_id=1, source_target_pairs={{0,2},{1,3},{2,0},{3,1},{4,6},{5,7},{6,4},{7,5},{8,10},{9,11},{10,... | collective-permute-start | bytes 786440 | tf_op jit(solution)/shard_map/ppermute | solution.py:744
  559.0 3.7 copy-start.20
  563.7 5.1 copy-start.17
  567.0 9.5 %copy-start.16 = (bf16[1,8,256,256]{3,2,1,0:T(8,128)(2,1)S(1)}, bf16[1,8,256,256]{3,2,1,0:T(8,128)(2,1)}, u32[]{:S(2)}) copy-start(bf16[1,8,256,256]{3,2,1,0:T(8,128)(2,1)} %get-tuple-element.47) | copy-start | bytes 3145732
  568.9 15.1 %collective-permute-start.5 = (bf16[2,2,128,288]{3,2,1,0:T(8,128)(2,1)}, bf16[2,2,128,288]{3,2,1,0:T(8,128)(2,1)S(1)}, u32[]{:S(2)}, u32[]{:S(2)}) collective-permute-start(bf16[2,2,128,288]{3,2,1,0:T(8,128)(2,1)} %dynamic-slice_bitcast_fusion.7), channel_id=1, source_target_pairs={{0,4},{4,0},{8,12},{12,8},{16,20},{20,16},{24,28},{28,24},{1,5},{5... | collective-permute-start | bytes 884744 | tf_op jit(solution)/shard_map/ppermute | solution.py:744
  574.6 2.6 copy-start.3
  574.6 2.6 copy-start.15
  574.6 2.6 copy-start.21
  575.9 8.7 %collective-permute-start = (bf16[2,2,128,512]{3,2,1,0:T(8,128)(2,1)S(1)}, bf16[2,2,128,512]{3,2,1,0:T(8,128)(2,1)S(1)}, u32[]{:S(2)}, u32[]{:S(2)}) collective-permute-start(bf16[2,2,128,512]{3,2,1,0:T(8,128)(2,1)S(1)} %dynamic-slice_bitcast_fusion.6), channel_id=1, source_target_pairs={{0,4},{4,0},{8,12},{12,8},{16,20},{20,16},{24,28},{28,24},{1,5},{5... | collective-permute-start | bytes 1572872 | tf_op jit(solution)/shard_map/ppermute | solution.py:744
  577.2 4.0 copy-start.2
  581.3 2.7 copy-start.9
  581.3 3.2 copy-start.8
  584.0 29.2 %copy-start.13 = (bf16[512,2048]{1,0:T(8,128)(2,1)S(1)}, bf16[512,2048]{1,0:T(8,128)(2,1)}, u32[]{:S(2)}) copy-start(bf16[512,2048]{1,0:T(8,128)(2,1)} %get-tuple-element.88) | copy-start | bytes 6291460
  584.1 7.2 %collective-permute-start.6 = (bf16[2,128,288]{2,1,0:T(8,128)(2,1)S(1)}, bf16[2,128,288]{2,1,0:T(8,128)(2,1)S(1)}, u32[]{:S(2)}, u32[]{:S(2)}) collective-permute-start(bf16[2,128,288]{2,1,0:T(8,128)(2,1)S(1)} %dynamic-slice_bitcast_fusion.13), channel_id=1, source_target_pairs={{0,16},{4,20},{8,24},{12,28},{16,0},{20,4},{24,8},{28,12},{1,17},{... | collective-permute-start | bytes 442376 | tf_op jit(solution)/shard_map/ppermute | solution.py:744
  584.7 8.4 %collective-permute-start.1 = (bf16[2,128,512]{2,1,0:T(8,128)(2,1)S(1)}, bf16[2,128,512]{2,1,0:T(8,128)(2,1)S(1)}, u32[]{:S(2)}, u32[]{:S(2)}) collective-permute-start(bf16[2,128,512]{2,1,0:T(8,128)(2,1)S(1)} %dynamic-slice_bitcast_fusion.12), channel_id=1, source_target_pairs={{0,8},{4,12},{8,0},{12,4},{16,24},{20,28},{24,16},{28,20},{1,9},{5... | collective-permute-start | bytes 786440 | tf_op jit(solution)/shard_map/ppermute | solution.py:744
  591.5 4.7 collective-permute-start.7
  593.2 5.5 collective-permute-start.2
  596.2 5.3 collective-permute-start.8
  598.7 5.8 collective-permute-start.3
  601.5 9.6 %collective-permute-start.9 = (bf16[128,288]{1,0:T(8,128)(2,1)S(1)}, bf16[128,288]{1,0:T(8,128)(2,1)S(1)}, u32[]{:S(2)}, u32[]{:S(2)}) collective-permute-start(bf16[128,288]{1,0:T(8,128)(2,1)S(1)} %add_convert_fusion.6), channel_id=1, source_target_pairs={{0,2},{1,3},{2,0},{3,1},{4,6},{5,7},{6,4},{7,5},{8,10},{9,11},{10,... | collective-permute-start | bytes 221192 | tf_op jit(solution)/shard_map/ppermute | solution.py:744
  604.5 8.0 %collective-permute-start.4 = (bf16[128,512]{1,0:T(8,128)(2,1)S(1)}, bf16[128,512]{1,0:T(8,128)(2,1)S(1)}, u32[]{:S(2)}, u32[]{:S(2)}) collective-permute-start(bf16[128,512]{1,0:T(8,128)(2,1)S(1)} %add_convert_fusion.5), channel_id=1, source_target_pairs={{0,2},{1,3},{2,0},{3,1},{4,6},{5,7},{6,4},{7,5},{8,10},{9,11},{10,... | collective-permute-start | bytes 393224 | tf_op jit(solution)/shard_map/ppermute | solution.py:744

commit v4 on v3

--- a/solution.py
+++ b/solution.py
@@ -52,52 +52,6 @@
     e = jnp.exp(s - top)
     p = e / jnp.sum(e, axis=2, keepdims=True)
     return p.reshape(rows, keys)
-
-
-def attn_bwd_kernel(heads, slot_ref, span_ref, q_ref, do_ref, kd_ref, dq_ref, ds_ref):
-    m, _, c, w = ds_ref.shape
-    hd = w // 2
-    kvd = kd_ref[0]
-    kd, vd = kvd[:, :hd], kvd[:, hd:]
-    qr = to_rows(q_ref[0], heads)
-    dor = to_rows(do_ref[0], heads)
-    p = softmax_rows(qr, kd, span_ref[0], heads)
-    dp = dot_nt(dor, vd)
-    rd = jnp.sum(dp * p, axis=1, keepdims=True)
-    ds = (p * (dp - rd)).astype(bf16)
-    sc = hd ** (-0.5)
-    dq = (dot_nn(ds, kd) * sc).astype(bf16)
-    dq_ref[0] = to_cols(dq, heads)
-    dk = dot_tn(ds, qr) * sc
-    dv = dot_tn(p.astype(bf16), dor)
-    dkv = jnp.concatenate([dk, dv], axis=1).astype(bf16)
-    oh = key_onehot(slot_ref[0], m * c)
-    ds_ref[...] = dot_nn(oh, dkv).astype(bf16).reshape(ds_ref.shape)
-
-
-def attn_bwd(heads, slot, span, qpad, dopad, kd):
-    m, c, d = qpad.shape
-    length, w = kd.shape[1], kd.shape[2]
-    return pl.pallas_call(
-        lambda *refs: attn_bwd_kernel(heads, *refs),
-        grid=(m,),
-        in_specs=[
-            pl.BlockSpec((1, 1, length), lambda k: (k, 0, 0)),
-            pl.BlockSpec((1, c, 128), lambda k: (k, 0, 0)),
-            pl.BlockSpec((1, c, d), lambda k: (k, 0, 0)),
-            pl.BlockSpec((1, c, d), lambda k: (k, 0, 0)),
-            pl.BlockSpec((1, length, w), lambda k: (k, 0, 0)),
-        ],
-        out_specs=[
-            pl.BlockSpec((1, c, d), lambda k: (k, 0, 0)),
-            pl.BlockSpec((m, 1, c, w), lambda k: (0, k, 0, 0)),
-        ],
-        out_shape=[
-            jax.ShapeDtypeStruct((m, c, d), bf16),
-            jax.ShapeDtypeStruct((m, m, c, w), bf16),
-        ],
-        compiler_params=pltpu.CompilerParams(vmem_limit_bytes=VMEM_LIMIT),
-    )(slot, span, qpad, dopad, kd)
 
 
 MESH = pl.DeviceIdType.MESH
@@ -249,7 +203,7 @@
 
 FWD_IN = ("x", "dy", "small", "group", "group_t", "q_dn", "q_up", "kv_dn", "kv_up", "mix_dn", "mix_up",
           "exp_dn", "exp_up", "red_dn", "red_up", "wq", "wkv", "wmix", "wexp", "wred")
-FWD_OUT = ("dres", "put", "slot", "info", "chosen", "low0", "low1", "low2", "low4", "e3",
+FWD_OUT = ("dres", "put", "slot", "info", "chosen", "low0", "low1", "low2", "low4", "e3", "gain",
            "a", "q", "o", "m", "resid", "kd", "gup", "gdn", "layer", "kvs", "ge", "gr", "ga", "gb", "gk")
 FWD_SCRATCH = ("y", "we_v", "wr_v", "a_v", "q_v", "kvp", "kvb", "kd_st", "gup_st", "gdn_st", "sm",
                "lowr", "er", "low3", "e4",
@@ -346,6 +300,8 @@
     for part in range(2):
         serve("norm_%d" % part)
         norm_rows(r["x"], 0, 1, r["a_v"], part)
+
+    r["gain"][...] = vec(0)
 
     t_row = lax.broadcasted_iota(jnp.int32, (1, length), 1)
     before_t = lax.broadcasted_iota(jnp.int32, (length, length), 0) < lax.broadcasted_iota(
@@ -679,13 +635,13 @@
     outs = dict(
         dres=s((n, d), f32), put=s((m, z.cap, n), bf16), slot=s((m, 1, n), jnp.int32),
         info=s((m, z.cap, 128), f32), chosen=s((n, 128), f32),
-        low0=s((n, rk), bf16), low1=s((n, rk), bf16), low2=s((n, rk), bf16), low4=s((n, rk), bf16), e3=s((n, rk), bf16),
+        low0=s((n, rk), bf16), low1=s((n, rk), bf16), low2=s((n, rk), bf16), low4=s((n, rk), bf16), e3=s((n, rk), bf16), gain=s((1, d), f32),
         a=s((n, d), bf16), q=s((n, d), bf16), o=s((n, d), bf16), m=s((n, d), bf16), resid=s((n, d), f32),
         kd=s((m, n, w), bf16), gup=s((m, SLOTS, rk, z.sub), bf16), gdn=s((m, SLOTS, rk, z.sub), bf16),
         layer=s((n, d), bf16), kvs=s((m, m, z.cap, w), bf16),
         ge=s((SLOTS, m, z.rows, z.fc), bf16), gr=s((SLOTS, m, z.sub, d), bf16),
         ga=s((2, m, half, d), bf16), gb=s((2, m, half, d), bf16), gk=s((1, m, z.rows, w), bf16))
-    in_vmem = FWD_OUT[:10]
+    in_vmem = FWD_OUT[:11]
     sends = m - 1 + m // 2
     dma = pltpu.SemaphoreType.DMA
     items = 2 * SLOTS + 5
@@ -714,57 +670,328 @@
 FWD_VMEM = 62 * 1024 * 1024
 
 
-def grads_kernel(scales, *refs):
-    out = refs[-1]
-    at = 0
-    for i, sc in enumerate(scales):
-        left, right = refs[2 * i][...], refs[2 * i + 1][...]
-        owners = out.shape[0]
-        w = right.shape[1] // owners
+class Job:
+    def __init__(self, members, replicas, work, got, out, send_sem, recv_sem, turn):
+        self.me, self.rep = lax.axis_index("shard"), lax.axis_index("rep")
+        self.work, self.got, self.out = work, got, out
+        self.send_sem, self.recv_sem = send_sem, recv_sem
+        bits = [1 << i for i in range(members.bit_length() - 1)]
+        bits = bits if turn == 0 else bits[:1] + bits[1:][::-1]
+        self.stages = []
+        at, decided = 0, 0
+        for b in bits:
+            free = [f for f in range(members) if not f & (decided | b)]
+            self.stages.append((b, True, at, free, decided))
+            at += len(free)
+            decided |= b
+        b = 1
+        while b < replicas:
+            self.stages.append((b, False, at, [0], decided))
+            at += 1
+            b *= 2
+
+    def copy(self, i, n):
+        b, shard, at, free, decided = self.stages[i]
+        if shard:
+            src = self.work.at[free[n] | (self.me & decided) | ((self.me ^ b) & b)]
+            to = (self.me ^ b, self.rep)
+        else:
+            src, to = self.work.at[self.me], (self.me, self.rep ^ b)
+        return pltpu.make_async_remote_copy(
+            src, self.got.at[at + n], self.send_sem.at[at + n], self.recv_sem.at[at + n],
+            device_id=to, device_id_type=MESH)
+
+    def start(self, i):
+        for n in range(len(self.stages[i][3])):
+            self.copy(i, n).start()
+
+    def add(self, i):
+        b, shard, at, free, decided = self.stages[i]
+        for n, f in enumerate(free):
+            cp = self.copy(i, n)
+            cp.wait_recv()
+            cp.wait_send()
+            keep = f | (self.me & decided) | (self.me & b) if shard else self.me
+            total = self.work[keep].astype(f32) + self.got[at + n].astype(f32)
+            if i + 1 < len(self.stages):
+                self.work[keep] = total.astype(bf16)
+            else:
+                blocks, _, lanes = total.shape
+                for j in range(blocks):
+                    self.out[:, j * lanes : (j + 1) * lanes] = total[j]
+
+    def move(self, i):
+        self.add(i)
+        if i + 1 < len(self.stages):
+            self.start(i + 1)
+
+
+BWD_IN = ("dres", "put", "slot", "info", "chosen", "low0", "low1", "low2", "low4", "e3", "gain",
+          "mix_dn", "mix_up", "q_dn", "q_up", "kv_dn", "kv_up",
+          "ga", "gb", "gk", "q", "a", "o", "m", "dy", "x", "kd", "gup", "gdn")
+JOBS = ("ja", "jb", "jc", "jd", "je", "jf")
+BWD_OUT = ("dx",) + tuple(j + "_out" for j in JOBS)
+BWD_SCRATCH = ("w_v", "wk_v", "t1", "t2", "q_v", "do_v", "dq", "kd_st", "ds_st", "dk_r") + tuple(
+    j + s for j in JOBS for s in ("_w", "_g", "_s", "_r")) + (
+    "w_sem", "t_sem", "g_sem", "kd_sem", "dk_send", "dk_recv", "out_sem")
+
+
+def job_shapes(z):
+    wide = z.rows // min(128, z.rows)
+    lanes = min(128, z.rows)
+    chunks = (SLOTS, z.sub) if z.aligned else (SLOTS * z.sub // 128, 128)
+    return dict(ja=chunks, jb=chunks, jc=(2 * wide, lanes), jd=(2 * wide, lanes),
+                je=(2 * wide, lanes), jf=(wide + 1, lanes))
+
+
+def bwd_kernel(z, *refs):
+    r = dict(zip(BWD_IN + BWD_OUT + BWD_SCRATCH, refs))
+    members, replicas, rows, fc, d, hd = z.members, z.replicas, z.rows, z.fc, z.d, z.hd
+    length, cap, w, heads, rk = z.length, z.cap, z.w, z.heads, z.rk
+    me, rep = lax.axis_index("shard"), lax.axis_index("rep")
+    half = rows // 2
+    halves = d // fc
+    w_v, t1, t2, q_v, do_v, dq, dres = (r[k] for k in ("w_v", "t1", "t2", "q_v", "do_v", "dq", "dres"))
+    ja, jb, jc, jd, je, jf = (
+        Job(members, replicas, r[j + "_w"], r[j + "_g"], r[j + "_out"], r[j + "_s"], r[j + "_r"], i % 2)
+        for i, j in enumerate(JOBS))
+    last = len(ja.stages) - 1
+
+    barrier = pltpu.get_barrier_semaphore()
+    others = [(me ^ o, rep) for o in range(1, members)]
+    b = 1
+    while b < replicas:
+        others.append((me, rep ^ b))
+        b *= 2
+    for to in others:
+        pl.semaphore_signal(barrier, inc=1, device_id=to, device_id_type=MESH)
+
+    def local(src, dst, sem):
+        return pltpu.make_async_copy(src, dst, sem)
+
+    def wide(which):
+        return [local(r[k].at[which, :, :, c * fc : (c + 1) * fc],
+                      w_v.at[c, :, h * half : (h + 1) * half], r["w_sem"].at[h, c])
+                for h, k in enumerate(("ga", "gb")) for c in range(halves)]
+
+    load_up = local(r["gup"], r["ja_w"], r["g_sem"].at[0])
+    load_dn = local(r["gdn"], r["jb_w"], r["g_sem"].at[1])
+    load_up.start()
+    load_dn.start()
+    mix = wide(WMIX)
+    for cp in mix:
+        cp.start()
+    load_m = local(r["m"], t1, r["t_sem"].at[0])
+    load_dy = local(r["dy"], t2, r["t_sem"].at[1])
+    load_q = local(r["q"], q_v, r["t_sem"].at[2])
+    load_k = local(r["gk"].at[0], r["wk_v"], r["t_sem"].at[3])
+    for cp in (load_m, load_dy, load_q, load_k):
+        cp.start()
+    pl.semaphore_wait(barrier, len(others))
+    load_up.wait()
+    ja.start(0)
+    load_dn.wait()
+    jb.start(0)
+
+    rank_of = (lax.broadcasted_iota(jnp.int32, (length, rk), 1) // z.rank).astype(f32)
+
+    def mask(p):
+        return jnp.where(rank_of == r["chosen"][:, 2 + p : 3 + p], 1.0, 0.0)
+
+    def terms(job, block, left, right, sc):
+        lanes = job.work.shape[3]
         g = dot_tn(left, right) * sc
-        for to in range(owners):
-            out[to, :, at : at + w] = g[:, to * w : (to + 1) * w].astype(bf16)
-        at += w
-
-
-def grads(owners, pairs):
-    rk = pairs[0][0].shape[1]
-    width = sum(p[1].shape[1] for p in pairs) // owners
+        width = right.shape[1] // members
+        for to in range(members):
+            for i in range(-(-width // lanes)):
+                part = g[:, to * width + i * lanes : to * width + min((i + 1) * lanes, width)]
+                if part.shape[1] < lanes:
+                    part = jnp.concatenate([part, jnp.zeros((rk, lanes - part.shape[1]), f32)], axis=1)
+                job.work[to, block + i] = part.astype(bf16)
+
+    per = r["jc_w"].shape[1] // 2
+
+    dresl = do_v
+    dresl[...] = dres[...].astype(bf16)
+    e2 = (scale_lora * dot_nt(dresl[...], r["mix_up"][...]) * mask(2)).astype(bf16)
+    terms(jd, per, r["low2"][...], dresl[...], scale_lora)
+    load_m.wait()
+    terms(jc, 0, r["e3"][...], t1[...], 1.0)
+    load_o = local(r["o"], t1, r["t_sem"].at[0])
+    load_o.start()
+    load_dy.wait()
+    terms(jd, 0, r["low4"][...], t2[...], scale_lora)
+    load_x = local(r["x"], t2, r["t_sem"].at[1])
+    load_x.start()
+    jd.start(0)
+    for cp in mix:
+        cp.wait()
+    ja.move(0)
+    dq[...] = dot_nt(dresl[:, 0:fc], w_v[0].reshape(d, fc)) + dot_nn(e2, r["mix_dn"][...])
+    jb.move(0)
+    for c in range(1, halves):
+        dq[...] += dot_nt(dresl[:, c * fc : (c + 1) * fc], w_v[c].reshape(d, fc))
+    do_v[...] = dq[...].astype(bf16)
+    query = wide(WQ)
+    for cp in query:
+        cp.start()
+    load_o.wait()
+    terms(jc, per, e2, t1[...], 1.0)
+    jc.start(0)
+    load_a = local(r["a"], t1, r["t_sem"].at[0])
+    load_a.start()
+    jd.move(0)
+    dq[...] = jnp.zeros_like(dq)
+    load_q.wait()
+
+    def kd_load(k, buf):
+        return local(r["kd"].at[k], r["kd_st"].at[buf], r["kd_sem"].at[buf])
+
+    def ds_copy(k, buf, o):
+        return pltpu.make_async_remote_copy(
+            r["ds_st"].at[buf, me ^ o], r["dk_r"].at[me, k], r["dk_send"].at[buf, o], r["dk_recv"].at[o],
+            device_id=(me ^ o, rep), device_id_type=MESH)
+
+    kd_load(0, 0).start()
+    groups = 4
+    sc = hd ** (-0.5)
+    acts = {0: lambda: jc.move(0), 1: lambda: ja.move(1), 2: lambda: (jb.move(1), jd.move(1))[0], 3: lambda: (ja.move(2), jc.move(1))[0],
+            4: lambda: (jb.move(2), jd.move(2))[0], 5: lambda: (ja.move(3), jc.move(2))[0],
+            6: lambda: (jb.move(3), jd.move(3))[0], 7: lambda: jc.move(3)}
+
+    def attend(k, _):
+        buf = lax.rem(k, 2)
+
+        @pl.when(k + 1 < members)
+        def _():
+            kd_load(k + 1, 1 - buf).start()
+
+        for i, act in acts.items():
+            pl.when(k == i)(act)
+        kd_load(k, buf).wait()
+        kvd = r["kd_st"][buf]
+        kd, vd = kvd[:, :hd], kvd[:, hd:]
+        put = r["put"][k]
+        qp = dot_nn(put, q_v[...]).astype(bf16)
+        dop = dot_nn(put, do_v[...]).astype(bf16)
+        info = r["info"][k]
+        n = heads // groups
+        dqs = []
+        dk = jnp.zeros((length, hd), f32)
+        dv = jnp.zeros((length, hd), f32)
+        for h in range(groups):
+            at = slice(h * n * hd, (h + 1) * n * hd)
+            qr, dor = to_rows(qp[:, at], n), to_rows(dop[:, at], n)
+            p = softmax_rows(qr, kd, info, n)
+            dp = dot_nt(dor, vd)
+            ds = (p * (dp - jnp.sum(dp * p, axis=1, keepdims=True))).astype(bf16)
+            dqs.append(to_cols((dot_nn(ds, kd) * sc).astype(bf16), n))
+            dk = dk + dot_tn(ds, qr)
+            dv = dv + dot_tn(p.astype(bf16), dor)
+        dq[...] += dot_tn(put, jnp.concatenate(dqs, axis=1))
+        dkv = jnp.concatenate([dk * sc, dv], axis=1).astype(bf16)
+        slots = dot_nn(key_onehot(r["slot"][k], z.slots), dkv).astype(bf16).reshape(members, cap, w)
+
+        @pl.when(k >= 2)
+        def _():
+            for o in range(1, members):
+                ds_copy(k, buf, o).wait_send()
+
+        r["ds_st"][buf] = slots
+        r["dk_r"][me, k] = r["ds_st"][buf, me]
+        for o in range(1, members):
+            ds_copy(k, buf, o).start()
+        return 0
+
+    lax.fori_loop(0, members, attend, 0)
+
+    q_v[...] = dq[...].astype(bf16)
+    e0 = (scale_lora * dot_nt(q_v[...], r["q_up"][...]) * mask(0)).astype(bf16)
+    load_a.wait()
+    terms(je, 0, e0, t1[...], 1.0)
+    terms(jf, 0, r["low0"][...], q_v[...], scale_lora)
+    for o in range(1, members):
+        local(r["dk_r"].at[me ^ o], r["dk_r"].at[me ^ o], r["dk_recv"].at[o]).wait()
+    dkv = jnp.zeros((length, w), f32)
+    for k in range(members):
+        total = r["dk_r"][0, k].astype(f32)
+        for s in range(1, members):
+            total = total + r["dk_r"][s, k].astype(f32)
+        dkv = dkv + dot_tn(r["put"][k], total.astype(bf16))
+    dkv = dkv.astype(bf16)
+    e1 = (scale_lora * dot_nt(dkv, r["kv_up"][...]) * mask(1)).astype(bf16)
+    terms(je, per, e1, t1[...], 1.0)
+    terms(jf, per, r["low1"][...], dkv, scale_lora)
+    je.start(0)
+    jf.start(0)
+    load_k.wait()
+    dq[...] = (dot_nn(e0, r["q_dn"][...]) + dot_nn(e1, r["kv_dn"][...])
+               + dot_nt(dkv, r["wk_v"][...].reshape(d, w)))
+    je.move(0)
+    jf.move(0)
+    for cp in query:
+        cp.wait()
+    for c in range(halves):
+        dq[...] += dot_nt(q_v[:, c * fc : (c + 1) * fc], w_v[c].reshape(d, fc))
+    load_x.wait()
+    gain = r["gain"][...]
+
+    def back(i, _):
+        at = pl.ds(pl.multiple_of(i * 128, 128), 128)
+        n, inv = norm_parts(t2[at, :].astype(f32))
+        do_v[at, :] = (dres[at, :] + norm_back(n, inv, gain, dq[at, :])).astype(bf16)
+        return 0
+
+    je.move(1)
+    jf.move(1)
+    lax.fori_loop(0, length // 128, back, 0)
+    out = local(do_v, r["dx"], r["out_sem"])
+    out.start()
+    for i in range(2, last + 1):
+        for job in (je, jf):
+            job.move(i)
+    for job in (ja, jb, jc, jd):
+        for i in range(4, last + 1):
+            job.move(i)
+    out.wait()
+    for buf in range(2):
+        for o in range(1, members):
+            ds_copy(buf, buf, o).wait_send()
+
+
+def backward(z, args):
     vm = pl.BlockSpec(memory_space=pltpu.VMEM)
-    return pl.pallas_call(
-        lambda *refs: grads_kernel([p[2] for p in pairs], *refs),
-        in_specs=[vm] * (2 * len(pairs)),
-        out_specs=vm,
-        out_shape=jax.ShapeDtypeStruct((owners, rk, width), bf16),
-        compiler_params=pltpu.CompilerParams(vmem_limit_bytes=VMEM_LIMIT),
-    )(*[x for p in pairs for x in p[:2]])
-
-
-def exchange(v, axis, bit):
-    return lax.ppermute(v, axis, [(i, i ^ bit) for i in range(lax.axis_size(axis))])
-
-
-def reduce_share(parts, turn):
-    me = lax.axis_index("shard")
-    count = parts.shape[0].bit_length() - 1
-    left = list(range(count))[::-1]
-    cur = parts.reshape((2,) * count + parts.shape[1:])
-    order = [0] + (list(range(1, count)) if turn == 0 else list(range(1, count))[::-1])
-    for i, bit in enumerate(order):
-        pos = left.index(bit)
-        mine = (me >> bit) & 1
-        send = lax.dynamic_index_in_dim(cur, 1 - mine, pos, keepdims=False)
-        keep = lax.dynamic_index_in_dim(cur, mine, pos, keepdims=False)
-        cur = keep.astype(f32) + exchange(send, "shard", 1 << bit).astype(f32)
-        left.remove(bit)
-        if i + 1 < count:
-            cur = cur.astype(bf16)
-    bit = 1
-    while bit < lax.axis_size("rep"):
-        low = cur.astype(bf16)
-        cur = low.astype(f32) + exchange(low, "rep", bit).astype(f32)
-        bit *= 2
-    return cur
+    hbm = pl.BlockSpec(memory_space=pl.ANY)
+    m, n, d, rk, w = z.members, z.length, z.d, z.rk, z.w
+    s = jax.ShapeDtypeStruct
+    dma = pltpu.SemaphoreType.DMA
+    shapes = job_shapes(z)
+    legs = m - 1 + z.replicas.bit_length() - 1
+    outs = dict(dx=s((n, d), bf16))
+    scratch = dict(
+        w_v=pltpu.VMEM((d // z.fc, m, z.rows, z.fc), bf16), wk_v=pltpu.VMEM((m, z.rows, w), bf16),
+        t1=pltpu.VMEM((n, d), bf16), t2=pltpu.VMEM((n, d), bf16), q_v=pltpu.VMEM((n, d), bf16), do_v=pltpu.VMEM((n, d), bf16),
+        dq=pltpu.VMEM((n, d), f32), kd_st=pltpu.VMEM((2, n, w), bf16), ds_st=pltpu.VMEM((2, m, z.cap, w), bf16),
+        dk_r=pltpu.VMEM((m, m, z.cap, w), bf16),
+        w_sem=dma((2, d // z.fc)), t_sem=dma((4,)), g_sem=dma((2,)), kd_sem=dma((2,)), dk_send=dma((2, m)),
+        dk_recv=dma((m,)), out_sem=dma(()))
+    for j, (blocks, lanes) in shapes.items():
+        outs[j + "_out"] = s((rk, blocks * lanes), f32)
+        scratch[j + "_w"] = pltpu.VMEM((m, blocks, rk, lanes), bf16)
+        scratch[j + "_g"] = pltpu.VMEM((legs, blocks, rk, lanes), bf16)
+        scratch[j + "_s"] = dma((legs,))
+        scratch[j + "_r"] = dma((legs,))
+    first_hbm = BWD_IN.index("ga")
+    got = pl.pallas_call(
+        lambda *refs: bwd_kernel(z, *refs),
+        in_specs=[vm] * first_hbm + [hbm] * (len(BWD_IN) - first_hbm),
+        out_specs=[hbm] + [vm] * len(JOBS),
+        out_shape=[outs[k] for k in BWD_OUT],
+        scratch_shapes=[scratch[k] for k in BWD_SCRATCH],
+        compiler_params=pltpu.CompilerParams(
+            vmem_limit_bytes=FWD_VMEM, collective_id=2, has_side_effects=True),
+    )(*[args[k] for k in BWD_IN])
+    return dict(zip(BWD_OUT, got))
 
 
 def local(tokens, out_grad, token_perm, seq_lens, adapter_ids,
@@ -800,47 +1027,23 @@
         q_dn=q_dn, q_up=q_up, kv_dn=kv_dn, kv_up=kv_up, mix_dn=mix_dn, mix_up=mix_up, exp_dn=exp_dn,
         exp_up=chunked(exp_up), red_dn=chunked(red_dn), red_up=red_up,
         wq=wq, wkv=wkv, wmix=wmix, wexp=chunked(wexp), wred=wred.reshape(SLOTS, z.sub, d)))
-    r_exp_up = reduce_share(got["gup"], 0)
-    r_red_dn = reduce_share(got["gdn"], 1)
-    wq_f, wmix_f = (jnp.stack([got["ga"][i], got["gb"][i]], axis=1).reshape(d, d) for i in (WQ, WMIX))
-    wkv_f = got["gk"].reshape(d, z.w)
-    attn_gain = lax.all_gather(attn_g, "shard", axis=0, tiled=True).astype(f32)
-    owner = jnp.arange(rk, dtype=jnp.int32) // rank
-    masks = [(owner[None, :].astype(f32) == got["chosen"][:, 2 + p : 3 + p]).astype(f32) for p in range(3)]
-    put = got["put"].reshape(z.slots, length)
-    low0, low1, low2, low4, e3 = (got[k] for k in ("low0", "low1", "low2", "low4", "e3"))
-    a, o, m, dres, layer_out = (got[k] for k in ("a", "o", "m", "dres", "layer"))
-    x = tokens.astype(f32)
-    nx, inv_x = norm_parts(x)
-    qpad = dot_nn(put, got["q"]).astype(bf16).reshape(members, z.cap, d)
+    if not z.aligned:
+        pack = 128 // z.sub
+        for k in ("gup", "gdn"):
+            got[k] = got[k].reshape(members, SLOTS // pack, pack, rk, z.sub).transpose(0, 1, 3, 2, 4).reshape(
+                members, SLOTS // pack, rk, 128)
+    back = backward(z, dict(
+        got, mix_dn=mix_dn, mix_up=mix_up, q_dn=q_dn, q_up=q_up, kv_dn=kv_dn, kv_up=kv_up, dy=out_grad, x=tokens))
+    c = d // members
+    outs = [back[j + "_out"] for j in JOBS]
 
     def stack(g):
         return g.reshape(experts, rank, g.shape[1])
 
-    def stack_chunks(g):
-        return stack(g.transpose(1, 0, 2).reshape(rk, SLOTS * z.sub))
-
-    dresl = dres.astype(bf16)
-    e2 = (scale_lora * dot_nt(dresl, mix_up) * masks[2]).astype(bf16)
-    do = (dot_nt(dresl, wmix_f) + dot_nn(e2, mix_dn)).astype(bf16)
-    r_down = reduce_share(grads(members, [(e3, m, 1.0), (e2, o, 1.0)]), 0)
-    r_up = reduce_share(grads(members, [(low4, out_grad, scale_lora), (low2, dresl, scale_lora)]), 1)
-    dopad = dot_nn(put, do).astype(bf16).reshape(members, z.cap, d)
-    dqpad, dslots = attn_bwd(z.heads, got["slot"], got["info"], qpad, dopad, got["kd"])
-    back = lax.all_to_all(dslots, "shard", split_axis=0, concat_axis=0, tiled=True)
-    dkvp = jnp.sum(back.astype(f32), axis=0).astype(bf16).reshape(z.slots, z.w)
-    dq = dot_tn(put, dqpad.reshape(z.slots, d)).astype(bf16)
-    dkv = dot_tn(put, dkvp).astype(bf16)
-    e0 = (scale_lora * dot_nt(dq, q_up) * masks[0]).astype(bf16)
-    e1 = (scale_lora * dot_nt(dkv, kv_up) * masks[1]).astype(bf16)
-    da = (dot_nt(dq, wq_f) + dot_nn(e0, q_dn)) + (dot_nt(dkv, wkv_f) + dot_nn(e1, kv_dn))
-    tokens_grad = (dres + norm_back(nx, inv_x, attn_gain, da)).astype(bf16)
-    r_qkv_down = reduce_share(grads(members, [(e0, a, 1.0), (e1, a, 1.0)]), 0)
-    r_qkv_up = reduce_share(grads(members, [(low0, dq, scale_lora), (low1, dkv, scale_lora)]), 1)
-    c = d // members
-    return (layer_out, tokens_grad, stack(r_qkv_down[:, :c]), stack(r_qkv_up[:, :c]), stack(r_qkv_down[:, c:]),
-            stack(r_qkv_up[:, c:]), stack(r_down[:, c:]), stack(r_up[:, c:]), stack(r_down[:, :c]),
-            stack_chunks(r_exp_up), stack_chunks(r_red_dn), stack(r_up[:, :c]))
+    g_exp_up, g_red_dn, one, two, three, four = outs
+    return (got["layer"], back["dx"], stack(three[:, :c]), stack(four[:, :c]), stack(three[:, c:]),
+            stack(four[:, c : c + z.w // members]), stack(one[:, c:]), stack(two[:, c:]), stack(one[:, :c]),
+            stack(g_exp_up), stack(g_red_dn), stack(two[:, :c]))
 
 
 def solution(mesh):

time: 624 us -> 479 us (0.77)
  Pallas kernels: 374 us -> 446 us
  waiting for transfers between devices: 67.7 us -> 0 us
  matrix products: 45.4 us -> 0 us
  local copies, waits for them, and re-layouts: 56 us -> 20.8 us
  starting transfers between devices: 29.3 us -> 0 us
  other arithmetic: 31 us -> 2.1 us
  blocking collectives: 9.66 us -> 0 us
    pallas_call x5 -> x1, Pallas kernels: 48.2 us -> 120 us  [backward(): pl.pallas_call(lambda *refs: bwd_kernel(z, *refs), in_specs=[vm] * first_...]
    ppermute x30 -> x0, waiting for transfers between devices: 67.7 us -> none  [exchange(): lax.ppermute(v, axis, [(i, i ^ bit) for i in range(lax.axis_size(axis))])]
    dot_general x12 -> x0, matrix products: 45.4 us -> none  [the longest x6 23.9 us: dot_nt(): lax.dot_general(a, b, (((1,), (1,)), ((), ())), preferred_element_type=f32)]
    another operation x5 -> x0, local copies, waits for them, and re-layouts: 29.6 us -> none  [the longest x3 27.9 us: local(): jnp.stack([got['ga'][i], got['gb'][i]], axis=1).reshape(d, d)]
    ppermute x30 -> x0, starting transfers between devices: 24.3 us -> none  [exchange(): lax.ppermute(v, axis, [(i, i ^ bit) for i in range(lax.axis_size(axis))])]
    another operation x2 -> x0, other arithmetic: 13.8 us -> none  [local(): jnp.stack([got['ga'][i], got['gb'][i]], axis=1).reshape(d, d)]
    squeeze x18 -> x0, local copies, waits for them, and re-layouts: 12 us -> none  [reduce_share(): send = lax.dynamic_index_in_dim(cur, 1 - mine, pos, keepdims=False)]
    convert_element_type x28 -> x0, other arithmetic: 11.4 us -> none  [the longest x12 6.56 us: reduce_share(): cur = cur.astype(bf16)]
  transfers between devices with their start and end apart: 31 -> 0, of which waited for: 21 -> 0; matrix products, arithmetic and copies ran while one was open for 18% -> 0% of each run, Pallas kernels for 7% -> 0%
where the time goes in v4:
time: 479 us; the launch traced here: 470 us
  Pallas kernels  446 us (93%)
  local copies, waits for them, and re-layouts  20.8 us (4%)
    pallas_call x1, Pallas kernels, forward(): pl.pallas_call(lambda *refs: fwd_kernel(z, *refs), in_specs=[hbm if k.sta...  326 us
    pallas_call x1, Pallas kernels, backward(): pl.pallas_call(lambda *refs: bwd_kernel(z, *refs), in_specs=[vm] * first_...  120 us

profile of v4, /device:TPU:0, one launch (start us, length us, event | category | flops | bytes accessed | tf_op | source)
XLA Modules:
  0.0 470.0 jit_solution(3708007090280642112)
XLA Ops:
  0.6 0.8 concatenate.23
  1.4 0.7 add_convert_fusion
  2.1 0.1 pad.13.clone
  2.2 0.7 broadcast_in_dim.26
  2.9 0.7 broadcast_in_dim.27
  3.5 0.7 broadcast_in_dim.28
  4.2 0.7 pad.9
  4.9 0.7 broadcast_in_dim.29
  5.5 0.7 broadcast_in_dim.30
  6.2 0.7 broadcast_in_dim.31
  6.8 0.7 broadcast_in_dim.32
  7.5 0.7 maximum_convert_fusion
  8.2 0.7 fusion.refs_2_
  8.9 0.9 reshape.126
  9.8 0.0 copy-start.3
  9.8 0.8 copy.41
  10.6 0.0 copy-done.3
  10.6 326.1 %shard_map.364 = (f32[512,2048]{1,0:T(8,128)}, bf16[8,96,512]{2,1,0:T(8,128)(2,1)}, s32[8,1,512]{2,1,0:T(1,128)}, f32[8,96,128]{2,1,0:T(8,128)}, f32[512,128]{1,...) custom-call(bf16[512,2048]{1,0:T(8,128)(2,1)} %refs_25_.1, ...), custom_call_target="tpu_custom_call" | custom-call | tf_op jit(solution)/shard_map/pallas_call | solution.py:658
  336.7 120.0 %shard_map.365 = (bf16[512,2048]{1,0:T(8,128)(2,1)}, f32[128,1024]{1,0:T(8,128)}, f32[128,1024]{1,0:T(8,128)}, f32[128,512]{1,0:T(8,128)}, f32[128,512]{1,0:T(8,...) custom-call(f32[512,2048]{1,0:T(8,128)} %get-tuple-element.42.refs_0_, bf16[8,96,512]{2,1,0:T(8,128)(2,1)} %get-tuple-element.43.refs_1_, ...), custom_call_target="tpu_custom_call" | custom-call | tf_op jit(solution)/shard_map/pallas_call | solution.py:985
  456.8 1.5 slice.27
  458.2 1.6 slice.25
  459.8 1.7 fusion.4
  461.5 1.9 fusion.2
  463.4 0.0 copy-start
  463.4 3.3 copy.46
  466.7 0.0 copy-done
  466.7 0.0 copy-start.2
  466.7 0.0 copy-start.1
  466.7 1.3 copy.47
  468.0 0.1 copy-done.2
  468.1 0.8 copy.48
  468.9 0.0 copy-done.1
  468.9 0.8 copy.49
  (3 shorter events, 0.1 us)
Async XLA Ops:
  9.8 0.9 copy-start.3
  463.4 3.3 copy-start
  466.7 1.4 copy-start.2
  466.7 2.2 copy-start.1

commit v5 on v4

v5 whole, which is shorter than its diff:
```python
import jax
import jax.numpy as jnp
from jax import lax
from jax.experimental import pallas as pl
from jax.experimental.pallas import tpu as pltpu
from jax.sharding import PartitionSpec as P
from typing import NamedTuple

scale_lora = 0.5
eps = 1e-05
f32 = jnp.float32
bf16 = jnp.bfloat16
neg_big = -1e30
log2_e = 1.4426950408889634
gelu_c = 0.7978845608028654
VMEM_LIMIT = 60 * 1024 * 1024


def dot_nn(a, b):
    return lax.dot_general(a, b, (((1,), (0,)), ((), ())), preferred_element_type=f32)


def dot_nt(a, b):
    return lax.dot_general(a, b, (((1,), (1,)), ((), ())), preferred_element_type=f32)


def dot_tn(a, b):
    return lax.dot_general(a, b, (((0,), (0,)), ((), ())), preferred_element_type=f32)


def key_onehot(slot_row, slots):
    ids = lax.broadcasted_iota(jnp.int32, (slots, slot_row.shape[1]), 0)
    return jnp.where(ids == slot_row, 1.0, 0.0).astype(bf16)


def to_rows(x, heads):
    hd = x.shape[1] // heads
    return jnp.concatenate([x[:, h * hd : (h + 1) * hd] for h in range(heads)], axis=0)


def to_cols(x, heads):
    c = x.shape[0] // heads
    return jnp.concatenate([x[h * c : (h + 1) * c] for h in range(heads)], axis=1)


def softmax_rows(qr, kd, span, heads):
    rows, keys = qr.shape[0], kd.shape[0]
    c = rows // heads
    u = lax.broadcasted_iota(jnp.int32, (c, keys), 1).astype(f32)
    allowed = (u >= span[:, 0:1]) & (u <= span[:, 1:2])
    s = jnp.where(allowed[None], dot_nt(qr, kd).reshape(heads, c, keys), neg_big)
    top = jnp.max(s, axis=2, keepdims=True)
    e = jnp.exp2((s - top) * (kd.shape[1] ** (-0.5) * log2_e))
    p = e * (1.0 / jnp.sum(e, axis=2, keepdims=True))
    return p.reshape(rows, keys)


MESH = pl.DeviceIdType.MESH


class Gather:
    def __init__(self, members, own, full, slots, send_sem, recv_sem):
        self.members = members
        self.me, self.rep = lax.axis_index("shard"), lax.axis_index("rep")
        self.own, self.full = own, full
        self.base = [sum(slots[:i]) for i in range(len(slots))]
        self.send_sem, self.recv_sem = send_sem, recv_sem
        self.bits = [1 << i for i in range(1, members.bit_length() - 1)]
        self.planes = list(range(0, members, 2))
        self.sent = {}

    def place(self, kind, slot, offset):
        return self.full[kind].at[slot, self.me ^ offset]

    def copy(self, kind, slot, offset, there, to, to_slot):
        mine = self.sent.setdefault((kind, slot), {})
        at = mine.setdefault((offset, there, to_slot), len(mine))
        src = self.own[kind](slot) if offset == 0 else self.place(kind, slot, offset)
        pltpu.make_async_remote_copy(
            src, self.full[kind].at[to_slot, self.me ^ offset],
            self.send_sem.at[self.base[kind] + slot, at],
            self.recv_sem.at[self.base[kind] + to_slot, there],
            device_id=to, device_id_type=MESH).start()

    def wait(self, kind, slot, offset):
        piece = self.place(kind, slot, offset)
        pltpu.make_async_copy(piece, piece, self.recv_sem.at[self.base[kind] + slot, offset]).wait()

    def order(self, kind):
        return self.bits if kind % 2 == 0 else self.bits[::-1]

    def stage(self, kind, offset):
        return max(i for i, b in enumerate(self.order(kind)) if offset & b)

    def issue(self, slot, kinds, plane=True):
        for kind in kinds:
            if plane:
                for b in self.order(kind):
                    self.copy(kind, slot, 0, b, (self.me ^ b, self.rep), slot)
            self.copy(kind, slot, 0, 1, (self.me ^ 1, self.rep), slot)

    def arrive(self, slot, kinds, direct, swap_to=None):
        for kind in kinds:
            order = self.order(kind)
            some = [o for o in self.planes if o and (bin(o).count("1") == 1) == direct]
            some.sort(key=lambda o: self.stage(kind, o))
            for o in some:
                self.wait(kind, slot, o)
                for i in range(self.stage(kind, o) + 1, len(order)):
                    self.copy(kind, slot, o, o ^ order[i], (self.me ^ order[i], self.rep), slot)
                if swap_to is not None:
                    self.copy(kind, slot, o, o, (self.me, self.rep ^ 1), swap_to)
                self.copy(kind, slot, o, o ^ 1, (self.me ^ 1, self.rep), slot)

    def swapped(self, slot, kinds):
        for kind in kinds:
            for o in self.planes[1:]:
                self.wait(kind, slot, o)
                self.copy(kind, slot, o, o ^ 1, (self.me ^ 1, self.rep), slot)

    def ready(self, slot, kinds):
        for kind in kinds:
            for o in range(1, self.members, 2):
                self.wait(kind, slot, o)

    def finish(self):
        for (kind, slot), mine in self.sent.items():
            piece = self.place(kind, slot, 0)
            for at in mine.values():
                pltpu.make_async_copy(piece, piece, self.send_sem.at[self.base[kind] + slot, at]).wait()


U, V, C = (0, 1, 2), (3, 4, 5), (6, 7)
SLOTS = 8
WE, WR, AT, AB, KV = range(5)
BOTH, HALVES = (WE, WR), (AT, AB)
WQ, WMIX = 0, 1
SEND, NEAR, FAR, SWAP = range(4)
MLP_ORDER = (0, 1, 4, 3, 2, 6, 5, 7)
SERVE = {
    0: ((SEND, KV, 0),),
    1: ((SEND, WR, 0),),
    10: ((NEAR, KV, 0),),
    21: ((SEND, WE, 0),),
    24: ((NEAR, WR, 0),),
    25: ((FAR, KV, 0),),
    2: ((SEND, AT, 0),),
    4: ((NEAR, WE, 0),),
    5: ((FAR, WR, 0), (NEAR, AT, 0), (SEND, AB, 0), (FAR, WE, 0), (SEND, WE, 1), (SWAP, WR, 3), (FAR, AT, 0), (SEND, AB, 1), (SWAP, WE, 3), (NEAR, AB, 0), (NEAR, WE, 1), (SEND, AT, 1), (FAR, AB, 0),),
    15: ((NEAR, AB, 1),),
    41: ((FAR, WE, 1), (SEND, WR, 1),),
    43: ((FAR, AB, 1),),
    44: ((NEAR, AT, 1), (SEND, WE, 2), (SWAP, WE, 4),),
    46: ((NEAR, WR, 1),),
    7: ((FAR, AT, 1),),
    16: ((SEND, WR, 2),),
    17: ((FAR, WR, 1),),
    12: ((NEAR, WE, 2),),
    13: ((SEND, WR, 6),),
    60: ((NEAR, WR, 2),),
    61: ((SWAP, WR, 4),),
    62: ((FAR, WE, 2), (SEND, WE, 6),),
    63: ((FAR, WR, 2),),
    64: ((NEAR, WR, 6), (SEND, WE, 7),),
    66: ((NEAR, WE, 6),),
    67: ((FAR, WR, 6), (SEND, WR, 7),),
    69: ((NEAR, WE, 7), (FAR, WE, 6), (SWAP, WE, 5),),
    70: ((NEAR, WR, 7), (SWAP, WR, 5),),
    72: ((FAR, WE, 7), (FAR, WR, 7),),
}


def chunk_of(slot, parity):
    slot = jnp.int32(slot)
    low = jnp.where(slot < 3, slot, slot + 2)
    high = jnp.where(slot < 3, slot + 5, slot - 3)
    return jnp.where(slot >= 6, slot - 3, jnp.where(parity == 0, low, high))


def norm_parts(v):
    center = v - jnp.mean(v, axis=-1, keepdims=True)
    inv = lax.rsqrt(jnp.mean(center * center, axis=-1, keepdims=True) + eps)
    return center * inv, inv


def norm_back(n, inv, gain, dn):
    w = gain * dn
    return (w - jnp.mean(w, axis=-1, keepdims=True)
            - n * jnp.mean(w * n, axis=-1, keepdims=True)) * inv


class Sizes:
    def __init__(self, members, replicas, length, d, ff, hd, rk, rank, seqs, projs):
        self.members, self.replicas, self.length, self.d, self.ff = members, replicas, length, d, ff
        self.hd, self.rk, self.rank, self.seqs, self.projs = hd, rk, rank, seqs, projs
        self.heads = d // hd
        self.cap = 3 * length // (2 * members)
        self.slots = members * self.cap
        self.w = 2 * hd
        self.rows = d // members
        self.sub = ff // members // SLOTS
        self.fc = self.sub * members
        self.aligned = self.sub % 128 == 0
        self.be_at = 7 * self.rows
        self.vb_at = self.be_at + ff // members
        self.len_at = self.vb_at + hd // members
        self.ids_at = self.len_at + seqs
        self.small_cols = -(-(self.ids_at + seqs * projs) // 128) * 128


class FwdIn(NamedTuple):
    x: object
    small: object
    group: object
    q_dn: object
    q_up: object
    kv_dn: object
    kv_up: object
    dy: object
    mix_dn: object
    mix_up: object
    exp_dn: object
    exp_up: object
    red_dn: object
    red_up: object
    wq: object
    wkv: object
    wmix: object
    wexp: object
    wred: object


class FwdOut(NamedTuple):
    dres: object
    put: object
    slot: object
    info: object
    chosen: object
    low0: object
    low1: object
    low2: object
    low4: object
    e3: object
    gain: object
    a: object
    q: object
    o: object
    m: object
    resid: object
    kd: object
    gup: object
    gdn: object
    layer: object
    kvs: object
    ge: object
    gr: object
    ga: object
    gb: object
    gk: object


class FwdScratch(NamedTuple):
    y: object
    dy_v: object
    mix_dn_v: object
    mix_up_v: object
    exp_dn_v: object
    exp_up_v: object
    red_dn_v: object
    red_up_v: object
    late_sem: object
    we_v: object
    wr_v: object
    a_v: object
    q_v: object
    kvp: object
    kvb: object
    kd_st: object
    gup_st: object
    gdn_st: object
    sm: object
    lowr: object
    er: object
    low3: object
    e4: object
    send_sem: object
    recv_sem: object
    sm_send: object
    sm_recv: object
    kv_send: object
    kv_recv: object
    stage_sem: object
    store_sem: object
    load_sem: object
    kvb_sem: object
    kd_sem: object
    g_sem: object
    out_sem: object


class FwdRefs(NamedTuple):
    x: object
    small: object
    group: object
    q_dn: object
    q_up: object
    kv_dn: object
    kv_up: object
    dy: object
    mix_dn: object
    mix_up: object
    exp_dn: object
    exp_up: object
    red_dn: object
    red_up: object
    wq: object
    wkv: object
    wmix: object
    wexp: object
    wred: object
    dres: object
    put: object
    slot: object
    info: object
    chosen: object
    low0: object
    low1: object
    low2: object
    low4: object
    e3: object
    gain: object
    a: object
    q: object
    o: object
    m: object
    resid: object
    kd: object
    gup: object
    gdn: object
    layer: object
    kvs: object
    ge: object
    gr: object
    ga: object
    gb: object
    gk: object
    y: object
    dy_v: object
    mix_dn_v: object
    mix_up_v: object
    exp_dn_v: object
    exp_up_v: object
    red_dn_v: object
    red_up_v: object
    late_sem: object
    we_v: object
    wr_v: object
    a_v: object
    q_v: object
    kvp: object
    kvb: object
    kd_st: object
    gup_st: object
    gdn_st: object
    sm: object
    lowr: object
    er: object
    low3: object
    e4: object
    send_sem: object
    recv_sem: object
    sm_send: object
    sm_recv: object
    kv_send: object
    kv_recv: object
    stage_sem: object
    store_sem: object
    load_sem: object
    kvb_sem: object
    kd_sem: object
    g_sem: object
    out_sem: object


def fwd_kernel(z, *refs):
    r = FwdRefs(*refs)
    members, rows, fc, sub, d, hd = z.members, z.rows, z.fc, z.sub, z.d, z.hd
    length, cap, w, heads, rk = z.length, z.cap, z.w, z.heads, z.rk
    me, rep = lax.axis_index("shard"), lax.axis_index("rep")
    parity = lax.rem(rep, 2)
    half = rows // 2
    att = (r.wq, r.wmix)
    g = Gather(
        members,
        [lambda s: r.ge.at[s, me],
         lambda s: r.wred.at[chunk_of(s, parity)],
         lambda s: att[s].at[0:half],
         lambda s: att[s].at[half:rows],
         lambda s: r.wkv],
        [r.ge, r.gr, r.ga, r.gb, r.gk],
        [SLOTS, SLOTS, 2, 2, 1], r.send_sem, r.recv_sem)
    we_v, wr_v, sm, y, dm = r.we_v, r.wr_v, r.sm, r.y, r.dres

    def serve(point):
        for op, kind, slot in SERVE.get(point, ()):
            swap_to = slot + 3 if slot in U and kind in BOTH else None
            if op == SEND:
                g.issue(slot, (kind,))
            elif op == SWAP:
                g.swapped(slot, (kind,))
            else:
                g.arrive(slot, (kind,), op == NEAR, swap_to)

    barrier = pltpu.get_barrier_semaphore()
    others = [(me ^ o, rep) for o in range(1, members)] + [(me, rep ^ 1)]
    for to in others:
        pl.semaphore_signal(barrier, inc=1, device_id=to, device_id_type=MESH)

    def stage_copies(slot):
        j = chunk_of(slot, parity)
        to = we_v.at[0, slot]
        if not z.aligned:
            return [pltpu.make_async_copy(r.wexp.at[j], to, r.stage_sem.at[slot])]
        return [pltpu.make_async_copy(
            r.wexp.at[:, pl.ds(pl.multiple_of(s * (z.ff // members) + j * sub, sub), sub)],
            to.at[:, s * sub : (s + 1) * sub], r.stage_sem.at[slot]) for s in range(members)]

    def stored(slot):
        return pltpu.make_async_copy(we_v.at[0, slot], r.ge.at[slot, me], r.store_sem.at[slot])

    def staged(slot):
        pltpu.make_async_copy(we_v.at[0, slot], we_v.at[0, slot], r.stage_sem.at[slot]).wait()
        stored(slot).start()

    for slot in range(SLOTS):
        for cp in stage_copies(slot):
            cp.start()
    pl.semaphore_wait(barrier, len(others))

    def small_copy(o):
        return pltpu.make_async_remote_copy(
            sm.at[me], sm.at[me], r.sm_send.at[o], r.sm_recv.at[o],
            device_id=(me ^ o, rep), device_id_type=MESH)

    serve(0)
    coming = [pltpu.make_async_copy(src, dst, r.late_sem.at[i]) for i, (src, dst) in enumerate((
        (r.mix_dn, r.mix_dn_v), (r.mix_up, r.mix_up_v), (r.dy, r.dy_v), (r.exp_dn, r.exp_dn_v),
        (r.exp_up, r.exp_up_v), (r.red_dn, r.red_dn_v), (r.red_up, r.red_up_v)))]
    for cp in coming:
        cp.start()
    r = r._replace(dy=r.dy_v, mix_dn=r.mix_dn_v, mix_up=r.mix_up_v, exp_dn=r.exp_dn_v, exp_up=r.exp_up_v,
                   red_dn=r.red_dn_v, red_up=r.red_up_v)
    sm[me] = r.small[...]
    for o in range(1, members):
        small_copy(o).start()
    for slot in range(SLOTS):
        staged(slot)
    for slot in range(SLOTS):
        stored(slot).wait()
    serve(1)
    for o in range(1, members):
        pltpu.make_async_copy(sm.at[me ^ o], sm.at[me ^ o], r.sm_recv.at[o]).wait()

    def vec(row):
        return jnp.concatenate([sm[s, :, row * rows : (row + 1) * rows] for s in range(members)], axis=1)

    def norm_rows(src, gain, bias, dst, part):
        gv, bv = vec(gain), vec(bias)

        def body(i, _):
            at = pl.ds(pl.multiple_of(i * 128, 128), 128)
            n, _inv = norm_parts(src[at, :].astype(f32))
            dst[at, :] = (n * gv + bv).astype(bf16)
            return 0

        lax.fori_loop(part * length // 256, (part + 1) * length // 256, body, 0)

    for part in range(2):
        serve(10 + part)
        norm_rows(r.x, 0, 1, r.a_v, part)

    r.gain[...] = vec(0)

    t_row = lax.broadcasted_iota(jnp.int32, (1, length), 1)
    before_t = lax.broadcasted_iota(jnp.int32, (length, length), 0) < lax.broadcasted_iota(
        jnp.int32, (length, length), 1)
    c_ids = lax.broadcasted_iota(jnp.int32, (cap, length), 0)
    lane = lax.broadcasted_iota(jnp.int32, (cap, 128), 1)
    span = length * z.replicas
    first = (me * z.replicas + rep) * length
    tf = t_row.astype(f32)
    src_cols = lax.div(r.group[...], span).astype(f32).T
    chosen = jnp.zeros((length, 128), f32)
    for k in range(members):
        serve(20 + k)
        row = r.group[k : k + 1, :]
        src = lax.div(row, span)
        earlier = jnp.where((src_cols[:, k : k + 1] == src.astype(f32)) & before_t, 1.0, 0.0)
        slot_row = src * cap + jnp.sum(earlier, axis=0, keepdims=True).astype(jnp.int32)
        r.slot[k] = slot_row
        hit = slot_row == c_ids + me * cap

        def pick(values):
            return jnp.sum(jnp.where(hit, values, 0.0), axis=1, keepdims=True)

        full = pick(jnp.ones_like(tf))
        tok = pick((row - first + 1).astype(f32)) - 1.0
        put = jnp.where(tok == tf, 1.0, 0.0).astype(bf16)
        r.put[k] = put
        end = jnp.zeros((1, 1), f32)
        start = jnp.zeros_like(tf)
        ids = [jnp.zeros_like(tf) for _ in range(z.projs)]
        for j in range(z.seqs):
            n = sm[k, :, z.len_at + j : z.len_at + j + 1]
            inside = (tf >= end) & (tf < end + n)
            end = end + n
            start = start + jnp.where(tf >= end, n, 0.0)
            for p in range(z.projs):
                at = z.ids_at + j * z.projs + p
                ids[p] = ids[p] + jnp.where(inside, sm[k, :, at : at + 1], 0.0)
        info = jnp.where(lane == 0, pick(start) + (1.0 - full), 0.0)
        info = jnp.where(lane == 1, pick(tf), info)
        for p in range(z.projs):
            info = jnp.where(lane == 2 + p, pick(ids[p]), info)
        r.info[k] = info
        chosen = chosen + dot_tn(put, info.astype(bf16))
    r.chosen[...] = chosen
    rank_of = lax.broadcasted_iota(jnp.int32, (length, rk), 1) // z.rank

    def mask(p):
        return jnp.where(rank_of.astype(f32) == r.chosen[:, 2 + p : 3 + p], 1.0, 0.0)

    a_v, q_v = r.a_v, r.q_v
    o_v = q_v
    serve(2)
    r.low0[...] = (dot_nt(a_v[...], r.q_dn[...]) * mask(0)).astype(bf16)
    r.low1[...] = (dot_nt(a_v[...], r.kv_dn[...]) * mask(1)).astype(bf16)
    out_a = pltpu.make_async_copy(a_v, r.a, r.out_sem.at[0])
    out_a.start()

    serve(3)
    g.ready(0, (KV,))
    kv_loads = [pltpu.make_async_copy(
        r.wkv if o == 0 else g.place(KV, 0, o), we_v.at[1, me ^ o, :, 0:w], r.kv_send.at[o]) for o in range(members)]
    for cp in kv_loads:
        cp.start()
    for cp in kv_loads:
        cp.wait()
    back_kv = pltpu.make_async_copy(we_v.at[1, me, :, 0:w], g.place(KV, 0, 0), r.kv_send.at[0])
    back_kv.start()
    vb = jnp.concatenate([sm[s, :, z.vb_at : z.vb_at + hd // members] for s in range(members)], axis=1)
    kv_bias = jnp.concatenate([jnp.zeros((1, hd), f32), vb], axis=1)
    kv = (dot_nn(a_v[...], we_v[1, :, :, 0:w].reshape(d, w)) + kv_bias
          + scale_lora * dot_nn(r.low1[...], r.kv_up[...])).astype(bf16)
    for k in range(members):
        r.kvp[k] = dot_nn(r.put[k], kv).astype(bf16)

    def kv_copy(o):
        return pltpu.make_async_remote_copy(
            r.kvp, r.kvs.at[me], r.kv_send.at[o], r.kv_recv.at[o],
            device_id=(me ^ o, rep), device_id_type=MESH)

    back_kv.wait()
    own_kv = pltpu.make_async_copy(r.kvp, r.kvs.at[me], r.kv_send.at[0])
    for o in range(1, members):
        kv_copy(o).start()
    own_kv.start()

    for slot in V:
        g.issue(slot, BOTH, False)
    serve(4)

    def wide_load(which):
        g.ready(which, HALVES)
        out = []
        for kind in HALVES:
            for o in range(members):
                src = g.own[kind](which) if o == 0 else g.place(kind, which, o)
                for c in range(d // fc):
                    out.append(pltpu.make_async_copy(
                        src.at[:, c * fc : (c + 1) * fc],
                        we_v.at[c, me ^ o, (kind - AT) * half : (kind - AT + 1) * half],
                        r.load_sem.at[kind - AT, c, o]))
        for cp in out:
            cp.start()
        for cp in out:
            cp.wait()
        back = [pltpu.make_async_copy(
            we_v.at[c, me, (kind - AT) * half : (kind - AT + 1) * half],
            g.place(kind, which, 0).at[:, c * fc : (c + 1) * fc],
            r.load_sem.at[kind - AT, c, 0]) for kind in HALVES for c in range(d // fc)]
        for cp in back:
            cp.start()
        return back

    serve(5)
    back_q = wide_load(WQ)
    q_bias = vec(2)
    for c in range(d // fc):
        serve(14 + c)
        at = slice(c * fc, (c + 1) * fc)
        q_v[:, at] = (dot_nn(a_v[...], we_v[c].reshape(d, fc)) + q_bias[:, at]
                      + scale_lora * dot_nn(r.low0[...], r.q_up[:, at])).astype(bf16)
    out_q = pltpu.make_async_copy(q_v, r.q, r.out_sem.at[1])
    out_q.start()

    for cp in back_q:
        cp.wait()

    serve(6)

    for o in range(1, members):
        pltpu.make_async_copy(r.kvs.at[me ^ o], r.kvs.at[me ^ o], r.kv_recv.at[o]).wait()
    own_kv.wait()
    for cp in coming:
        cp.wait()
    dm[...] = jnp.zeros_like(dm)

    def kvb_load(k, buf):
        return pltpu.make_async_copy(r.kvs.at[:, k], r.kvb.at[buf], r.kvb_sem.at[buf])

    def kd_out(k, buf):
        return pltpu.make_async_copy(r.kd_st.at[buf], r.kd.at[k], r.kd_sem.at[buf])

    kvb_load(0, 0).start()
    groups = 2

    def attend(k, _):
        buf = lax.rem(k, 2)

        @pl.when(k + 1 < members)
        def _():
            kvb_load(k + 1, 1 - buf).start()

        for i in range(min(members, 16)):
            if 40 + i in SERVE:
                pl.when(k == i)(lambda i=i: serve(40 + i))
        kvb_load(k, buf).wait()
        oh = key_onehot(r.slot[k], z.slots)
        kvd = dot_tn(oh, r.kvb[buf].reshape(z.slots, w)).astype(bf16)

        @pl.when(k >= 2)
        def _():
            kd_out(k, buf).wait()

        r.kd_st[buf] = kvd
        kd_out(k, buf).start()
        put = r.put[k]
        qp = dot_nn(put, q_v[...]).astype(bf16)
        info = r.info[k]
        outs = []
        per = heads // groups
        for h in range(groups):
            qr = to_rows(qp[:, h * per * hd : (h + 1) * per * hd], per)
            p = softmax_rows(qr, kvd[:, :hd], info, per).astype(bf16)
            outs.append(to_cols(dot_nn(p, kvd[:, hd:]).astype(bf16), per))
        dm[...] += dot_tn(put, jnp.concatenate(outs, axis=1))
        return 0

    lax.fori_loop(0, members, attend, 0)
    out_q.wait()
    o_v[...] = dm[...].astype(bf16)
    out_o = pltpu.make_async_copy(o_v, r.o, r.out_sem.at[2])
    out_o.start()
    r.low2[...] = (dot_nt(o_v[...], r.mix_dn[...]) * mask(2)).astype(bf16)
    serve(7)
    back_m = wide_load(WMIX)
    mix_bias = vec(3)
    for c in range(d // fc):
        serve(16 + c)
        at = slice(c * fc, (c + 1) * fc)
        y[:, at] = (r.x[:, at].astype(f32) + dot_nn(o_v[...], we_v[c].reshape(d, fc)) + mix_bias[:, at]
                    + scale_lora * dot_nn(r.low2[...], r.mix_up[:, at]))

    def load(slot, buf):
        out = [pltpu.make_async_copy(r.ge.at[slot], we_v.at[buf], r.load_sem.at[0, buf, 0])]
        for o in range(members):
            src = g.own[WR](slot) if o == 0 else g.place(WR, slot, o)
            out.append(pltpu.make_async_copy(src, wr_v.at[buf, me ^ o], r.load_sem.at[1, buf, o]))
        return out

    def fetch(slot, buf):
        g.ready(slot, BOTH)
        for cp in load(slot, buf):
            cp.start()

    for cp in back_m:
        cp.wait()
    out_r = pltpu.make_async_copy(y, r.resid, r.out_sem.at[3])
    out_r.start()
    out_a.wait()
    m_v = a_v
    for part in range(2):
        serve(12 + part)
        norm_rows(y, 4, 5, m_v, part)
    serve(8)
    out_m = pltpu.make_async_copy(m_v, r.m, r.out_sem.at[0])
    out_m.start()
    r.low3[...] = (dot_nt(m_v[...], r.exp_dn[...]) * mask(3)).astype(bf16)
    r.e4[...] = (scale_lora * dot_nt(r.dy[...], r.red_up[...]) * mask(4)).astype(bf16)
    dm[...] = jnp.zeros_like(dm)
    r.lowr[...] = jnp.zeros_like(r.lowr)
    r.er[...] = jnp.zeros_like(r.er)
    out_r.wait()
    y[...] += vec(6)

    def g_out(j, buf):
        return (pltpu.make_async_copy(r.gup_st.at[buf], r.gup.at[:, j], r.g_sem.at[0, buf]),
                pltpu.make_async_copy(r.gdn_st.at[buf], r.gdn.at[:, j], r.g_sem.at[1, buf]))

    serve(9)
    fetch(MLP_ORDER[0], 0)

    def step(n, _):
        for i in range(SLOTS):
            if 60 + 2 * i in SERVE:
                pl.when(n == i)(lambda i=i: serve(60 + 2 * i))
        buf = lax.rem(n, 2)
        slot = jnp.int32(0)
        for i, q in enumerate(MLP_ORDER):
            slot = jnp.where(n == i, q, slot)
        for cp in load(slot, buf):
            cp.wait()
        j = chunk_of(slot, parity)
        we = we_v[buf].reshape(d, fc)
        wr = wr_v[buf].reshape(fc, d)
        if z.aligned:
            def cut(ref):
                return jnp.concatenate([ref[:, pl.ds(pl.multiple_of(s * (z.ff // members) + j * sub, sub), sub)]
                                        for s in range(members)], axis=1)
            bup, adn = cut(r.exp_up), cut(r.red_dn)
        else:
            bup, adn = r.exp_up[j], r.red_dn[j]
        be = jnp.zeros((1, fc), f32)
        for i in range(SLOTS):
            lo = z.be_at + i * sub
            row = jnp.concatenate([sm[s, :, lo : lo + sub] for s in range(members)], axis=1)
            be = jnp.where(j == i, row, be)
        hid = dot_nn(m_v[...], we) + be
        hid = hid + scale_lora * dot_nn(r.low3[...], bup)
        cube = hid * hid * hid
        t = jnp.tanh(gelu_c * (hid + 0.044715 * cube))
        act = (0.5 * hid * (1.0 + t)).astype(bf16)
        slope = 0.5 * (1.0 + t) + 0.5 * hid * (1.0 - t * t) * (
            gelu_c * (1.0 + 3.0 * 0.044715 * hid * hid)
        )
        dact = dot_nt(r.dy[...], wr) + dot_nn(r.e4[...], adn)
        dh = (dact * slope).astype(bf16)
        for i in range(SLOTS):
            def middle(i=i):
                serve(61 + 2 * i)
                if i + 1 < SLOTS:
                    fetch(MLP_ORDER[i + 1], (i + 1) % 2)
            pl.when(n == i)(middle)
        y[...] += dot_nn(act, wr)
        dm[...] += dot_nt(dh, we)
        r.lowr[...] += dot_nt(act, adn)
        r.er[...] += dot_nt(dh, bup)
        gup = (scale_lora * dot_tn(r.low3[...], dh)).astype(bf16)
        gdn = dot_tn(r.e4[...], act).astype(bf16)

        @pl.when(n >= 2)
        def _():
            for cp in g_out(j, buf):
                cp.wait()

        for to in range(members):
            r.gup_st[buf, to] = gup[:, to * sub : (to + 1) * sub]
            r.gdn_st[buf, to] = gdn[:, to * sub : (to + 1) * sub]
        for cp in g_out(j, buf):
            cp.start()
        return 0

    lax.fori_loop(0, SLOTS, step, 0)

    low4 = (r.lowr[...] * mask(4)).astype(bf16)
    r.low4[...] = low4
    out_o.wait()
    layer_v = q_v
    for c in range(d // fc):
        at = slice(c * fc, (c + 1) * fc)
        layer_v[:, at] = (y[:, at] + scale_lora * dot_nn(low4, r.red_up[:, at])).astype(bf16)
    out_l = pltpu.make_async_copy(layer_v, r.layer, r.out_sem.at[1])
    out_l.start()
    back_r = pltpu.make_async_copy(r.resid, y, r.out_sem.at[3])
    back_r.start()
    e3 = (scale_lora * r.er[...] * mask(3)).astype(bf16)
    r.e3[...] = e3
    gain = vec(4)
    back_r.wait()

    def last(i, _):
        at = pl.ds(pl.multiple_of(i * 128, 128), 128)
        n, inv = norm_parts(y[at, :])
        dn = dm[at, :] + dot_nn(r.e3[at, :], r.exp_dn[...])
        dm[at, :] = r.dy[at, :].astype(f32) + norm_back(n, inv, gain, dn)
        return 0

    lax.fori_loop(0, length // 128, last, 0)
    out_l.wait()
    out_m.wait()
    for buf in range(2):
        kd_out(buf, buf).wait()
        for cp in g_out(buf, buf):
            cp.wait()
    for o in range(1, members):
        small_copy(o).wait_send()
        kv_copy(o).wait_send()
    g.finish()


def forward(z, args):
    vm = pl.BlockSpec(memory_space=pltpu.VMEM)
    hbm = pl.BlockSpec(memory_space=pl.ANY)
    m, n, d, rk, w = z.members, z.length, z.d, z.rk, z.w
    s = jax.ShapeDtypeStruct
    half = z.rows // 2
    outs = dict(
        dres=s((n, d), f32), put=s((m, z.cap, n), bf16), slot=s((m, 1, n), jnp.int32),
        info=s((m, z.cap, 128), f32), chosen=s((n, 128), f32),
        low0=s((n, rk), bf16), low1=s((n, rk), bf16), low2=s((n, rk), bf16), low4=s((n, rk), bf16), e3=s((n, rk), bf16), gain=s((1, d), f32),
        a=s((n, d), bf16), q=s((n, d), bf16), o=s((n, d), bf16), m=s((n, d), bf16), resid=s((n, d), f32),
        kd=s((m, n, w), bf16), gup=s((m, SLOTS, rk, z.sub), bf16), gdn=s((m, SLOTS, rk, z.sub), bf16),
        layer=s((n, d), bf16), kvs=s((m, m, z.cap, w), bf16),
        ge=s((SLOTS, m, z.rows, z.fc), bf16), gr=s((SLOTS, m, z.sub, d), bf16),
        ga=s((2, m, half, d), bf16), gb=s((2, m, half, d), bf16), gk=s((1, m, z.rows, w), bf16))
    in_vmem = 11
    sends = m - 1 + m // 2
    dma = pltpu.SemaphoreType.DMA
    items = 2 * SLOTS + 5
    scratch = dict(
        y=pltpu.VMEM((n, d), f32), dy_v=pltpu.VMEM((n, d), bf16), mix_dn_v=pltpu.VMEM((rk, d), bf16),
        mix_up_v=pltpu.VMEM((rk, d), bf16), exp_dn_v=pltpu.VMEM((rk, d), bf16),
        exp_up_v=pltpu.VMEM(args.exp_up.shape, bf16), red_dn_v=pltpu.VMEM(args.exp_up.shape, bf16),
        red_up_v=pltpu.VMEM((rk, d), bf16), late_sem=dma((7,)), we_v=pltpu.VMEM((2, m, z.rows, z.fc), bf16), wr_v=pltpu.VMEM((2, m, z.sub, d), bf16),
        a_v=pltpu.VMEM((n, d), bf16), q_v=pltpu.VMEM((n, d), bf16),
        kvp=pltpu.VMEM((m, z.cap, w), bf16), kvb=pltpu.VMEM((2, m, z.cap, w), bf16),
        kd_st=pltpu.VMEM((2, n, w), bf16), gup_st=pltpu.VMEM((2, m, rk, z.sub), bf16),
        gdn_st=pltpu.VMEM((2, m, rk, z.sub), bf16), sm=pltpu.VMEM((m, 1, z.small_cols), f32),
        lowr=pltpu.VMEM((n, rk), f32), er=pltpu.VMEM((n, rk), f32), low3=pltpu.VMEM((n, rk), bf16), e4=pltpu.VMEM((n, rk), bf16),
        send_sem=dma((items, sends)), recv_sem=dma((items, m)), sm_send=dma((m,)), sm_recv=dma((m,)),
        kv_send=dma((m,)), kv_recv=dma((m,)), stage_sem=dma((SLOTS,)), store_sem=dma((SLOTS,)),
        load_sem=dma((2, 2, m)), kvb_sem=dma((2,)), kd_sem=dma((2,)), g_sem=dma((2, 2)), out_sem=dma((4,)))
    got = pl.pallas_call(
        lambda *refs: fwd_kernel(z, *refs),
        in_specs=[vm] * 7 + [hbm] * 12,
        out_specs=[vm] * in_vmem + [hbm] * (len(FwdOut._fields) - in_vmem),
        out_shape=list(FwdOut(**outs)),
        scratch_shapes=list(FwdScratch(**scratch)),
        compiler_params=pltpu.CompilerParams(
            vmem_limit_bytes=FWD_VMEM, collective_id=1, has_side_effects=True),
    )(*args)
    return FwdOut(*got)


FWD_VMEM = 62 * 1024 * 1024


class Job:
    def __init__(self, members, replicas, work, got, out, send_sem, recv_sem, turn):
        self.me, self.rep = lax.axis_index("shard"), lax.axis_index("rep")
        self.work, self.got, self.out = work, got, out
        self.send_sem, self.recv_sem = send_sem, recv_sem
        bits = [1 << i for i in range(members.bit_length() - 1)]
        bits = bits if turn == 0 else bits[:1] + bits[1:][::-1]
        self.shard_stages = len(bits)
        self.stages = []
        at, decided = 0, 0
        for b in bits:
            free = [f for f in range(members) if not f & (decided | b)]
            self.stages.append((b, at, free, decided))
            at += len(free)
            decided |= b
        rk = work.shape[2]
        turns = [1 << i for i in range(replicas.bit_length() - 1)]
        sizes = [rk >> (i + 1) for i in range(len(turns))]
        row = 0
        for b, size in list(zip(turns, sizes)) + list(zip(turns, sizes))[::-1]:
            if row + size > rk:
                at, row = at + 1, 0
            self.stages.append((b, at, row, size))
            row += size
        self.sem_at = [s[1] for s in self.stages[: len(bits)]] + [
            self.stages[len(bits) - 1][1] + 1 + i for i in range(2 * len(turns))]
        self.count = len(self.stages)

    def rows(self, i):
        b, _, _, size = self.stages[i]
        start = jnp.int32(0)
        for b2, _, _, size2 in self.stages[self.shard_stages : self.shard_stages + self.turns()]:
            if b2 < b:
                start = start + lax.rem(lax.div(self.rep, b2), 2) * size2
        mine = lax.rem(lax.div(self.rep, b), 2)
        near = pl.ds(pl.multiple_of(start + mine * size, size), size)
        far = pl.ds(pl.multiple_of(start + (1 - mine) * size, size), size)
        return near, far

    def turns(self):
        return (self.count - self.shard_stages) // 2

    def copy(self, i, n=0):
        if i < self.shard_stages:
            b, at, free, decided = self.stages[i]
            src = self.work.at[free[n] | (self.me & decided) | ((self.me ^ b) & b)]
            dst, to = self.got.at[at + n], (self.me ^ b, self.rep)
        else:
            b, at, row, size = self.stages[i]
            near, far = self.rows(i)
            src = self.work.at[self.me, :, far if i < self.shard_stages + self.turns() else near]
            dst, to = self.got.at[at, :, row : row + size], (self.me, self.rep ^ b)
        sem = self.sem_at[i] + n
        return pltpu.make_async_remote_copy(
            src, dst, self.send_sem.at[sem], self.recv_sem.at[sem], device_id=to, device_id_type=MESH)

    def start(self, i):
        for n in range(len(self.stages[i][2]) if i < self.shard_stages else 1):
            self.copy(i, n).start()

    def add(self, i):
        if i < self.shard_stages:
            b, at, free, decided = self.stages[i]
            for n, f in enumerate(free):
                cp = self.copy(i, n)
                cp.wait_recv()
                cp.wait_send()
                keep = f | (self.me & decided) | (self.me & b)
                self.work[keep] = (self.work[keep].astype(f32) + self.got[at + n].astype(f32)).astype(bf16)
            return
        b, at, row, size = self.stages[i]
        cp = self.copy(i)
        cp.wait_recv()
        cp.wait_send()
        near, far = self.rows(i)
        came = self.got[at, :, row : row + size]
        if i < self.shard_stages + self.turns():
            kept = self.work[self.me, :, near].astype(f32) + came.astype(f32)
            self.work[self.me, :, near] = kept.astype(bf16)
        else:
            self.work[self.me, :, far] = came
        if i + 1 == self.count:
            blocks, lanes = self.work.shape[1], self.work.shape[3]
            for j in range(blocks):
                self.out[:, j * lanes : (j + 1) * lanes] = self.work[self.me, j].astype(f32)

    def move(self, i):
        self.add(i)
        if i + 1 < self.count:
            self.start(i + 1)


class BwdIn(NamedTuple):
    dres: object
    put: object
    slot: object
    info: object
    chosen: object
    low0: object
    low1: object
    low2: object
    low4: object
    e3: object
    gain: object
    mix_dn: object
    mix_up: object
    q_dn: object
    q_up: object
    kv_dn: object
    kv_up: object
    ga: object
    gb: object
    gk: object
    q: object
    a: object
    o: object
    m: object
    dy: object
    x: object
    kd: object
    gup: object
    gdn: object


class BwdOut(NamedTuple):
    dx: object
    ja_out: object
    jb_out: object
    jc_out: object
    jd_out: object
    je_out: object
    jf_out: object
    jg_out: object


class BwdScratch(NamedTuple):
    w_v: object
    wk_v: object
    t1: object
    t2: object
    q_v: object
    do_v: object
    dq: object
    kd_st: object
    ds_st: object
    dk_r: object
    w_sem: object
    t_sem: object
    g_sem: object
    kd_sem: object
    dk_send: object
    dk_recv: object
    out_sem: object
    ja_w: object
    ja_g: object
    ja_s: object
    ja_r: object
    jb_w: object
    jb_g: object
    jb_s: object
    jb_r: object
    jc_w: object
    jc_g: object
    jc_s: object
    jc_r: object
    jd_w: object
    jd_g: object
    jd_s: object
    jd_r: object
    je_w: object
    je_g: object
    je_s: object
    je_r: object
    jf_w: object
    jf_g: object
    jf_s: object
    jf_r: object
    jg_w: object
    jg_g: object
    jg_s: object
    jg_r: object


class BwdRefs(NamedTuple):
    dres: object
    put: object
    slot: object
    info: object
    chosen: object
    low0: object
    low1: object
    low2: object
    low4: object
    e3: object
    gain: object
    mix_dn: object
    mix_up: object
    q_dn: object
    q_up: object
    kv_dn: object
    kv_up: object
    ga: object
    gb: object
    gk: object
    q: object
    a: object
    o: object
    m: object
    dy: object
    x: object
    kd: object
    gup: object
    gdn: object
    dx: object
    ja_out: object
    jb_out: object
    jc_out: object
    jd_out: object
    je_out: object
    jf_out: object
    jg_out: object
    w_v: object
    wk_v: object
    t1: object
    t2: object
    q_v: object
    do_v: object
    dq: object
    kd_st: object
    ds_st: object
    dk_r: object
    w_sem: object
    t_sem: object
    g_sem: object
    kd_sem: object
    dk_send: object
    dk_recv: object
    out_sem: object
    ja_w: object
    ja_g: object
    ja_s: object
    ja_r: object
    jb_w: object
    jb_g: object
    jb_s: object
    jb_r: object
    jc_w: object
    jc_g: object
    jc_s: object
    jc_r: object
    jd_w: object
    jd_g: object
    jd_s: object
    jd_r: object
    je_w: object
    je_g: object
    je_s: object
    je_r: object
    jf_w: object
    jf_g: object
    jf_s: object
    jf_r: object
    jg_w: object
    jg_g: object
    jg_s: object
    jg_r: object


def job_shapes(z):
    wide = z.rows // min(128, z.rows)
    lanes = min(128, z.rows)
    chunks = (SLOTS, z.sub) if z.aligned else (SLOTS * z.sub // 128, 128)
    return (chunks, chunks, (2 * wide, lanes), (2 * wide, lanes), (wide, lanes), (wide, lanes), (wide + 1, lanes))


def bwd_kernel(z, *refs):
    r = BwdRefs(*refs)
    members, replicas, rows, fc, d, hd = z.members, z.replicas, z.rows, z.fc, z.d, z.hd
    length, cap, w, heads, rk = z.length, z.cap, z.w, z.heads, z.rk
    me, rep = lax.axis_index("shard"), lax.axis_index("rep")
    half = rows // 2
    halves = d // fc
    w_v, t1, t2, q_v, do_v, dq, dres = r.w_v, r.t1, r.t2, r.q_v, r.do_v, r.dq, r.dres
    outs = refs[len(BwdIn._fields) + 1 : len(BwdIn._fields) + len(BwdOut._fields)]
    held = refs[-4 * len(outs) :]
    ja, jb, jc, jd, je, jf, jg = (
        Job(members, replicas, held[4 * i], held[4 * i + 1], out, held[4 * i + 2], held[4 * i + 3], i % 2)
        for i, out in enumerate(outs))

    barrier = pltpu.get_barrier_semaphore()
    others = [(me ^ o, rep) for o in range(1, members)]
    b = 1
    while b < replicas:
        others.append((me, rep ^ b))
        b *= 2
    for to in others:
        pl.semaphore_signal(barrier, inc=1, device_id=to, device_id_type=MESH)

    def local(src, dst, sem):
        return pltpu.make_async_copy(src, dst, sem)

    def wide(which):
        return [local(part.at[which, :, :, c * fc : (c + 1) * fc],
                      w_v.at[c, :, h * half : (h + 1) * half], r.w_sem.at[h, c])
                for h, part in enumerate((r.ga, r.gb)) for c in range(halves)]

    load_up = local(r.gup, r.ja_w, r.g_sem.at[0])
    load_dn = local(r.gdn, r.jb_w, r.g_sem.at[1])
    load_up.start()
    load_dn.start()
    mix = wide(WMIX)
    for cp in mix:
        cp.start()
    load_m = local(r.m, t1, r.t_sem.at[0])
    load_dy = local(r.dy, t2, r.t_sem.at[1])
    load_q = local(r.q, q_v, r.t_sem.at[2])
    load_k = local(r.gk.at[0], r.wk_v, r.t_sem.at[3])
    for cp in (load_m, load_dy, load_q, load_k):
        cp.start()
    pl.semaphore_wait(barrier, len(others))
    load_up.wait()
    ja.start(0)
    load_dn.wait()
    jb.start(0)

    rank_of = (lax.broadcasted_iota(jnp.int32, (length, rk), 1) // z.rank).astype(f32)

    def mask(p):
        return jnp.where(rank_of == r.chosen[:, 2 + p : 3 + p], 1.0, 0.0)

    def terms(job, block, left, right, sc):
        lanes = job.work.shape[3]
        g = dot_tn(left, right) * sc
        width = right.shape[1] // members
        for to in range(members):
            for i in range(-(-width // lanes)):
                part = g[:, to * width + i * lanes : to * width + min((i + 1) * lanes, width)]
                if part.shape[1] < lanes:
                    part = jnp.concatenate([part, jnp.zeros((rk, lanes - part.shape[1]), f32)], axis=1)
                job.work[to, block + i] = part.astype(bf16)

    per = r.jc_w.shape[1] // 2

    dresl = do_v
    dresl[...] = dres[...].astype(bf16)
    e2 = (scale_lora * dot_nt(dresl[...], r.mix_up[...]) * mask(2)).astype(bf16)
    terms(jd, per, r.low2[...], dresl[...], scale_lora)
    load_m.wait()
    terms(jc, 0, r.e3[...], t1[...], 1.0)
    load_o = local(r.o, t1, r.t_sem.at[0])
    load_o.start()
    load_dy.wait()
    terms(jd, 0, r.low4[...], t2[...], scale_lora)
    load_x = local(r.x, t2, r.t_sem.at[1])
    load_x.start()
    jd.start(0)
    for cp in mix:
        cp.wait()
    ja.move(0)
    dq[...] = dot_nt(dresl[:, 0:fc], w_v[0].reshape(d, fc)) + dot_nn(e2, r.mix_dn[...])
    jb.move(0)
    for c in range(1, halves):
        dq[...] += dot_nt(dresl[:, c * fc : (c + 1) * fc], w_v[c].reshape(d, fc))
    do_v[...] = dq[...].astype(bf16)
    query = wide(WQ)
    for cp in query:
        cp.start()
    load_o.wait()
    terms(jc, per, e2, t1[...], 1.0)
    jc.start(0)
    load_a = local(r.a, t1, r.t_sem.at[0])
    load_a.start()
    jd.move(0)
    dq[...] = jnp.zeros_like(dq)
    load_q.wait()

    def kd_load(k, buf):
        return local(r.kd.at[k], r.kd_st.at[buf], r.kd_sem.at[buf])

    def ds_copy(k, buf, o):
        return pltpu.make_async_remote_copy(
            r.ds_st.at[buf, me ^ o], r.dk_r.at[me, k], r.dk_send.at[buf, o], r.dk_recv.at[o],
            device_id=(me ^ o, rep), device_id_type=MESH)

    kd_load(0, 0).start()
    groups = 4
    sc = hd ** (-0.5)
    plan = (((jc, 0),), (), ((ja, 1), (jd, 1), (jb, 1)), ((jc, 1),), ((ja, 2), (jb, 2), (jd, 2)), ((jc, 2), (ja, 3), (jb, 3)),
            ((jd, 3), (jc, 3), (ja, 4), (jb, 4)), ((jd, 4), (jc, 4), (ja, 5), (jb, 5)))

    def act(some):
        for job, i in some:
            job.move(i)

    def attend(k, _):
        buf = lax.rem(k, 2)

        @pl.when(k + 1 < members)
        def _():
            kd_load(k + 1, 1 - buf).start()

        for i, some in enumerate(plan):
            pl.when(k == i)(lambda some=some: act(some))
        kd_load(k, buf).wait()
        kvd = r.kd_st[buf]
        kd, vd = kvd[:, :hd], kvd[:, hd:]
        put = r.put[k]
        qp = dot_nn(put, q_v[...]).astype(bf16)
        dop = dot_nn(put, do_v[...]).astype(bf16)
        info = r.info[k]
        n = heads // groups
        dqs = []
        dk = jnp.zeros((length, hd), f32)
        dv = jnp.zeros((length, hd), f32)
        for h in range(groups):
            at = slice(h * n * hd, (h + 1) * n * hd)
            qr, dor = to_rows(qp[:, at], n), to_rows(dop[:, at], n)
            p = softmax_rows(qr, kd, info, n)
            dp = dot_nt(dor, vd)
            ds = (p * (dp - jnp.sum(dp * p, axis=1, keepdims=True))).astype(bf16)
            dqs.append(to_cols((dot_nn(ds, kd) * sc).astype(bf16), n))
            dk = dk + dot_tn(ds, qr)
            dv = dv + dot_tn(p.astype(bf16), dor)
        dq[...] += dot_tn(put, jnp.concatenate(dqs, axis=1))
        dkv = jnp.concatenate([dk * sc, dv], axis=1).astype(bf16)
        slots = dot_nn(key_onehot(r.slot[k], z.slots), dkv).astype(bf16).reshape(members, cap, w)

        @pl.when(k >= 2)
        def _():
            for o in range(1, members):
                ds_copy(k, buf, o).wait_send()

        r.ds_st[buf] = slots
        r.dk_r[me, k] = r.ds_st[buf, me]
        for o in range(1, members):
            ds_copy(k, buf, o).start()
        return 0

    lax.fori_loop(0, members, attend, 0)

    following = {ja: 6, jb: 6, jc: 5, jd: 5, je: 0, jf: 0, jg: 0}

    def go(*jobs):
        for job in jobs:
            if following[job] < job.count:
                job.move(following[job])
                following[job] += 1

    go(ja, jb)
    q_v[...] = dq[...].astype(bf16)
    e0 = (scale_lora * dot_nt(q_v[...], r.q_up[...]) * mask(0)).astype(bf16)
    load_a.wait()
    terms(je, 0, e0, t1[...], 1.0)
    je.start(0)
    terms(jf, 0, r.low0[...], q_v[...], scale_lora)
    jf.start(0)
    for o in range(1, members):
        local(r.dk_r.at[me ^ o], r.dk_r.at[me ^ o], r.dk_recv.at[o]).wait()
    go(jd, jc)
    dkv = jnp.zeros((length, w), f32)
    for k in range(members):
        total = r.dk_r[0, k].astype(f32)
        for s in range(1, members):
            total = total + r.dk_r[s, k].astype(f32)
        dkv = dkv + dot_tn(r.put[k], total.astype(bf16))
    dkv = dkv.astype(bf16)
    go(je, jf)
    e1 = (scale_lora * dot_nt(dkv, r.kv_up[...]) * mask(1)).astype(bf16)
    terms(jg, 0, e1, t1[...], 1.0)
    terms(jg, per, r.low1[...], dkv, scale_lora)
    jg.start(0)
    load_k.wait()
    dq[...] = (dot_nn(e0, r.q_dn[...]) + dot_nn(e1, r.kv_dn[...])
               + dot_nt(dkv, r.wk_v[...].reshape(d, w)))
    go(jd, jc, je, jf, jg)
    for cp in query:
        cp.wait()
    for c in range(halves):
        dq[...] += dot_nt(q_v[:, c * fc : (c + 1) * fc], w_v[c].reshape(d, fc))
        go(je, jf, jg)
    load_x.wait()
    gain = r.gain[...]

    def back(i, _):
        at = pl.ds(pl.multiple_of(i * 128, 128), 128)
        n, inv = norm_parts(t2[at, :].astype(f32))
        do_v[at, :] = (dres[at, :] + norm_back(n, inv, gain, dq[at, :])).astype(bf16)
        return 0

    for part in range(2):
        lax.fori_loop(part * length // 256, (part + 1) * length // 256, back, 0)
        go(je, jf, jg)
    out = local(do_v, r.dx, r.out_sem)
    out.start()
    while any(following[job] < job.count for job in following):
        go(ja, jb, jc, jd, je, jf, jg)
    out.wait()
    for buf in range(2):
        for o in range(1, members):
            ds_copy(buf, buf, o).wait_send()


def backward(z, args):
    vm = pl.BlockSpec(memory_space=pltpu.VMEM)
    hbm = pl.BlockSpec(memory_space=pl.ANY)
    m, n, d, rk, w = z.members, z.length, z.d, z.rk, z.w
    s = jax.ShapeDtypeStruct
    dma = pltpu.SemaphoreType.DMA
    shapes = job_shapes(z)
    legs = m - 1 + 2
    sems = m - 1 + 2 * (z.replicas.bit_length() - 1)
    scratch = dict(
        w_v=pltpu.VMEM((d // z.fc, m, z.rows, z.fc), bf16), wk_v=pltpu.VMEM((m, z.rows, w), bf16),
        t1=pltpu.VMEM((n, d), bf16), t2=pltpu.VMEM((n, d), bf16), q_v=pltpu.VMEM((n, d), bf16), do_v=pltpu.VMEM((n, d), bf16),
        dq=pltpu.VMEM((n, d), f32), kd_st=pltpu.VMEM((2, n, w), bf16), ds_st=pltpu.VMEM((2, m, z.cap, w), bf16),
        dk_r=pltpu.VMEM((m, m, z.cap, w), bf16),
        w_sem=dma((2, d // z.fc)), t_sem=dma((4,)), g_sem=dma((2,)), kd_sem=dma((2,)), dk_send=dma((2, m)),
        dk_recv=dma((m,)), out_sem=dma(()))
    scratch = [scratch[k] for k in BwdScratch._fields[: len(scratch)]]
    job_outs = [s((rk, blocks * lanes), f32) for blocks, lanes in shapes]
    job_scratch = [x for blocks, lanes in shapes for x in (
        pltpu.VMEM((m, blocks, rk, lanes), bf16), pltpu.VMEM((legs, blocks, rk, lanes), bf16), dma((sems,)), dma((sems,)))]
    first_hbm = 17
    got = pl.pallas_call(
        lambda *refs: bwd_kernel(z, *refs),
        in_specs=[vm] * first_hbm + [hbm] * (len(BwdIn._fields) - first_hbm),
        out_specs=[hbm] + [vm] * len(shapes),
        out_shape=[s((n, d), bf16)] + job_outs,
        scratch_shapes=scratch + job_scratch,
        compiler_params=pltpu.CompilerParams(
            vmem_limit_bytes=FWD_VMEM, collective_id=2, has_side_effects=True),
    )(*BwdIn(**args))
    return BwdOut(*got)


def final(sums, z, experts, rank):
    c, n = z.rows, z.w // z.members
    ff = z.ff // z.members
    cuts = ((4, 0, c), (5, 0, c), (6, 0, c), (6, c, n), (2, c, c), (3, c, c), (2, 0, c), (0, 0, ff), (1, 0, ff), (3, 0, c))

    def kernel(*refs):
        for (job, at, width), out in zip(cuts, refs[len(sums):]):
            out[...] = refs[job][:, at : at + width].reshape(experts, rank, width)

    vm = pl.BlockSpec(memory_space=pltpu.VMEM)
    return pl.pallas_call(
        kernel, in_specs=[vm] * len(sums), out_specs=[vm] * len(cuts),
        out_shape=[jax.ShapeDtypeStruct((experts, rank, w), f32) for _, _, w in cuts])(*sums)


def local(tokens, out_grad, token_perm, seq_lens, adapter_ids,
          attn_g, attn_b, wq, bq, wkv, bv, wmix, bmix, mlp_g, mlp_b, wexp, bexp, wred, bred,
          q_dn, q_up, kv_dn, kv_up, mix_dn, mix_up, exp_dn, exp_up, red_dn, red_up):
    members = lax.axis_size("shard")
    replicas = lax.axis_size("rep")
    rep = lax.axis_index("rep")
    length, d = tokens.shape
    experts, rank = q_dn.shape[:2]
    rk = experts * rank
    z = Sizes(members, replicas, length, d, wexp.shape[1], bv.shape[0] * members, rk, rank,
              seq_lens.shape[1], adapter_ids.shape[2])
    flat = lambda s: s.reshape(rk, s.shape[2])
    q_dn, q_up, kv_dn, kv_up, mix_dn, mix_up, exp_dn, exp_up, red_dn, red_up = map(
        flat, (q_dn, q_up, kv_dn, kv_up, mix_dn, mix_up, exp_dn, exp_up, red_dn, red_up))
    group = lax.dynamic_index_in_dim(
        token_perm.reshape(members, replicas, length), rep, 1, keepdims=False)

    small = jnp.concatenate(
        [v.astype(f32) for v in (attn_g, attn_b, bq, bmix, mlp_g, mlp_b, bred, bexp, bv, seq_lens[0], adapter_ids.reshape(-1))]
        + [jnp.zeros((z.small_cols - z.ids_at - seq_lens.shape[1] * adapter_ids.shape[2],), f32)])[None]
    by_chunk = lambda s: s.reshape(s.shape[0], members, SLOTS, z.sub).transpose(2, 0, 1, 3).reshape(
        SLOTS, s.shape[0], z.fc)
    chunked = (lambda s: s) if z.aligned else by_chunk
    got = forward(z, FwdIn(
        x=tokens, dy=out_grad, small=small, group=group,
        q_dn=q_dn, q_up=q_up, kv_dn=kv_dn, kv_up=kv_up, mix_dn=mix_dn, mix_up=mix_up, exp_dn=exp_dn,
        exp_up=chunked(exp_up), red_dn=chunked(red_dn), red_up=red_up,
        wq=wq, wkv=wkv, wmix=wmix, wexp=chunked(wexp), wred=wred.reshape(SLOTS, z.sub, d)))
    gup, gdn = got.gup, got.gdn
    if not z.aligned:
        pack = 128 // z.sub
        gup, gdn = (g.reshape(members, SLOTS // pack, pack, rk, z.sub).transpose(0, 1, 3, 2, 4).reshape(
            members, SLOTS // pack, rk, 128) for g in (gup, gdn))
    back = backward(z, dict(
        dres=got.dres, put=got.put, slot=got.slot, info=got.info, chosen=got.chosen, low0=got.low0, low1=got.low1,
        low2=got.low2, low4=got.low4, e3=got.e3, gain=got.gain, ga=got.ga, gb=got.gb, gk=got.gk, q=got.q, a=got.a,
        o=got.o, m=got.m, kd=got.kd, gup=gup, gdn=gdn,
        mix_dn=mix_dn, mix_up=mix_up, q_dn=q_dn, q_up=q_up, kv_dn=kv_dn, kv_up=kv_up, dy=out_grad, x=tokens))
    g = final(back[1:], z, experts, rank)
    return (got.layer, back.dx, *g)


def solution(mesh):
    both = ("shard", "rep")
    row, vec = P("shard", None), P("shard")
    in_specs = (
        P(both, None), P(both, None), P(), P(both, None), P(both, None, None),
        vec, vec, row, vec, row, vec, row, vec, vec, vec, row, vec, row, vec,
    ) + (P(),) * 10
    out_specs = (P(both, None), P(both, None)) + (P(None, None, "shard"),) * 10
    return jax.shard_map(local, mesh=mesh, in_specs=in_specs, out_specs=out_specs, check_vma=False)
```

time: 479 us -> 465 us (0.971)
  local copies, waits for them, and re-layouts: 20.8 us -> 12.9 us
  Pallas kernels: 446 us -> 440 us
    slice x4 -> x0, local copies, waits for them, and re-layouts: 6.61 us -> none  [the longest x1 1.89 us: local(): two[:, :c]]
    concatenate x3 -> x1, local copies, waits for them, and re-layouts: 0.87 us -> 6.09 us  [local(): jnp.concatenate([v.astype(f32) for v in (attn_g, attn_b, bq, bmix, mlp_g,...]
    pallas_call x1, Pallas kernels: 120 us -> 115 us  [backward(): pl.pallas_call(lambda *refs: bwd_kernel(z, *refs), in_specs=[vm] * first_...]
    pallas_call x1 -> x2, Pallas kernels: 326 us -> 326 us  [the longest x1 323 us: forward(): pl.pallas_call(lambda *refs: fwd_kernel(z, *refs), in_specs=[vm] * 7 + [h...]
where the time goes in v5:
time: 465 us; the launch traced here: 456 us
  Pallas kernels  440 us (95%)
  local copies, waits for them, and re-layouts  12.9 us (3%)
    pallas_call x1, Pallas kernels, forward(): pl.pallas_call(lambda *refs: fwd_kernel(z, *refs), in_specs=[vm] * 7 + [h...  323 us
    pallas_call x1, Pallas kernels, backward(): pl.pallas_call(lambda *refs: bwd_kernel(z, *refs), in_specs=[vm] * first_...  115 us

profile of v5, /device:TPU:0, one launch (start us, length us, event | category | flops | bytes accessed | tf_op | source)
XLA Modules:
  0.0 455.7 jit_solution(2142336749857663054)
XLA Ops:
  0.6 0.7 convert_bitcast_fusion
  1.3 0.7 convert_element_type.50
  2.0 0.1 convert_element_type.51
  2.1 6.1 %concatenate.3 = f32[2944]{0:T(1024)S(1)} concatenate(bf16[256]{0:T(256)(128)(2,1)} %param.34, bf16[256]{0:T(256)(128)(2,1)} %param.35, bf16[256]{0:T(256)(128)(2,1)} %param.37, bf16[256]{0:T(256)(128)(2,1)} %param.41, bf16[256]{0:T(256)(128)(2,1)} %param.42, bf16[256]{0:T(256)(128)(2,1)} %param.43, bf16[256]{0:T(256)(128)(2,1)} %param.47, bf16[1024]{0:T(1024)(128)(2,1)} %param.45, ...), dimensions={0} | concatenate | bytes 17888 | tf_op jit(solution)/shard_map/concatenate | solution.py:1426
  8.2 0.6 broadcast_in_dim.7.refs_1_
  8.8 0.9 reshape.63
  9.7 0.6 copy.43
  10.3 322.7 %shard_map.364 = (f32[512,2048]{1,0:T(8,128)}, bf16[8,96,512]{2,1,0:T(8,128)(2,1)}, s32[8,1,512]{2,1,0:T(1,128)}, f32[8,96,128]{2,1,0:T(8,128)}, f32[512,128]{1,...) custom-call(bf16[512,2048]{1,0:T(8,128)(2,1)} %refs_25_.1, ...), custom_call_target="tpu_custom_call" | custom-call | tf_op jit(solution)/shard_map/pallas_call | solution.py:844
  333.0 114.8 %shard_map.365 = (bf16[512,2048]{1,0:T(8,128)(2,1)}, f32[128,1024]{1,0:T(8,128)}, f32[128,1024]{1,0:T(8,128)}, f32[128,512]{1,0:T(8,128)}, f32[128,512]{1,0:T(8,...) custom-call(f32[512,2048]{1,0:T(8,128)} %get-tuple-element.53.refs_0_, ...), custom_call_target="tpu_custom_call" | custom-call | tf_op jit(solution)/shard_map/pallas_call | solution.py:1382
  447.9 2.8 shard_map.366
  450.6 0.0 copy-start
  450.7 3.3 copy.46
  454.0 0.0 copy-done
  454.0 1.3 copy.47
  (2 shorter events, 0.0 us)
Async XLA Ops:
  450.6 3.3 copy-start

commit v6 on v5

--- a/solution.py
+++ b/solution.py
@@ -203,14 +203,24 @@
         self.aligned = self.sub % 128 == 0
         self.be_at = 7 * self.rows
         self.vb_at = self.be_at + ff // members
-        self.len_at = self.vb_at + hd // members
-        self.ids_at = self.len_at + seqs
-        self.small_cols = -(-(self.ids_at + seqs * projs) // 128) * 128
+        self.len_at = self.vb_at + 128
+        self.ids_at = self.len_at + 128
+        self.small_cols = self.ids_at + 128
 
 
 class FwdIn(NamedTuple):
     x: object
-    small: object
+    attn_g: object
+    attn_b: object
+    bq: object
+    bmix: object
+    mlp_g: object
+    mlp_b: object
+    bred: object
+    bexp: object
+    bv: object
+    lens: object
+    ids: object
     group: object
     q_dn: object
     q_up: object
@@ -300,7 +310,17 @@
 
 class FwdRefs(NamedTuple):
     x: object
-    small: object
+    attn_g: object
+    attn_b: object
+    bq: object
+    bmix: object
+    mlp_g: object
+    mlp_b: object
+    bred: object
+    bexp: object
+    bv: object
+    lens: object
+    ids: object
     group: object
     q_dn: object
     q_up: object
@@ -450,7 +470,13 @@
         cp.start()
     r = r._replace(dy=r.dy_v, mix_dn=r.mix_dn_v, mix_up=r.mix_up_v, exp_dn=r.exp_dn_v, exp_up=r.exp_up_v,
                    red_dn=r.red_dn_v, red_up=r.red_up_v)
-    sm[me] = r.small[...]
+    sm[me] = jnp.zeros((1, z.small_cols), f32)
+    for i, v in enumerate((r.attn_g, r.attn_b, r.bq, r.bmix, r.mlp_g, r.mlp_b, r.bred)):
+        sm[me, :, i * rows : (i + 1) * rows] = v[...].astype(f32).reshape(1, rows)
+    sm[me, :, z.be_at : z.vb_at] = r.bexp[...].astype(f32).reshape(1, z.vb_at - z.be_at)
+    sm[me, :, z.vb_at : z.vb_at + hd // members] = r.bv[...].astype(f32).reshape(1, hd // members)
+    sm[me, :, z.len_at : z.len_at + z.seqs] = r.lens[...].astype(f32)
+    sm[me, :, z.ids_at : z.ids_at + z.seqs * z.projs] = r.ids[...].astype(f32)
     for o in range(1, members):
         small_copy(o).start()
     for slot in range(SLOTS):
@@ -843,7 +869,7 @@
         load_sem=dma((2, 2, m)), kvb_sem=dma((2,)), kd_sem=dma((2,)), g_sem=dma((2, 2)), out_sem=dma((4,)))
     got = pl.pallas_call(
         lambda *refs: fwd_kernel(z, *refs),
-        in_specs=[vm] * 7 + [hbm] * 12,
+        in_specs=[vm] * 17 + [hbm] * 12,
         out_specs=[vm] * in_vmem + [hbm] * (len(FwdOut._fields) - in_vmem),
         out_shape=list(FwdOut(**outs)),
         scratch_shapes=list(FwdScratch(**scratch)),
@@ -856,88 +882,78 @@
 FWD_VMEM = 62 * 1024 * 1024
 
 
+HALVE, PLANE, SCATTER, COLLECT = range(4)
+
+
 class Job:
-    def __init__(self, members, replicas, work, got, out, send_sem, recv_sem, turn):
+    def __init__(self, members, replicas, work, got, out, send_sem, recv_sem, turn, direct):
         self.me, self.rep = lax.axis_index("shard"), lax.axis_index("rep")
         self.work, self.got, self.out = work, got, out
         self.send_sem, self.recv_sem = send_sem, recv_sem
+        self.size = work.shape[2] // replicas
         bits = [1 << i for i in range(members.bit_length() - 1)]
         bits = bits if turn == 0 else bits[:1] + bits[1:][::-1]
-        self.shard_stages = len(bits)
         self.stages = []
         at, decided = 0, 0
-        for b in bits:
+        for b in bits[:1] if direct else bits:
             free = [f for f in range(members) if not f & (decided | b)]
-            self.stages.append((b, at, free, decided))
+            self.stages.append((HALVE, at, free, b, decided))
             at += len(free)
             decided |= b
-        rk = work.shape[2]
-        turns = [1 << i for i in range(replicas.bit_length() - 1)]
-        sizes = [rk >> (i + 1) for i in range(len(turns))]
-        row = 0
-        for b, size in list(zip(turns, sizes)) + list(zip(turns, sizes))[::-1]:
-            if row + size > rk:
-                at, row = at + 1, 0
-            self.stages.append((b, at, row, size))
-            row += size
-        self.sem_at = [s[1] for s in self.stages[: len(bits)]] + [
-            self.stages[len(bits) - 1][1] + 1 + i for i in range(2 * len(turns))]
+        if direct:
+            self.stages.append((PLANE, at, list(range(2, members, 2)), 0, 0))
+            at += members // 2 - 1
+        turns = list(range(1, replicas))
+        self.stages.append((SCATTER, at, turns, at, 0))
+        self.stages.append((COLLECT, at + len(turns), turns, at + 1, 0))
         self.count = len(self.stages)
 
-    def rows(self, i):
-        b, _, _, size = self.stages[i]
-        start = jnp.int32(0)
-        for b2, _, _, size2 in self.stages[self.shard_stages : self.shard_stages + self.turns()]:
-            if b2 < b:
-                start = start + lax.rem(lax.div(self.rep, b2), 2) * size2
-        mine = lax.rem(lax.div(self.rep, b), 2)
-        near = pl.ds(pl.multiple_of(start + mine * size, size), size)
-        far = pl.ds(pl.multiple_of(start + (1 - mine) * size, size), size)
-        return near, far
-
-    def turns(self):
-        return (self.count - self.shard_stages) // 2
-
-    def copy(self, i, n=0):
-        if i < self.shard_stages:
-            b, at, free, decided = self.stages[i]
-            src = self.work.at[free[n] | (self.me & decided) | ((self.me ^ b) & b)]
+    def rows(self, rep):
+        return pl.ds(pl.multiple_of(rep * self.size, self.size), self.size)
+
+    def copy(self, i, n):
+        kind, at, items, b, decided = self.stages[i]
+        item = items[n]
+        if kind == HALVE:
+            src = self.work.at[item | (self.me & decided) | ((self.me ^ b) & b)]
             dst, to = self.got.at[at + n], (self.me ^ b, self.rep)
+        elif kind == PLANE:
+            src, dst, to = self.work.at[self.me ^ item], self.got.at[at + n], (self.me ^ item, self.rep)
         else:
-            b, at, row, size = self.stages[i]
-            near, far = self.rows(i)
-            src = self.work.at[self.me, :, far if i < self.shard_stages + self.turns() else near]
-            dst, to = self.got.at[at, :, row : row + size], (self.me, self.rep ^ b)
-        sem = self.sem_at[i] + n
+            src = self.work.at[self.me, :, self.rows(self.rep ^ item if kind == SCATTER else self.rep)]
+            dst = self.got.at[b, :, n * self.size : (n + 1) * self.size]
+            to = (self.me, self.rep ^ item)
         return pltpu.make_async_remote_copy(
-            src, dst, self.send_sem.at[sem], self.recv_sem.at[sem], device_id=to, device_id_type=MESH)
+            src, dst, self.send_sem.at[at + n], self.recv_sem.at[at + n], device_id=to, device_id_type=MESH)
 
     def start(self, i):
-        for n in range(len(self.stages[i][2]) if i < self.shard_stages else 1):
+        for n in range(len(self.stages[i][2])):
             self.copy(i, n).start()
 
     def add(self, i):
-        if i < self.shard_stages:
-            b, at, free, decided = self.stages[i]
-            for n, f in enumerate(free):
-                cp = self.copy(i, n)
-                cp.wait_recv()
-                cp.wait_send()
-                keep = f | (self.me & decided) | (self.me & b)
+        kind, at, items, b, decided = self.stages[i]
+        for n in range(len(items)):
+            cp = self.copy(i, n)
+            cp.wait_recv()
+            cp.wait_send()
+        if kind == HALVE:
+            for n, item in enumerate(items):
+                keep = item | (self.me & decided) | (self.me & b)
                 self.work[keep] = (self.work[keep].astype(f32) + self.got[at + n].astype(f32)).astype(bf16)
-            return
-        b, at, row, size = self.stages[i]
-        cp = self.copy(i)
-        cp.wait_recv()
-        cp.wait_send()
-        near, far = self.rows(i)
-        came = self.got[at, :, row : row + size]
-        if i < self.shard_stages + self.turns():
-            kept = self.work[self.me, :, near].astype(f32) + came.astype(f32)
-            self.work[self.me, :, near] = kept.astype(bf16)
+        elif kind == PLANE:
+            total = self.work[self.me].astype(f32)
+            for n in range(len(items)):
+                total = total + self.got[at + n].astype(f32)
+            self.work[self.me] = total.astype(bf16)
+        elif kind == SCATTER:
+            near = self.rows(self.rep)
+            total = self.work[self.me, :, near].astype(f32)
+            for n in range(len(items)):
+                total = total + self.got[b, :, n * self.size : (n + 1) * self.size].astype(f32)
+            self.work[self.me, :, near] = total.astype(bf16)
         else:
-            self.work[self.me, :, far] = came
-        if i + 1 == self.count:
+            for n, item in enumerate(items):
+                self.work[self.me, :, self.rows(self.rep ^ item)] = self.got[b, :, n * self.size : (n + 1) * self.size]
             blocks, lanes = self.work.shape[1], self.work.shape[3]
             for j in range(blocks):
                 self.out[:, j * lanes : (j + 1) * lanes] = self.work[self.me, j].astype(f32)
@@ -1142,15 +1158,11 @@
     outs = refs[len(BwdIn._fields) + 1 : len(BwdIn._fields) + len(BwdOut._fields)]
     held = refs[-4 * len(outs) :]
     ja, jb, jc, jd, je, jf, jg = (
-        Job(members, replicas, held[4 * i], held[4 * i + 1], out, held[4 * i + 2], held[4 * i + 3], i % 2)
+        Job(members, replicas, held[4 * i], held[4 * i + 1], out, held[4 * i + 2], held[4 * i + 3], i % 2, i >= 4)
         for i, out in enumerate(outs))
 
     barrier = pltpu.get_barrier_semaphore()
-    others = [(me ^ o, rep) for o in range(1, members)]
-    b = 1
-    while b < replicas:
-        others.append((me, rep ^ b))
-        b *= 2
+    others = [(me ^ o, rep) for o in range(1, members)] + [(me, rep ^ o) for o in range(1, replicas)]
     for to in others:
         pl.semaphore_signal(barrier, inc=1, device_id=to, device_id_type=MESH)
 
@@ -1243,8 +1255,8 @@
     kd_load(0, 0).start()
     groups = 4
     sc = hd ** (-0.5)
-    plan = (((jc, 0),), (), ((ja, 1), (jd, 1), (jb, 1)), ((jc, 1),), ((ja, 2), (jb, 2), (jd, 2)), ((jc, 2), (ja, 3), (jb, 3)),
-            ((jd, 3), (jc, 3), (ja, 4), (jb, 4)), ((jd, 4), (jc, 4), (ja, 5), (jb, 5)))
+    plan = (((jc, 0),), (), ((ja, 1), (jb, 1), (jd, 1)), (), ((jc, 1), (ja, 2), (jb, 2)), ((jd, 2),), ((jc, 2), (ja, 3), (jb, 3)),
+            ((jd, 3),))
 
     def act(some):
         for job, i in some:
@@ -1296,7 +1308,7 @@
 
     lax.fori_loop(0, members, attend, 0)
 
-    following = {ja: 6, jb: 6, jc: 5, jd: 5, je: 0, jf: 0, jg: 0}
+    following = {ja: 4, jb: 4, jc: 3, jd: 4, je: 0, jf: 0, jg: 0}
 
     def go(*jobs):
         for job in jobs:
@@ -1366,7 +1378,7 @@
     dma = pltpu.SemaphoreType.DMA
     shapes = job_shapes(z)
     legs = m - 1 + 2
-    sems = m - 1 + 2 * (z.replicas.bit_length() - 1)
+    sems = m - 1 + 2 * (z.replicas - 1)
     scratch = dict(
         w_v=pltpu.VMEM((d // z.fc, m, z.rows, z.fc), bf16), wk_v=pltpu.VMEM((m, z.rows, w), bf16),
         t1=pltpu.VMEM((n, d), bf16), t2=pltpu.VMEM((n, d), bf16), q_v=pltpu.VMEM((n, d), bf16), do_v=pltpu.VMEM((n, d), bf16),
@@ -1423,14 +1435,12 @@
     group = lax.dynamic_index_in_dim(
         token_perm.reshape(members, replicas, length), rep, 1, keepdims=False)
 
-    small = jnp.concatenate(
-        [v.astype(f32) for v in (attn_g, attn_b, bq, bmix, mlp_g, mlp_b, bred, bexp, bv, seq_lens[0], adapter_ids.reshape(-1))]
-        + [jnp.zeros((z.small_cols - z.ids_at - seq_lens.shape[1] * adapter_ids.shape[2],), f32)])[None]
     by_chunk = lambda s: s.reshape(s.shape[0], members, SLOTS, z.sub).transpose(2, 0, 1, 3).reshape(
         SLOTS, s.shape[0], z.fc)
     chunked = (lambda s: s) if z.aligned else by_chunk
     got = forward(z, FwdIn(
-        x=tokens, dy=out_grad, small=small, group=group,
+        x=tokens, dy=out_grad, attn_g=attn_g, attn_b=attn_b, bq=bq, bmix=bmix, mlp_g=mlp_g, mlp_b=mlp_b, bred=bred, bexp=bexp, bv=bv,
+        lens=seq_lens, ids=adapter_ids.reshape(1, -1), group=group,
         q_dn=q_dn, q_up=q_up, kv_dn=kv_dn, kv_up=kv_up, mix_dn=mix_dn, mix_up=mix_up, exp_dn=exp_dn,
         exp_up=chunked(exp_up), red_dn=chunked(red_dn), red_up=red_up,
         wq=wq, wkv=wkv, wmix=wmix, wexp=chunked(wexp), wred=wred.reshape(SLOTS, z.sub, d)))

time: 465 us -> 453 us (0.974)
  local copies, waits for them, and re-layouts: 12.9 us -> 7.39 us
  Pallas kernels: 440 us -> 435 us
    concatenate x1 -> x0, local copies, waits for them, and re-layouts: 6.09 us -> none  [local(): jnp.concatenate([v.astype(f32) for v in (attn_g, attn_b, bq, bmix, mlp_g,...]
    pallas_call x1, Pallas kernels: 115 us -> 110 us  [backward(): pl.pallas_call(lambda *refs: bwd_kernel(z, *refs), in_specs=[vm] * first_...]
where the time goes in v6:
time: 453 us; the launch traced here: 444 us
  Pallas kernels  435 us (96%)
  local copies, waits for them, and re-layouts  7.39 us (2%)
    pallas_call x1, Pallas kernels, forward(): pl.pallas_call(lambda *refs: fwd_kernel(z, *refs), in_specs=[vm] * 17 + [...  323 us
    pallas_call x1, Pallas kernels, backward(): pl.pallas_call(lambda *refs: bwd_kernel(z, *refs), in_specs=[vm] * first_...  110 us

profile of v6, /device:TPU:0, one launch (start us, length us, event | category | flops | bytes accessed | tf_op | source)
XLA Modules:
  0.0 443.9 jit_solution(241342504612525334)
XLA Ops:
  0.6 1.3 reshape.63.refs_11_
  1.9 0.9 reshape.64
  2.8 0.6 copy.43
  3.4 322.8 %shard_map.364 = (f32[512,2048]{1,0:T(8,128)}, bf16[8,96,512]{2,1,0:T(8,128)(2,1)}, s32[8,1,512]{2,1,0:T(1,128)}, f32[8,96,128]{2,1,0:T(8,128)}, f32[512,128]{1,...) custom-call(bf16[512,2048]{1,0:T(8,128)(2,1)} %refs_25_.3, ...), custom_call_target="tpu_custom_call" | custom-call | tf_op jit(solution)/shard_map/pallas_call | solution.py:870
  326.2 109.9 %shard_map.365 = (bf16[512,2048]{1,0:T(8,128)(2,1)}, f32[128,1024]{1,0:T(8,128)}, f32[128,1024]{1,0:T(8,128)}, f32[128,512]{1,0:T(8,128)}, f32[128,512]{1,0:T(8,...) custom-call(f32[512,2048]{1,0:T(8,128)} %get-tuple-element.53.refs_0_, ...), custom_call_target="tpu_custom_call" | custom-call | tf_op jit(solution)/shard_map/pallas_call | solution.py:1394
  436.1 2.8 shard_map.366
  438.9 0.0 copy-start
  438.9 3.3 copy.46
  442.2 0.0 copy-done
  442.2 1.3 copy.47
  (1 shorter events, 0.0 us)
Async XLA Ops:
  438.9 3.3 copy-start

commit v7 on v6

--- a/solution.py
+++ b/solution.py
@@ -476,7 +476,9 @@
     sm[me, :, z.be_at : z.vb_at] = r.bexp[...].astype(f32).reshape(1, z.vb_at - z.be_at)
     sm[me, :, z.vb_at : z.vb_at + hd // members] = r.bv[...].astype(f32).reshape(1, hd // members)
     sm[me, :, z.len_at : z.len_at + z.seqs] = r.lens[...].astype(f32)
-    sm[me, :, z.ids_at : z.ids_at + z.seqs * z.projs] = r.ids[...].astype(f32)
+    for j in range(z.seqs):
+        at = z.ids_at + j * z.projs
+        sm[me, :, at : at + z.projs] = r.ids[0, j : j + 1, :].astype(f32)
     for o in range(1, members):
         small_copy(o).start()
     for slot in range(SLOTS):
@@ -1255,8 +1257,8 @@
     kd_load(0, 0).start()
     groups = 4
     sc = hd ** (-0.5)
-    plan = (((jc, 0),), (), ((ja, 1), (jb, 1), (jd, 1)), (), ((jc, 1), (ja, 2), (jb, 2)), ((jd, 2),), ((jc, 2), (ja, 3), (jb, 3)),
-            ((jd, 3),))
+    plan = ((), (), ((jc, 0),), (), ((ja, 1), (jb, 1), (jd, 1)), (), ((jc, 1), (ja, 2), (jb, 2)), ((jd, 2),))
+
 
     def act(some):
         for job, i in some:
@@ -1308,7 +1310,7 @@
 
     lax.fori_loop(0, members, attend, 0)
 
-    following = {ja: 4, jb: 4, jc: 3, jd: 4, je: 0, jf: 0, jg: 0}
+    following = {ja: 3, jb: 3, jc: 2, jd: 3, je: 0, jf: 0, jg: 0}
 
     def go(*jobs):
         for job in jobs:
@@ -1440,7 +1442,7 @@
     chunked = (lambda s: s) if z.aligned else by_chunk
     got = forward(z, FwdIn(
         x=tokens, dy=out_grad, attn_g=attn_g, attn_b=attn_b, bq=bq, bmix=bmix, mlp_g=mlp_g, mlp_b=mlp_b, bred=bred, bexp=bexp, bv=bv,
-        lens=seq_lens, ids=adapter_ids.reshape(1, -1), group=group,
+        lens=seq_lens, ids=adapter_ids, group=group,
         q_dn=q_dn, q_up=q_up, kv_dn=kv_dn, kv_up=kv_up, mix_dn=mix_dn, mix_up=mix_up, exp_dn=exp_dn,
         exp_up=chunked(exp_up), red_dn=chunked(red_dn), red_up=red_up,
         wq=wq, wkv=wkv, wmix=wmix, wexp=chunked(wexp), wred=wred.reshape(SLOTS, z.sub, d)))

time: 453 us -> 449 us (level)
  no operation moved by 1% of the time
where the time goes in v7:
time: 449 us; the launch traced here: 440 us
  Pallas kernels  433 us (96%)
  local copies, waits for them, and re-layouts  6.12 us (1%)
    pallas_call x1, Pallas kernels, forward(): pl.pallas_call(lambda *refs: fwd_kernel(z, *refs), in_specs=[vm] * 17 + [...  323 us
    pallas_call x1, Pallas kernels, backward(): pl.pallas_call(lambda *refs: bwd_kernel(z, *refs), in_specs=[vm] * first_...  107 us

profile of v7, /device:TPU:0, one launch (start us, length us, event | category | flops | bytes accessed | tf_op | source)
XLA Modules:
  0.0 440.3 jit_solution(14752872472211568964)
XLA Ops:
  0.6 0.9 reshape.60
  1.5 0.6 copy.43
  2.1 322.8 %shard_map.364 = (f32[512,2048]{1,0:T(8,128)}, bf16[8,96,512]{2,1,0:T(8,128)(2,1)}, s32[8,1,512]{2,1,0:T(1,128)}, f32[8,96,128]{2,1,0:T(8,128)}, f32[512,128]{1,...) custom-call(bf16[512,2048]{1,0:T(8,128)(2,1)} %refs_25_.3, ...), custom_call_target="tpu_custom_call" | custom-call | tf_op jit(solution)/shard_map/pallas_call | solution.py:872
  325.0 107.5 %shard_map.365 = (bf16[512,2048]{1,0:T(8,128)(2,1)}, f32[128,1024]{1,0:T(8,128)}, f32[128,1024]{1,0:T(8,128)}, f32[128,512]{1,0:T(8,128)}, f32[128,512]{1,0:T(8,...) custom-call(f32[512,2048]{1,0:T(8,128)} %get-tuple-element.53.refs_0_, ...), custom_call_target="tpu_custom_call" | custom-call | tf_op jit(solution)/shard_map/pallas_call | solution.py:1396
  432.5 2.8 shard_map.366
  435.3 0.0 copy-start
  435.3 3.3 copy.46
  438.6 0.0 copy-done
  438.6 1.3 copy.47
  (1 shorter events, 0.0 us)
Async XLA Ops:
  435.3 3.3 copy-start

commit v8 on v7

--- a/solution.py
+++ b/solution.py
@@ -481,11 +481,11 @@
         sm[me, :, at : at + z.projs] = r.ids[0, j : j + 1, :].astype(f32)
     for o in range(1, members):
         small_copy(o).start()
+    serve(1)
     for slot in range(SLOTS):
         staged(slot)
     for slot in range(SLOTS):
         stored(slot).wait()
-    serve(1)
     for o in range(1, members):
         pltpu.make_async_copy(sm.at[me ^ o], sm.at[me ^ o], r.sm_recv.at[o]).wait()
 

time: 449 us -> 449 us (level)
  no operation moved by 1% of the time
where the time goes in v8:
time: 449 us; the launch traced here: 440 us
  Pallas kernels  433 us (96%)
  local copies, waits for them, and re-layouts  6.12 us (1%)
    pallas_call x1, Pallas kernels, forward(): pl.pallas_call(lambda *refs: fwd_kernel(z, *refs), in_specs=[vm] * 17 + [...  323 us
    pallas_call x1, Pallas kernels, backward(): pl.pallas_call(lambda *refs: bwd_kernel(z, *refs), in_specs=[vm] * first_...  108 us

profile of v8, /device:TPU:0, one launch (start us, length us, event | category | flops | bytes accessed | tf_op | source)
XLA Modules:
  0.0 440.3 jit_solution(14553466852825443532)
XLA Ops:
  0.6 0.9 reshape.60
  1.5 0.6 copy.43
  2.1 322.8 %shard_map.364 = (f32[512,2048]{1,0:T(8,128)}, bf16[8,96,512]{2,1,0:T(8,128)(2,1)}, s32[8,1,512]{2,1,0:T(1,128)}, f32[8,96,128]{2,1,0:T(8,128)}, f32[512,128]{1,...) custom-call(bf16[512,2048]{1,0:T(8,128)(2,1)} %refs_25_.3, ...), custom_call_target="tpu_custom_call" | custom-call | tf_op jit(solution)/shard_map/pallas_call | solution.py:872
  325.0 107.5 %shard_map.365 = (bf16[512,2048]{1,0:T(8,128)(2,1)}, f32[128,1024]{1,0:T(8,128)}, f32[128,1024]{1,0:T(8,128)}, f32[128,512]{1,0:T(8,128)}, f32[128,512]{1,0:T(8,...) custom-call(f32[512,2048]{1,0:T(8,128)} %get-tuple-element.53.refs_0_, ...), custom_call_target="tpu_custom_call" | custom-call | tf_op jit(solution)/shard_map/pallas_call | solution.py:1396
  432.5 2.8 shard_map.366
  435.3 0.0 copy-start
  435.3 3.3 copy.46
  438.6 0.0 copy-done
  438.6 1.3 copy.47
  (1 shorter events, 0.0 us)
Async XLA Ops:
  435.3 3.3 copy-start
